TPU v7x, 128 devices: a whole 4x4x4 slice. The times are simulated.
128 devices in a mesh: member: 8 (over x_lo, z), space: 16 (over y, x_hi, core).
Axes of the slice: x: 4 (x_hi: 2, x_lo: 2; x = x_hi * 2 + x_lo), y: 4, z: 4, core: 2. Of those that a mesh axis runs over, the one named last changes fastest.
Arguments:
- initial_ensemble: float32 [64, 6, 128, 512], P('member', None, 'space'), may hold values from -6 to 6
- obs_value: float32 [16, 2048], P('space'), may hold values from -6 to 6
- obs_error: float32 [16, 2048], P('space'), may hold values from 0.25 to 4
- obs_location: int32 [16, 2048], P('space'), may hold values from 0 to 24575, as said below
- patch_obs: int32 [16, 512, 64], P('space', 'member'), may hold values from 0 to 2047, as said below
- cotangent: float32 [64, 6, 128, 512], P('member', None, 'space'), may hold values from -6 to 6
Outputs:
- analysis: float32 [64, 6, 128, 512], P('member', None, 'space')
- gradient: float32 [64, 6, 128, 512], P('member', None, 'space')
Inputs may be any that keep to these rules, and one draw needn't show every extreme that they name: `obs_location`: observation j of a tile lies in column (j * 512) // 2048; observation 0 lies at cell 0 and observation 2048 - 1 at cell 6 * 8 * 512 - 1. `patch_obs`: entry q of patch p is (((8 c + 3) * 2048) // 1024 + e) mod 2048 with c = p // 4 and -(32) <= e <= 32; entries may repeat.
All inputs are finite; a program needn't handle non-finite values.
Results may differ from a plain program's by a relative error of at most 0.0003.
Values sent between devices are 32-bit elements; how exact they have to be, the bound alone decides.
No kernel may reach another device: no remote copies, remote signals or barrier semaphores. Data moves between devices by JAX's collectives and lax.ppermute only.
A program may use at most 192 MiB of HBM per device.

v0:
```python
import jax
import jax.numpy as jnp
from jax import lax
from jax.sharding import PartitionSpec as P

FIELDS = 3
LEV = 2
SUBDOMAIN_HEIGHT = 8
MESH_WIDTH = 512
LOC_R = 8
NS_ITERS = 4
STEPS = 1


time_step = 0.2
coriolis = 0.5
stratification = 1.0
mixing = 0.3
highest = lax.Precision.HIGHEST


def padded_2(cells, sides, width):
    for axis, dim in sides:
        count = lax.axis_size(axis)
        head = lax.slice_in_dim(cells, 0, width, axis=dim)
        tail = lax.slice_in_dim(cells, cells.shape[dim] - width, cells.shape[dim], axis=dim)
        cells = jnp.concatenate(
            [
                lax.ppermute(tail, axis, [(i, (i + 1) % count) for i in range(count)]),
                cells,
                lax.ppermute(head, axis, [((i + 1) % count, i) for i in range(count)]),
            ],
            axis=dim,
        )
    return cells


def laid_out(tiles, dim):
    lengths = list(tiles.shape[1:])
    lengths[dim] *= tiles.shape[0]
    return jnp.moveaxis(tiles, 0, dim).reshape(lengths)


def copy_for_each(value, axis):
    copies = jnp.broadcast_to(value, (lax.axis_size(axis), *value.shape))
    return lax.all_to_all(copies, axis, split_axis=0, concat_axis=0, tiled=True)


def gathered_copies(value, axis, dim):
    return laid_out(copy_for_each(value, axis), dim)


def in_blocks(value, dim, peers):
    lengths = value.shape
    tiles = value.reshape(*lengths[:dim], peers, lengths[dim] // peers, *lengths[dim + 1 :])
    return jnp.moveaxis(tiles, dim, 0)


def edges_of(length, count):
    unit = 8 if length >= 8 * count else 1
    return [length // unit * k // count * unit for k in range(1, count)]


def several_exchanges(value, axis, pieces, split_dim, concat_dim):
    tiles = in_blocks(value, split_dim, lax.axis_size(axis))
    widest = max(range(1, max(2, tiles.ndim - 1)), key=lambda d: tiles.shape[d])
    done = []
    for piece in jnp.split(tiles, edges_of(tiles.shape[widest], pieces), axis=widest):
        if piece.size:
            done.append(lax.all_to_all(piece, axis, split_axis=0, concat_axis=0, tiled=True))
    return laid_out(jnp.concatenate(done, axis=widest), concat_dim)


def in_one_piece(arrays, axis, split_dim, concat_dim, along):
    both = jnp.concatenate(arrays, axis=along)
    whole, at, done = (
        lax.all_to_all(both, axis, split_axis=split_dim, concat_axis=concat_dim, tiled=True),
        0,
        [],
    )
    for a in arrays:
        done.append(lax.slice_in_dim(whole, at, at + a.shape[along], axis=along))
        at += a.shape[along]
    return tuple(done)


def summed_on_arrival(value, axis, dim):
    peers = lax.axis_size(axis)
    tiles = lax.all_to_all(in_blocks(value, dim, peers), axis, 0, 0, tiled=True)
    return jnp.sum(tiles, axis=0)


def row_diff(padded):
    return (
        padded[..., :-4, :]
        - 8.0 * padded[..., 1:-3, :]
        + 8.0 * padded[..., 3:-1, :]
        - padded[..., 4:, :]
    ) / 12.0


def col_diff(field):
    return (
        jnp.roll(field, 2, axis=-1)
        - 8.0 * jnp.roll(field, 1, axis=-1)
        + 8.0 * jnp.roll(field, -1, axis=-1)
        - jnp.roll(field, -2, axis=-1)
    ) / 12.0


def tendency(padded):
    members = padded.shape[0]
    layered = padded.reshape(members, FIELDS, LEV, padded.shape[2], padded.shape[3])
    interior = layered[:, :, :, 2:-2, :]
    along_rows = row_diff(layered)
    along_cols = col_diff(interior)
    speed_u = interior[:, 0]
    speed_v = interior[:, 1]
    carried = speed_u[:, None] * along_rows + speed_v[:, None] * along_cols
    rate_u = -carried[:, 0] + coriolis * speed_v - along_rows[:, 2]
    rate_v = -carried[:, 1] - coriolis * speed_u - along_cols[:, 2]
    rate_b = -carried[:, 2] - stratification * (along_rows[:, 0] + along_cols[:, 1])
    rates = jnp.stack([rate_u, rate_v, rate_b], axis=1)
    above = jnp.concatenate([interior[:, :, 1:], interior[:, :, -1:]], axis=2)
    below = jnp.concatenate([interior[:, :, :1], interior[:, :, :-1]], axis=2)
    rates = rates + mixing * (above - 2.0 * interior + below)
    return rates.reshape(members, FIELDS * LEV, interior.shape[3], interior.shape[4])


def exchange_rims(edges):
    return padded_2(edges, (("space", 2),), 2)


def padded_rows(grid):
    edges = jnp.concatenate([grid[:, :, :2], grid[:, :, -2:]], axis=2)
    extended = exchange_rims(edges)
    return jnp.concatenate([extended[:, :, :2], grid, extended[:, :, -2:]], axis=2)


def return_rims(grad_padded):
    interior = grad_padded[:, :, 2:-2]
    edges = jnp.concatenate([grad_padded[:, :, :2], grad_padded[:, :, -2:]], axis=2)
    extended = exchange_rims(edges)
    interior = interior.at[:, :, :2].add(extended[:, :, :2])
    return interior.at[:, :, -2:].add(extended[:, :, -2:])


def analyse(ensemble, obs_ens, obs_values, obs_errors, obs_cells, patch_lists, first_col):
    members = ensemble.shape[0]
    variables = ensemble.shape[1]
    tile_rows = ensemble.shape[2]
    columns = ensemble.shape[3]
    half_rows = tile_rows // 2
    quads = columns // 4
    patch_count = half_rows * quads
    patch_ids = jnp.arange(patch_count, dtype=jnp.int32)
    patch_col = patch_ids // half_rows
    patch_row = patch_ids % half_rows
    picked = obs_ens[:, patch_lists]
    mean_obs = jnp.mean(picked, axis=0)
    spread = picked - mean_obs
    innovation = obs_values[patch_lists] - mean_obs
    located = obs_cells[patch_lists]
    obs_row = located // MESH_WIDTH % SUBDOMAIN_HEIGHT
    obs_col = located % MESH_WIDTH
    row_gap = (obs_row - 2 * patch_row[:, None]).astype(jnp.float32) - 0.5
    col_shift = obs_col - 4 * (patch_col[:, None] + first_col // 4)
    col_shift = (col_shift + MESH_WIDTH // 2) % MESH_WIDTH - MESH_WIDTH // 2
    col_gap = col_shift.astype(jnp.float32) - 1.5
    weight = (
        jnp.exp(-(row_gap * row_gap + col_gap * col_gap) / (2.0 * LOC_R * LOC_R))
        / obs_errors[patch_lists]
    )
    scaled = spread * weight
    identity = jnp.eye(members, dtype=jnp.float32)
    gram = (members - 1.0) * identity + jnp.einsum(
        "kpq,jpq->pkj", scaled, spread, precision=highest
    )
    scale = jnp.sqrt(jnp.sum(gram * gram, axis=(1, 2)))
    root_iter = gram / scale[:, None, None]
    inverse_root = jnp.broadcast_to(identity, gram.shape)
    for sweep in range(NS_ITERS):
        factor = 1.5 * identity - 0.5 * jnp.einsum(
            "pij,pjk->pik", inverse_root, root_iter, precision=highest
        )
        root_iter = jnp.einsum("pij,pjk->pik", root_iter, factor, precision=highest)
        inverse_root = jnp.einsum("pij,pjk->pik", factor, inverse_root, precision=highest)
    forcing = jnp.einsum("kpq,pq->pk", scaled, innovation, precision=highest)
    half_way = jnp.einsum("pij,pj->pi", inverse_root, forcing, precision=highest)
    mean_weight = (
        jnp.einsum("pij,pj->pi", inverse_root, half_way, precision=highest) / scale[:, None]
    )
    weights = (
        jnp.sqrt(members - 1.0) * inverse_root / jnp.sqrt(scale)[:, None, None]
        + mean_weight[:, :, None]
    )
    patch_cells = ensemble.reshape(members, variables, half_rows, 2, quads, 4).transpose(
        4, 2, 0, 1, 3, 5
    )
    patch_cells = patch_cells.reshape(patch_count, members, variables * 8)
    centre = jnp.mean(patch_cells, axis=1, keepdims=True)
    anomaly = patch_cells - centre
    updated = centre + jnp.einsum("pkc,pkj->pjc", anomaly, weights, precision=highest)
    updated = updated.reshape(quads, half_rows, members, variables, 2, 4).transpose(
        2, 3, 1, 4, 0, 5
    )
    return updated.reshape(members, variables, tile_rows, columns)


def owner_update(fore_owned, cot_owned, obs_ens, obs_values, obs_errors, obs_cells, patch_lists):
    columns = fore_owned.shape[3]
    width_block = min(32, columns)
    turn_count = columns // width_block
    patch_block = fore_owned.shape[2] // 2 * (width_block // 4)
    first_col = lax.axis_index("member") * columns

    def one_turn(obs_total, turn_index):
        col_start = turn_index * width_block
        fore_block = lax.dynamic_slice_in_dim(fore_owned, col_start, width_block, 3)
        cot_block = lax.dynamic_slice_in_dim(cot_owned, col_start, width_block, 3)
        list_block = lax.dynamic_slice_in_dim(patch_lists, turn_index * patch_block, patch_block, 0)

        def local_update(ensemble, observed):
            return analyse(
                ensemble,
                observed,
                obs_values,
                obs_errors,
                obs_cells,
                list_block,
                first_col + col_start,
            )

        updated, pullback = jax.vjp(local_update, fore_block, obs_ens)
        grad_block, grad_obs = pullback(cot_block)
        return (obs_total + grad_obs, (updated, grad_block))

    start_total = jnp.zeros(obs_ens.shape, jnp.float32)
    obs_total, stacked = lax.scan(one_turn, start_total, jnp.arange(turn_count, dtype=jnp.int32))
    updated_all = stacked[0].transpose(1, 2, 3, 0, 4).reshape(fore_owned.shape)
    grad_all = stacked[1].transpose(1, 2, 3, 0, 4).reshape(fore_owned.shape)
    return (updated_all, grad_all, obs_total)


def shards(initial_ensemble, obs_value, obs_error, obs_location, patch_obs, cotangent):
    obs_values = obs_value[0]
    obs_errors = obs_error[0]
    obs_cells = obs_location[0]
    patch_lists = patch_obs[0]
    current = initial_ensemble
    step_count = 0
    first_pad = padded_rows(current)
    first_rate = tendency(first_pad)
    middle = current + time_step * first_rate
    second_pad = padded_rows(middle)
    second_rate = tendency(second_pad)
    trajectory = [(first_pad, second_pad)]
    current = current + 0.5 * time_step * (first_rate + second_rate)
    member_values = current.reshape(current.shape[0], -1)[:, obs_cells]
    obs_ens = gathered_copies(member_values, "member", 0)
    fore_owned, cot_owned = (
        several_exchanges(current, "member", 2, 3, 0),
        several_exchanges(cotangent, "member", 2, 3, 0),
    )
    updated_owned, grad_owned, obs_total = owner_update(
        fore_owned, cot_owned, obs_ens, obs_values, obs_errors, obs_cells, patch_lists
    )
    analysis, grad_state = in_one_piece((updated_owned, grad_owned), "member", 0, 3, 1)
    my_grad_obs = summed_on_arrival(obs_total, "member", 0)
    flat_grad = grad_state.reshape(grad_state.shape[0], -1).at[:, obs_cells].add(my_grad_obs)
    gradient = flat_grad.reshape(grad_state.shape)
    for step_count in reversed(range(STEPS)):
        first_pad, second_pad = trajectory[step_count]
        second_pull = jax.vjp(tendency, second_pad)[1]
        grad_middle = return_rims(second_pull(0.5 * time_step * gradient)[0])
        grad_first = 0.5 * time_step * gradient + time_step * grad_middle
        first_pull = jax.vjp(tendency, first_pad)[1]
        gradient = gradient + grad_middle + return_rims(first_pull(grad_first)[0])
    return (analysis, gradient)


def solution(mesh):
    placed = (
        P("member", None, "space", None),
        P("space", None),
        P("space", None),
        P("space", None),
        P("space", "member", None),
        P("member", None, "space", None),
    )
    return jax.shard_map(
        shards,
        mesh=mesh,
        in_specs=placed,
        out_specs=(P("member", None, "space", None), P("member", None, "space", None)),
        check_vma=False,
    )
```

profile of v0, /device:TPU:31, one launch (start us, length us, event | category | flops | bytes accessed | tf_op | source)
XLA Modules:
  0.0 595.0 jit_solution(13425415123303683804)
XLA Ops:
  3.8 4.7 collective-permute-start
  8.8 3.7 collective-permute-done.1
  21.8 4.8 collective-permute-start.2
  29.0 6.5 %all-to-all-start.2 = ((f32[8,1,12288]{2,1,0:T(1,128)}), f32[8,1,12288]{2,1,0:T(1,128)S(1)}, u32[]{:S(2)}, u32[]{:S(2)}) async-start(f32[8,1,12288]{2,1,0:T(1,128)} %reshape.604), calls=%async_computation.2 | async-start | bytes 786432 | tf_op jit(solution)/shard_map/all_to_all | solution.py:70
  41.8 3.2 multiply_add_fusion.8
  48.1 5.5 all-to-all-start.3
  60.2 4.3 all-to-all-start
  65.9 6.4 %all-to-all-done = f32[8,1,12288]{2,1,0:T(1,128)S(1)} async-done(((f32[8,1,12288]{2,1,0:T(1,128)}), f32[8,1,12288]{2,1,0:T(1,128)S(1)}, u32[]{:S(2)}, u32[]{:S(2)}) %all-to-all-start) | async-done | bytes 393248 | tf_op jit(solution)/shard_map/all_to_all | solution.py:70
  72.3 3.9 all-to-all-start.1
  76.2 6.7 %copy.399 = f32[8,6,8,512]{0,3,2,1:T(8,128)} copy(f32[8,6,8,512]{3,2,1,0:T(8,128)S(1)} %add.445) | data formatting | bytes 1572864 | tf_op jit(solution)/shard_map/add | solution.py:258
  82.9 10.0 %gather_fusion.4 = f32[2048,8]{1,0:T(8,128)S(1)} fusion(f32[8,24576]{0,1:T(8,128)} %bitcast.462, s32[2048]{0:T(1024)S(1)} %broadcast_clamp_fusion.1), kind=kCustom, calls=%fused_computation.4 | custom fusion | bytes 139264 | tf_op jit(solution)/shard_map/gather | solution.py:259
  94.2 5.1 all-to-all-start.4
  101.9 2.6 reduce.21
  114.2 312.1 %while.21 = (s32[]{:T(128)}, f32[64,2048]{0,1:T(8,128)S(1)}, f32[2,64,6,8,32]{1,4,0,3,2:T(8,128)}, f32[2,64,6,8,32]{1,4,0,3,2:T(8,128)}, s32[2]{0:T(128)S(1)}, /...) while((s32[]{:T(128)}, f32[64,2048]{0,1:T(8,128)S(1)}, ...), condition=%wide.region_12.13_spmd, body=%wide.region_0.12_spmd.sunk | while | flops 3670212864 | bytes 138591568 | solution.py:239
  116.1 11.8 %gather_fusion.3 = f32[2048]{0:T(1024)S(1)} fusion(f32[2048]{0:T(1024)S(1)} %get-tuple-element.658, s32[2048]{0:T(1024)S(1)} %broadcast_clamp_fusion.3), kind=kCustom, calls=%fused_computation.3.clone.1 | custom fusion | bytes 24576 | tf_op jit(solution)/shard_map/while/body/eval_jaxpr/jvp()/gather | solution.py:162
  128.0 11.8 %gather_fusion.2 = s32[2048]{0:T(1024)S(1)} fusion(s32[2048]{0:T(1024)S(1)} %get-tuple-element.655, s32[2048]{0:T(1024)S(1)} %broadcast_clamp_fusion.3), kind=kCustom, calls=%fused_computation.1.clone.1 | custom fusion | bytes 24576 | tf_op jit(solution)/shard_map/while/body/eval_jaxpr/jvp()/gather | solution.py:163
  139.8 11.8 %gather_fusion.1 = f32[2048]{0:T(1024)S(1)} fusion(f32[2048]{0:T(1024)S(1)} %get-tuple-element.657, s32[2048]{0:T(1024)S(1)} %broadcast_clamp_fusion.3), kind=kCustom, calls=%fused_computation.2.clone.1 | custom fusion | bytes 24576 | tf_op jit(solution)/shard_map/while/body/eval_jaxpr/jvp()/gather | solution.py:172
  157.9 7.7 %gather_fusion = f32[2048,64]{1,0:T(8,128)} fusion(f32[64,2048]{0,1:T(8,128)S(1)} %get-tuple-element.654, s32[2048]{0:T(1024)S(1)} %broadcast_clamp_fusion.3), kind=kCustom, calls=%fused_computation.clone.1 | custom fusion | bytes 1056768 | tf_op jit(solution)/shard_map/while/body/eval_jaxpr/jvp()/gather | solution.py:159
  169.1 2.0 multiply_reduce_fusion.11
  189.9 2.6 copy.619
  192.5 4.4 multiply_reduce_fusion.12
  197.1 2.2 convolution_add_fusion.22
  205.1 2.7 fusion.427
  207.8 2.8 fusion.424
  222.9 2.2 convolution_add_fusion.19
  234.5 2.1 convolution_add_fusion.20
  246.4 2.0 fusion.439
  251.1 11.9 %scatter_fusion = f32[64,2048]{0,1:T(8,128)S(1)} fusion(f32[64,2048]{0,1:T(8,128)S(1)} %get-tuple-element.626, s32[2048]{0:T(1024)S(1)} %reshape.634, f32[2048,64]{1,0:T(8,128)S(1)} %bitcast.434), kind=kCustom, calls=%fused_computation.5.clone.1 | custom fusion | flops 131072 | bytes 1581056 | tf_op jit(solution)/shard_map/while/body/eval_jaxpr/transpose(jvp())/scatter-add | solution.py:159
  263.0 2.7 constant_dynamic-update-slice_fusion.3
  267.3 11.8 %gather_fusion.3 = f32[2048]{0:T(1024)S(1)} fusion(f32[2048]{0:T(1024)S(1)} %get-tuple-element.658, s32[2048]{0:T(1024)S(1)} %broadcast_clamp_fusion.3), kind=kCustom, calls=%fused_computation.3.clone.1 | custom fusion | bytes 24576 | tf_op jit(solution)/shard_map/while/body/eval_jaxpr/jvp()/gather | solution.py:162
  279.1 11.8 %gather_fusion.2 = s32[2048]{0:T(1024)S(1)} fusion(s32[2048]{0:T(1024)S(1)} %get-tuple-element.655, s32[2048]{0:T(1024)S(1)} %broadcast_clamp_fusion.3), kind=kCustom, calls=%fused_computation.1.clone.1 | custom fusion | bytes 24576 | tf_op jit(solution)/shard_map/while/body/eval_jaxpr/jvp()/gather | solution.py:163
  291.0 11.8 %gather_fusion.1 = f32[2048]{0:T(1024)S(1)} fusion(f32[2048]{0:T(1024)S(1)} %get-tuple-element.657, s32[2048]{0:T(1024)S(1)} %broadcast_clamp_fusion.3), kind=kCustom, calls=%fused_computation.2.clone.1 | custom fusion | bytes 24576 | tf_op jit(solution)/shard_map/while/body/eval_jaxpr/jvp()/gather | solution.py:172
  309.1 7.9 %gather_fusion = f32[2048,64]{1,0:T(8,128)} fusion(f32[64,2048]{0,1:T(8,128)S(1)} %get-tuple-element.654, s32[2048]{0:T(1024)S(1)} %broadcast_clamp_fusion.3), kind=kCustom, calls=%fused_computation.clone.1 | custom fusion | bytes 1056768 | tf_op jit(solution)/shard_map/while/body/eval_jaxpr/jvp()/gather | solution.py:159
  320.5 2.0 multiply_reduce_fusion.11
  341.1 2.6 copy.619
  343.7 4.4 multiply_reduce_fusion.12
  348.3 2.4 convolution_add_fusion.22
  356.5 2.7 fusion.427
  359.3 2.8 fusion.424
  385.7 2.1 convolution_add_fusion.20
  397.6 2.0 fusion.439
  402.3 11.9 %scatter_fusion = f32[64,2048]{0,1:T(8,128)S(1)} fusion(f32[64,2048]{0,1:T(8,128)S(1)} %get-tuple-element.626, s32[2048]{0:T(1024)S(1)} %reshape.634, f32[2048,64]{1,0:T(8,128)S(1)} %bitcast.434), kind=kCustom, calls=%fused_computation.5.clone.1 | custom fusion | flops 131072 | bytes 1581056 | tf_op jit(solution)/shard_map/while/body/eval_jaxpr/transpose(jvp())/scatter-add | solution.py:159
  414.2 2.7 constant_dynamic-update-slice_fusion.3
  427.5 5.1 all-to-all-start.6
  432.6 2.2 pad_maximum_fusion
  434.8 2.7 copy.406
  437.5 4.8 reshape.606
  442.3 5.1 all-to-all-start.5
  449.8 17.7 %all-to-all-done.5 = f32[8,1,49152]{2,1,0:T(1,128)S(1)} async-done(((f32[8,1,49152]{2,1,0:T(1,128)}), f32[8,1,49152]{2,1,0:T(1,128)S(1)}, u32[]{:S(2)}, u32[]{:S(2)}) %all-to-all-start.5) | async-done | bytes 1572896 | tf_op jit(solution)/shard_map/all_to_all | solution.py:77
  467.6 6.2 %reduce.23 = f32[8,49152]{1,0:T(8,128)} reduce(f32[8,1,49152]{2,1,0:T(1,128)S(1)} %all-to-all-done.5, f32[]{:T(128)} %broadcast.891), dimensions={1}, to_apply=%all_to_all.36.reduce_sub_computation | reduce | bytes 3145732 | tf_op jit(solution)/shard_map/all_to_all | solution.py:77
  473.8 2.7 reshape.607
  476.5 3.4 copy.407
  479.9 2.8 all_to_all.39
  483.8 6.7 %copy.408 = f32[8,6,8,512]{0,3,2,1:T(8,128)} copy(f32[8,6,8,512]{3,2,1,0:T(8,128)S(1)} %get-tuple-element.412) | data formatting | bytes 1572864 | tf_op jit(solution)/shard_map/slice | solution.py:82
  490.5 19.9 %scatter_fusion.1 = f32[8,24576]{0,1:T(8,128)} fusion(f32[8,24576]{0,1:T(8,128)} %bitcast.432, s32[2048]{0:T(1024)S(1)} %bitcast.498, f32[2048,8]{1,0:T(8,128)} %copy.410), kind=kCustom, calls=%fused_computation.6 | custom fusion | flops 16384 | bytes 204800 | tf_op jit(solution)/shard_map/scatter-add | solution.py:270
  510.3 12.2 %broadcast_multiply_fusion.2 = (f32[8,24576]{0,1:T(8,128)}, f32[8,24576]{0,1:T(8,128)}) fusion(f32[8,24576]{0,1:T(8,128)} %scatter_fusion.1), kind=kLoop, calls=%fused_computation.149 | loop fusion | flops 393216 | bytes 2359296 | tf_op jit(solution)/shard_map/transpose(jvp())/mul | solution.py:126
  522.5 9.5 %fusion.123 = (f32[8,1,2,8,512]{0,4,3,2,1:T(8,128)}, f32[8,1,2,8,512]{0,4,3,2,1:T(8,128)}, f32[8,1,2,8,512]{0,4,3,2,1:T(8,128)}) fusion(f32[8,3,2,8,512]{0,4,3,2,1:T(8,128)} %bitcast.460), kind=kLoop, calls=%fused_computation.284 | loop fusion | bytes 1572864 | tf_op jit(solution)/shard_map/transpose(jvp())/unstack | solution.py:123
  532.0 2.8 copy.492
  534.9 2.9 copy.493
  537.9 2.9 copy.494
  544.7 7.5 %copy.415 = f32[8,3,2,8,512]{4,3,2,1,0:T(8,128)S(1)} copy(f32[8,3,2,8,512]{0,4,3,2,1:T(8,128)} %bitcast.459) | data formatting | bytes 1572864 | tf_op jit(solution)/shard_map/transpose(jvp())/mul | solution.py:126
  559.8 7.4 %copy.423 = f32[8,6,8,512]{3,0,2,1:T(8,128)S(1)} copy(f32[8,6,8,512]{0,3,2,1:T(8,128)} %bitcast.433) | data formatting | bytes 1572864 | tf_op jit(solution)/shard_map/reshape | solution.py:271
  568.0 8.3 %collective-permute-done.5 = f32[8,6,2,512]{3,0,2,1:T(8,128)S(1)} collective-permute-done((f32[8,6,2,512]{3,0,2,1:T(8,128)S(1)}, f32[8,6,2,512]{3,0,2,1:T(8,128)S(1)}, u32[]{:S(2)}, u32[]{:S(2)}) %collective-permute-start.5) | collective-permute-done | bytes 196640 | tf_op jit(solution)/shard_map/ppermute | solution.py:31
  586.7 6.2 %collective-permute-done.7 = f32[8,6,2,512]{3,0,2,1:T(8,128)S(1)} collective-permute-done((f32[8,6,2,512]{3,0,2,1:T(8,128)S(1)}, f32[8,6,2,512]{3,0,2,1:T(8,128)S(1)}, u32[]{:S(2)}, u32[]{:S(2)}) %collective-permute-start.7) | collective-permute-done | bytes 196640 | tf_op jit(solution)/shard_map/ppermute | solution.py:31
  (485 shorter events, 213.9 us)
Async XLA Ops:
  0.6 7.9 %copy-start.63 = (f32[8,6,8,512]{3,2,1,0:T(8,128)S(1)}, f32[8,6,8,512]{3,2,1,0:T(8,128)}, u32[]{:S(2)}) copy-start(f32[8,6,8,512]{3,2,1,0:T(8,128)} %param.21) | copy-start | bytes 2359300
  2.3 10.2 %collective-permute-start.1 = (f32[8,6,2,512]{3,0,2,1:T(8,128)S(1)}, f32[8,6,2,512]{3,0,2,1:T(8,128)S(1)}, u32[]{:S(2)}, u32[]{:S(2)}) collective-permute-start(f32[8,6,2,512]{3,0,2,1:T(8,128)S(1)} %copy.595), channel_id=1, source_target_pairs={{1,0},{2,1},{3,2},{4,3},{5,4},{6,5},{7,6},{8,7},{9,8},{10,9},{11,1... | collective-permute-start | bytes 589832 | tf_op jit(solution)/shard_map/ppermute | solution.py:31
  3.8 10.0 %copy-start.30 = (f32[8,6,8,512]{3,2,1,0:T(8,128)S(1)}, f32[8,6,8,512]{3,2,1,0:T(8,128)}, u32[]{:S(2)}) copy-start(f32[8,6,8,512]{3,2,1,0:T(8,128)} %param.16) | copy-start | bytes 2359300
  3.8 8.9 %collective-permute-start = (f32[8,6,2,512]{3,0,2,1:T(8,128)}, f32[8,6,2,512]{3,0,2,1:T(8,128)}, u32[]{:S(2)}, u32[]{:S(2)}) collective-permute-start(f32[8,6,2,512]{3,0,2,1:T(8,128)} %copy.596), channel_id=1, source_target_pairs={{0,1},{1,2},{2,3},{3,4},{4,5},{5,6},{6,7},{7,8},{8,9},{9,10},{10,1... | collective-permute-start | bytes 589832 | tf_op jit(solution)/shard_map/ppermute | solution.py:29
  21.8 15.1 %collective-permute-start.2 = (f32[8,6,2,512]{3,0,2,1:T(8,128)}, f32[8,6,2,512]{3,0,2,1:T(8,128)}, u32[]{:S(2)}, u32[]{:S(2)}) collective-permute-start(f32[8,6,2,512]{3,0,2,1:T(8,128)} %get-tuple-element.473), channel_id=1, source_target_pairs={{0,1},{1,2},{2,3},{3,4},{4,5},{5,6},{6,7},{7,8},{8,9},{9,10},{10,1... | collective-permute-start | bytes 589832 | tf_op jit(solution)/shard_map/ppermute | solution.py:29
  26.6 10.3 %collective-permute-start.3 = (f32[8,6,2,512]{3,0,2,1:T(8,128)}, f32[8,6,2,512]{3,0,2,1:T(8,128)}, u32[]{:S(2)}, u32[]{:S(2)}) collective-permute-start(f32[8,6,2,512]{3,0,2,1:T(8,128)} %get-tuple-element.474), channel_id=1, source_target_pairs={{1,0},{2,1},{3,2},{4,3},{5,4},{6,5},{7,6},{8,7},{9,8},{10,9},{11,1... | collective-permute-start | bytes 589832 | tf_op jit(solution)/shard_map/ppermute | solution.py:31
  27.6 7.9 %copy-start.42 = (f32[8,4,6,8,64]{4,0,3,2,1:T(8,128)S(1)}, f32[8,4,6,8,64]{4,0,3,2,1:T(8,128)}, u32[]{:S(2)}) copy-start(f32[8,4,6,8,64]{4,0,3,2,1:T(8,128)} %get-tuple-element.415) | copy-start | bytes 1179652
  29.0 19.1 %all-to-all-start.2 = ((f32[8,1,12288]{2,1,0:T(1,128)}), f32[8,1,12288]{2,1,0:T(1,128)S(1)}, u32[]{:S(2)}, u32[]{:S(2)}) async-start(f32[8,1,12288]{2,1,0:T(1,128)} %reshape.604), calls=%async_computation.2 | async-start | bytes 786432 | tf_op jit(solution)/shard_map/all_to_all | solution.py:70
  46.7 6.9 %copy-start.45 = (f32[8,3,2,8,512]{4,3,2,1,0:T(8,128)S(1)}, f32[8,3,2,8,512]{4,3,2,1,0:T(8,128)}, u32[]{:S(2)}) copy-start(f32[8,3,2,8,512]{4,3,2,1,0:T(8,128)} %get-tuple-element.378) | copy-start | bytes 2359300
  48.1 12.1 %all-to-all-start.3 = ((f32[8,1,12288]{2,1,0:T(1,128)}), f32[8,1,12288]{2,1,0:T(1,128)}, u32[]{:S(2)}, u32[]{:S(2)}) async-start(f32[8,1,12288]{2,1,0:T(1,128)} %reshape.602), calls=%async_computation.3 | async-start | bytes 786432 | tf_op jit(solution)/shard_map/all_to_all | solution.py:70
  57.0 7.5 %copy-start.41 = (f32[8,4,6,8,64]{4,0,3,2,1:T(8,128)S(1)}, f32[8,4,6,8,64]{4,0,3,2,1:T(8,128)}, u32[]{:S(2)}) copy-start(f32[8,4,6,8,64]{4,0,3,2,1:T(8,128)} %get-tuple-element.417) | copy-start | bytes 1179652
  60.2 12.1 %all-to-all-start = ((f32[8,1,12288]{2,1,0:T(1,128)}), f32[8,1,12288]{2,1,0:T(1,128)S(1)}, u32[]{:S(2)}, u32[]{:S(2)}) async-start(f32[8,1,12288]{2,1,0:T(1,128)} %reshape.600), calls=%async_computation | async-start | bytes 786432 | tf_op jit(solution)/shard_map/all_to_all | solution.py:70
  64.5 11.6 %copy-start = (s32[1,2048]{1,0:T(1,128)S(1)}, s32[1,2048]{1,0:T(1,128)}, u32[]{:S(2)}) copy-start(s32[1,2048]{1,0:T(1,128)} %param.19) | copy-start | bytes 24580
  72.3 10.6 %copy-start.54 = (f32[8,1,12288]{2,1,0:T(1,128)}, f32[8,1,12288]{2,1,0:T(1,128)S(1)}, u32[]{:S(2)}) copy-start(f32[8,1,12288]{2,1,0:T(1,128)S(1)} %all-to-all-done) | copy-start | bytes 1179652
  72.3 21.0 %all-to-all-start.1 = ((f32[8,1,12288]{2,1,0:T(1,128)}), f32[8,1,12288]{2,1,0:T(1,128)S(1)}, u32[]{:S(2)}, u32[]{:S(2)}) async-start(f32[8,1,12288]{2,1,0:T(1,128)} %reshape.598), calls=%async_computation.1 | async-start | bytes 786432 | tf_op jit(solution)/shard_map/all_to_all | solution.py:70
  76.2 6.8 %copy-start.65 = (s32[2048,1]{0,1:T(1,128)}, s32[2048,1]{0,1:T(1,128)S(1)}, u32[]{:S(2)}) copy-start(s32[2048,1]{0,1:T(1,128)S(1)} %compare_select_fusion.1) | copy-start | bytes 24580
  93.3 6.6 %copy-start.56 = (f32[8,1,12288]{2,1,0:T(1,128)}, f32[8,1,12288]{2,1,0:T(1,128)S(1)}, u32[]{:S(2)}) copy-start(f32[8,1,12288]{2,1,0:T(1,128)S(1)} %all-to-all-done.1) | copy-start | bytes 1179652
  94.2 18.5 %all-to-all-start.4 = ((f32[8,8,2048]{2,1,0:T(8,128)}), f32[8,8,2048]{2,1,0:T(8,128)}, u32[]{:S(2)}, u32[]{:S(2)}) async-start(f32[8,8,2048]{2,1,0:T(8,128)} %broadcast_in_dim.96), calls=%async_computation.4 | async-start | bytes 1048576 | tf_op jit(solution)/shard_map/all_to_all | solution.py:46
  106.8 2.0 copy-start.57
  171.1 1.9 copy-start.23
  174.3 3.0 copy-start.17
  176.1 2.5 copy-start.9
  178.6 4.1 copy-start.13
  182.7 2.5 copy-start.15
  192.5 4.6 copy-start.27
  192.5 4.6 copy-start.29
  197.1 2.2 copy-start.28
  201.0 2.2 copy-start.4
  202.1 3.0 copy-start.22
  205.1 2.7 copy-start.16
  207.8 2.8 copy-start.20
  212.4 2.9 copy-start.8
  217.3 1.9 copy-start.12
  225.1 1.9 copy-start.6
  228.9 1.9 copy-start.10
  239.6 2.0 copy-start.26
  322.5 1.9 copy-start.23
  325.8 3.0 copy-start.17
  327.5 2.5 copy-start.9
  330.0 3.9 copy-start.13
  333.9 2.5 copy-start.15
  343.7 4.6 copy-start.27
  343.7 4.6 copy-start.29
  348.3 2.4 copy-start.28
  352.4 2.2 copy-start.4
  353.5 3.0 copy-start.22
  356.5 2.7 copy-start.16
  359.2 2.8 copy-start.20
  363.8 2.9 copy-start.8
  368.7 1.9 copy-start.12
  376.3 1.9 copy-start.6
  380.0 1.9 copy-start.10
  390.9 2.0 copy-start.26
  427.5 14.8 %all-to-all-start.6 = ((f32[8,8,2048]{2,1,0:T(8,128)}), f32[8,8,2048]{2,1,0:T(8,128)}, u32[]{:S(2)}, u32[]{:S(2)}) async-start(f32[8,8,2048]{2,1,0:T(8,128)} %bitcast.77), calls=%async_computation.6 | async-start | bytes 1048576 | tf_op jit(solution)/shard_map/all_to_all | solution.py:89
  442.3 25.3 %all-to-all-start.5 = ((f32[8,1,49152]{2,1,0:T(1,128)}), f32[8,1,49152]{2,1,0:T(1,128)S(1)}, u32[]{:S(2)}, u32[]{:S(2)}) async-start(f32[8,1,49152]{2,1,0:T(1,128)} %reshape.606), calls=%async_computation.5 | async-start | bytes 3145728 | tf_op jit(solution)/shard_map/all_to_all | solution.py:77
  483.8 6.7 %copy-start.66 = (s32[2048,1]{0,1:T(1,128)S(1)}, s32[2048,1]{0,1:T(1,128)}, u32[]{:S(2)}) copy-start(s32[2048,1]{0,1:T(1,128)} %copy-done.65) | copy-start | bytes 24580
  534.9 6.0 %copy-start.48 = (f32[8,1,2,8,512]{4,3,2,1,0:T(8,128)}, f32[8,1,2,8,512]{4,3,2,1,0:T(8,128)S(1)}, u32[]{:S(2)}) copy-start(f32[8,1,2,8,512]{4,3,2,1,0:T(8,128)S(1)} %neg.168) | copy-start | bytes 786436
  537.9 3.0 copy-start.50
  537.9 3.0 copy-start.61
  542.4 2.3 copy-start.39
  559.1 8.9 %collective-permute-start.4 = (f32[8,6,2,512]{3,0,2,1:T(8,128)S(1)}, f32[8,6,2,512]{3,0,2,1:T(8,128)S(1)}, u32[]{:S(2)}, u32[]{:S(2)}) collective-permute-start(f32[8,6,2,512]{3,0,2,1:T(8,128)S(1)} %get-tuple-element.436), channel_id=1, source_target_pairs={{0,1},{1,2},{2,3},{3,4},{4,5},{5,6},{6,7},{7,8},{8,9},{9,10},{10,1... | collective-permute-start | bytes 589832 | tf_op jit(solution)/shard_map/ppermute | solution.py:29
  567.3 9.0 %collective-permute-start.5 = (f32[8,6,2,512]{3,0,2,1:T(8,128)S(1)}, f32[8,6,2,512]{3,0,2,1:T(8,128)S(1)}, u32[]{:S(2)}, u32[]{:S(2)}) collective-permute-start(f32[8,6,2,512]{3,0,2,1:T(8,128)S(1)} %get-tuple-element.435), channel_id=1, source_target_pairs={{1,0},{2,1},{3,2},{4,3},{5,4},{6,5},{7,6},{8,7},{9,8},{10,9},{11,1... | collective-permute-start | bytes 589832 | tf_op jit(solution)/shard_map/ppermute | solution.py:31
  584.0 2.7 collective-permute-start.6
  584.2 8.8 %collective-permute-start.7 = (f32[8,6,2,512]{3,0,2,1:T(8,128)S(1)}, f32[8,6,2,512]{3,0,2,1:T(8,128)S(1)}, u32[]{:S(2)}, u32[]{:S(2)}) collective-permute-start(f32[8,6,2,512]{3,0,2,1:T(8,128)S(1)} %get-tuple-element.433), channel_id=1, source_target_pairs={{1,0},{2,1},{3,2},{4,3},{5,4},{6,5},{7,6},{8,7},{9,8},{10,9},{11,1... | collective-permute-start | bytes 589832 | tf_op jit(solution)/shard_map/ppermute | solution.py:31
  (48 other events, 61.7 us)
where the time goes:
time: 603 us; the launch traced here: 595 us
  local copies, waits for them, and re-layouts  237 us (39%)
  matrix products  150 us (25%)
  other arithmetic  99 us (16%)
  starting transfers between devices  47.8 us (8%)
  waiting for transfers between devices  46.1 us (8%)
  loops' own time  13 us (2%)
    dot_general x22, matrix products, analyse(): jnp.einsum('pij,pjk->pik', factor, inverse_root, precision=highest)  38.3 us
    dot_general x22, matrix products, analyse(): jnp.einsum('pij,pjk->pik', inverse_root, root_iter, precision=highest)  37.9 us
    unnamed x108, local copies, waits for them, and re-layouts  33.7 us
    dot_general x18, matrix products, analyse(): root_iter = jnp.einsum('pij,pjk->pik', root_iter, factor, precision=highest)  29.9 us
    scatter-add x2, other arithmetic, analyse(): picked = obs_ens[:, patch_lists]  23.7 us
    gather x4, local copies, waits for them, and re-layouts, analyse(): obs_errors[patch_lists]  23.7 us
    gather x4, local copies, waits for them, and re-layouts, analyse(): located = obs_cells[patch_lists]  23.7 us
    gather x4, local copies, waits for them, and re-layouts, analyse(): innovation = obs_values[patch_lists] - mean_obs  23.7 us
  transfers between devices with their start and end apart: 15, of which 7 were waited for; matrix products, arithmetic and copies ran while one was open for 12% of the time, Pallas kernels for 0%

commit v1 on v0

v1 whole, which is shorter than its diff:
```python
import functools
import math

import jax
import jax.numpy as jnp
from jax import lax
from jax.experimental import pallas as pl
from jax.experimental.pallas import tpu as pltpu
from jax.sharding import PartitionSpec as P

VARS = 6
ROWS = 8
COLS = 512
MEMBERS = 64
PER_DEV = 8
STRIDE = VARS * ROWS
NOBS = 2048
WINDOW = 80
LOCAL_OBS = 320
QUADS = 16
LOC_R = 8

time_step = 0.2
f32 = jnp.float32
bf16 = jnp.bfloat16
VMEM_LIMIT = 50 * 1024 * 1024


def call(kernel, outs, scratch, flops, moved, *args):
    spec = pl.BlockSpec(memory_space=pltpu.VMEM)
    return pl.pallas_call(
        kernel,
        out_shape=[jax.ShapeDtypeStruct(s, f32) for s in outs],
        in_specs=[spec] * len(args),
        out_specs=[spec] * len(outs),
        scratch_shapes=scratch,
        compiler_params=pltpu.CompilerParams(vmem_limit_bytes=VMEM_LIMIT),
        cost_estimate=pl.CostEstimate(flops=flops, bytes_accessed=moved, transcendentals=0),
    )(*args)


def lane_shift(q, by):
    return pltpu.roll(q, by % COLS, 1)


def col_diff(q):
    near = lane_shift(q, -1) - lane_shift(q, 1)
    far = lane_shift(q, -2) - lane_shift(q, 2)
    return near * (8.0 / 12.0) - far * (1.0 / 12.0)


def row_diff(ref, v, i):
    near = ref[v, i + 1] - ref[v, i - 1]
    far = ref[v, i + 2] - ref[v, i - 2]
    return near * (8.0 / 12.0) - far * (1.0 / 12.0)


def tendency(ref, i):
    rates = [None] * VARS
    for l in range(2):
        u, v, b = ref[l, i], ref[2 + l, i], ref[4 + l, i]
        ru, rv, rb = (row_diff(ref, k + l, i) for k in (0, 2, 4))
        cu, cv, cb = col_diff(u), col_diff(v), col_diff(b)
        rates[l] = 0.5 * v - (u * ru + v * cu) - rb + 0.3 * (ref[1 - l, i] - u)
        rates[2 + l] = -0.5 * u - (u * rv + v * cv) - cb + 0.3 * (ref[3 - l, i] - v)
        rates[4 + l] = -(u * rb + v * cb) - (ru + cv) + 0.3 * (ref[5 - l, i] - b)
    return rates


def planes_of(x_ref, v):
    return jnp.swapaxes(x_ref[:, v], 0, 1)


def edge_kernel(x_ref, first_ref, last_ref):
    for v in range(VARS):
        planes = planes_of(x_ref, v)
        first_ref[4 * v : 4 * v + 4] = planes[:4]
        last_ref[4 * v : 4 * v + 4] = planes[4:]


def pack_planes(even, odd, store):
    low = lax.broadcasted_iota(jnp.int32, (PER_DEV, 128), 1) < 64
    for t in range(4):
        a, b = even[:, 128 * t : 128 * t + 128], odd[:, 128 * t : 128 * t + 128]
        store(2 * t, jnp.where(low, a, pltpu.roll(b, 64, 1)))
        store(2 * t + 1, jnp.where(low, pltpu.roll(a, 64, 1), b))


def unpack_planes(load):
    low = lax.broadcasted_iota(jnp.int32, (PER_DEV, 128), 1) < 64
    even, odd = [], []
    for t in range(4):
        a, b = load(2 * t), load(2 * t + 1)
        even.append(jnp.where(low, a, pltpu.roll(b, 64, 1)))
        odd.append(jnp.where(low, pltpu.roll(a, 64, 1), b))
    return jnp.concatenate(even, axis=1), jnp.concatenate(odd, axis=1)


def cot_kernel(x_ref, out_ref):
    for v in range(VARS):
        planes = planes_of(x_ref, v)
        for r in range(4):

            def store(d, value, t=v * 4 + r):
                out_ref[d, t] = value

            pack_planes(planes[2 * r], planes[2 * r + 1], store)


def load_state(s_ref, x_ref, top_ref, bot_ref):
    for v in range(VARS):
        s_ref[v, 4:12] = planes_of(x_ref, v)
        for r in range(4):
            s_ref[v, r] = top_ref[v * 4 + r]
            s_ref[v, 12 + r] = bot_ref[v * 4 + r]


def forward_kernel(
    x_ref, top_ref, bot_ref, sel_ref, out_ref, mid_ref, first_ref, last_ref, s_ref, fore_ref
):
    load_state(s_ref, x_ref, top_ref, bot_ref)

    def middle(i, carry):
        rates = tendency(s_ref, i + 2)
        for v in range(VARS):
            mid_ref[v, i] = s_ref[v, i + 2] + time_step * rates[v]
        return carry

    lax.fori_loop(0, 12, middle, 0)

    def finish(i, carry):
        rates = tendency(mid_ref, i + 2)
        for v in range(VARS):
            fore_ref[v, i] = 0.5 * (s_ref[v, i + 4] + mid_ref[v, i + 2]) + 0.5 * time_step * rates[v]
        return carry

    lax.fori_loop(0, ROWS, finish, 0)

    for v in range(VARS):
        for r in range(2):
            first_ref[v * 2 + r] = mid_ref[v, 4 + r]
            last_ref[v * 2 + r] = mid_ref[v, 6 + r]

    def pack(v, carry):
        for r in range(4):

            def store(d, value, r=r):
                out_ref[d, v * 4 + r] = value

            pack_planes(fore_ref[v, 2 * r], fore_ref[v, 2 * r + 1], store)
        return carry

    lax.fori_loop(0, VARS, pack, 0)

    for o in range(4):
        chosen = jnp.broadcast_to(sel_ref[o : o + 1, :], (PER_DEV, COLS))

        def pick(v, acc, chosen=chosen):
            for r in range(ROWS):
                acc = jnp.where(chosen == v * ROWS + r, fore_ref[v, r], acc)
            return acc

        seen = lax.fori_loop(0, VARS, pick, jnp.zeros((PER_DEV, COLS), f32))
        for d in range(8):
            out_ref[d, 24 + o] = lane_shift(seen, 8 - 64 * d)[:, :128]


def collect_kernel(got_ref, sel_ref, g_ref, first_ref, last_ref):
    lane = lax.broadcasted_iota(jnp.int32, (PER_DEV, 128), 1)
    sums, chosen = [], []
    for o in range(4):
        total = jnp.zeros((PER_DEV, COLS), f32)
        for d in range(8):
            piece = jnp.where(lane < WINDOW, got_ref[d, 24 + o], 0.0)
            wide = jnp.concatenate([piece, jnp.zeros((PER_DEV, COLS - 128), f32)], axis=1)
            total = total + lane_shift(wide, 64 * d - 8)
        sums.append(total)
        chosen.append(jnp.broadcast_to(sel_ref[o : o + 1, :], (PER_DEV, COLS)))

    for v in range(VARS):
        for r in range(4):
            pair = unpack_planes(lambda d: got_ref[d, v * 4 + r])
            for k in range(2):
                row = 2 * r + k
                value = pair[k]
                for o in range(4):
                    value = value + jnp.where(chosen[o] == v * ROWS + row, sums[o], 0.0)
                g_ref[v * ROWS + row] = value
                if row < 4:
                    first_ref[v * 4 + row] = value
                else:
                    last_ref[v * 4 + row - 4] = value


def place_kernel(got_ref, out_ref):
    for v in range(VARS):
        planes = []
        for r in range(4):
            planes.extend(unpack_planes(lambda d: got_ref[d, v * 4 + r]))
        out_ref[:, v] = jnp.swapaxes(jnp.stack(planes), 0, 1)


def pull_products(s_ref, g_ref, prod_ref, start, stop):
    def body(i, carry):
        for l in range(2):
            u = s_ref[l, i]
            gu, gv, gb = g_ref[l, i], g_ref[2 + l, i], g_ref[4 + l, i]
            prod_ref[l, i] = u * gu + gb
            prod_ref[2 + l, i] = u * gv
            prod_ref[4 + l, i] = u * gb + gu
        return carry

    lax.fori_loop(start, stop, body, 0)


def pull_row(s_ref, g_ref, prod_ref, i):
    out = [None] * VARS
    for l in range(2):
        u, v, b = s_ref[l, i], s_ref[2 + l, i], s_ref[4 + l, i]
        gu, gv, gb = g_ref[l, i], g_ref[2 + l, i], g_ref[4 + l, i]
        ru, rv, rb = (row_diff(s_ref, k + l, i) for k in (0, 2, 4))
        cu, cv, cb = col_diff(u), col_diff(v), col_diff(b)
        out[l] = (
            row_diff(prod_ref, l, i) + col_diff(v * gu)
            - (gu * ru + gv * rv + gb * rb) - 0.5 * gv + 0.3 * (g_ref[1 - l, i] - gu)
        )
        out[2 + l] = (
            row_diff(prod_ref, 2 + l, i) + col_diff(v * gv + gb)
            - (gu * cu + gv * cv + gb * cb) + 0.5 * gu + 0.3 * (g_ref[3 - l, i] - gv)
        )
        out[4 + l] = (
            row_diff(prod_ref, 4 + l, i) + col_diff(v * gb + gv) + 0.3 * (g_ref[5 - l, i] - gb)
        )
    return out


def backward_kernel(
    x_ref, top_ref, bot_ref, mid_ref, mid_top_ref, mid_bot_ref, g_ref, g_top_ref, g_bot_ref,
    out_ref, s_ref, m_ref, c_ref, prod_ref, gm_ref,
):
    load_state(s_ref, x_ref, top_ref, bot_ref)
    for v in range(VARS):
        for r in range(2):
            m_ref[v, r] = mid_top_ref[v * 2 + r]
            m_ref[v, 14 + r] = mid_bot_ref[v * 2 + r]
        for r in range(12):
            m_ref[v, 2 + r] = mid_ref[v, r]
        for r in range(ROWS):
            c_ref[v, 4 + r] = g_ref[v * ROWS + r]
        for r in range(4):
            c_ref[v, r] = g_top_ref[v * 4 + r]
            c_ref[v, 12 + r] = g_bot_ref[v * 4 + r]

    pull_products(m_ref, c_ref, prod_ref, 0, 16)

    def second(i, carry):
        got = pull_row(m_ref, c_ref, prod_ref, i)
        for v in range(VARS):
            gm_ref[v, i] = 0.5 * time_step * got[v]
        return carry

    lax.fori_loop(2, 14, second, 0)

    def combine(i, carry):
        for v in range(VARS):
            g, gm = c_ref[v, i], gm_ref[v, i]
            c_ref[v, i] = 0.5 * time_step * g + time_step * gm
            gm_ref[v, i] = g + gm
        return carry

    lax.fori_loop(2, 14, combine, 0)
    pull_products(s_ref, c_ref, prod_ref, 2, 14)

    def first(i, carry):
        got = pull_row(s_ref, c_ref, prod_ref, i)
        for v in range(VARS):
            gm_ref[v, i] = gm_ref[v, i] + got[v]
        return carry

    lax.fori_loop(4, 12, first, 0)
    for v in range(VARS):
        out_ref[:, v] = jnp.swapaxes(gm_ref[v, 4:12], 0, 1)


def halves(x):
    high = x.astype(bf16)
    return high, (x - high.astype(f32)).astype(bf16)


def dot(a, b):
    return lax.dot_general(a, b, (((1,), (0,)), ((), ())), preferred_element_type=f32)


def dot_first(a, b):
    return lax.dot_general(a, b, (((0,), (0,)), ((), ())), preferred_element_type=f32)


def times(left, right, product=dot):
    lh, ll = left
    rh, rl = right
    return product(lh, rh) + (product(lh, rl) + product(ll, rh))


def stack(*parts):
    return tuple(jnp.concatenate(p, axis=0) for p in zip(*parts))


def analysis_kernel(
    fore_ref, cot_ref, list_ref, meta_ref, up_ref, gr_ref, x_ref, c_ref, y_ref, d_ref, go_ref, block_ref
):
    width = 4 * MEMBERS
    block_row = lax.broadcasted_iota(jnp.int32, (width, width), 0) // MEMBERS
    block_col = lax.broadcasted_iota(jnp.int32, (width, width), 1) // MEMBERS
    block_ref[...] = jnp.where(block_row == block_col, 1.0, 0.0).astype(bf16)

    for src, dst in ((fore_ref, x_ref), (cot_ref, c_ref)):

        def turn(v, carry, src=src, dst=dst):
            for h in range(2):
                tall = [src[s, v * 4 + 2 * h + k] for k in range(2) for s in range(8)]
                dst[v, :, 128 * h : 128 * h + 128] = jnp.concatenate(tall, axis=0).T
            return carry

        lax.fori_loop(0, VARS, turn, 0)

    for o in range(4):
        tall = [fore_ref[s, 24 + o] for s in range(8)]
        seen = jnp.concatenate(tall + tall, axis=0).T[:WINDOW]
        mean = jnp.sum(seen, axis=1, keepdims=True) * (1.0 / 128.0)
        spread = seen - mean
        at = pl.ds(o, WINDOW, stride=4)
        y_ref[at, :] = spread
        d_ref[at, :] = meta_ref[0, at, :] - mean
    go_ref[...] = jnp.zeros(go_ref.shape, f32)

    def block_of(pair):
        mask = block_ref[...]
        return tuple(jnp.concatenate([p] * 4, axis=0) * mask for p in pair)

    def block_sum(x):
        high, low = halves(x)
        return dot(high, block_ref[...]) + dot(low, block_ref[...])

    def row_sum(x):
        return block_sum(jnp.broadcast_to(jnp.sum(x, axis=0, keepdims=True), (8, width)))

    def one_row(x, right):
        return times(halves(x), right)

    lane = lax.broadcasted_iota(jnp.int32, (MEMBERS, width), 1)
    sub = lax.broadcasted_iota(jnp.int32, (MEMBERS, width), 0)
    identity = jnp.where(lane % MEMBERS == sub, 1.0, 0.0)
    entry = lax.broadcasted_iota(jnp.int32, (WINDOW, width), 0)
    patch_row = (lax.broadcasted_iota(jnp.int32, (WINDOW, width), 1) // MEMBERS).astype(f32)
    col_gap = (entry // 4).astype(f32) - 9.5
    col_gap_sq = col_gap * col_gap
    left_half = lax.broadcasted_iota(jnp.int32, (96, width), 0) % 8 < 4
    row8 = lax.broadcasted_iota(jnp.int32, (8, width), 0)

    def solve(quad):
        at = pl.ds(pl.multiple_of(16 * quad, 16), WINDOW)
        lists = list_ref[pl.ds(quad, 1), :]
        hits = jnp.where(jnp.broadcast_to(lists, (WINDOW, width)) == entry, 1.0, 0.0).astype(bf16)
        count = dot(hits, block_ref[...])
        obs_row = jnp.concatenate([meta_ref[1, at, :]] * 2, axis=1)
        error = jnp.concatenate([meta_ref[2, at, :]] * 2, axis=1)
        row_gap = obs_row - 2.0 * patch_row - 0.5
        weight = count * jnp.exp((row_gap * row_gap + col_gap_sq) * (-1.0 / (2.0 * LOC_R * LOC_R))) / error
        y = y_ref[at, :]
        scaled = weight * jnp.concatenate([y, y], axis=1)
        d = d_ref[at, :]
        gain = weight * jnp.concatenate([d, d], axis=1)
        scaled_pair = halves(scaled)
        gram = times(halves(y[:, :MEMBERS]), scaled_pair, dot_first) + (MEMBERS - 1.0) * identity
        inv = lax.rsqrt(row_sum(gram * gram))
        t0 = gram * inv[:1]
        forcing = jnp.sum(scaled * jnp.concatenate([d, d], axis=1), axis=0, keepdims=True)
        forcing = jnp.broadcast_to(forcing, (8, width))

        m0 = 1.5 * identity - 0.5 * t0
        z1 = halves(m0)
        r0 = block_of(z1)
        t0p = halves(t0)
        u0 = halves(times(t0p, r0))
        t1f = times(u0, r0)
        t1 = halves(t1f)
        r1 = block_of(halves(1.5 * identity - 0.5 * t1f))
        both = times(stack(z1, t1), r1)
        z2, u1 = halves(both[:MEMBERS]), halves(both[MEMBERS:])
        t2f = times(u1, r1)
        t2 = halves(t2f)
        r2 = block_of(halves(1.5 * identity - 0.5 * t2f))
        both = times(stack(z2, t2), r2)
        z3, u2 = halves(both[:MEMBERS]), halves(both[MEMBERS:])
        t3f = times(u2, r2)
        r3 = block_of(halves(1.5 * identity - 0.5 * t3f))
        z4 = block_of(halves(times(z3, r3)))
        half_way = one_row(forcing, z4)
        mean_weight = one_row(half_way, z4) * inv
        state = (t0, t0p, u0, t1, u1, t2, u2, z1, z2, z3, r0, r1, r2, r3)
        return at, inv, z4, forcing, half_way, mean_weight, scaled, scaled_pair, gain, state

    def pull_root(e, state):
        t0, t0p, u0, t1, u1, t2, u2, z1, z2, z3, r0, r1, r2, r3 = state
        dt0 = halves(e)
        dm = halves(-0.5 * e)
        s0 = block_of(dm)
        du0 = halves(times(dt0, r0) + times(t0p, s0))
        dt1f = times(du0, r0) + times(u0, s0)
        dt1 = halves(dt1f)
        s1 = block_of(halves(-0.5 * dt1f))
        both = times(stack(dm, dt1), r1) + times(stack(z1, t1), s1)
        dz2, du1 = halves(both[:MEMBERS]), halves(both[MEMBERS:])
        dt2f = times(du1, r1) + times(u1, s1)
        dt2 = halves(dt2f)
        s2 = block_of(halves(-0.5 * dt2f))
        both = times(stack(dz2, dt2), r2) + times(stack(z2, t2), s2)
        dz3, du2 = halves(both[:MEMBERS]), halves(both[MEMBERS:])
        dt3f = times(du2, r2) + times(u2, s2)
        s3 = block_of(halves(-0.5 * dt3f))
        return times(dz3, r3) + times(z3, s3)

    def fold(x):
        x = x[:, :128] + x[:, 128:]
        return x + pltpu.roll(x, 64, 1)

    def pair_of_quads(p, carry):
        pieces = [
            (v, pl.ds(pl.multiple_of(64 * k + 8 * p, 8), 8)) for v in range(VARS) for k in range(2)
        ]
        x = jnp.concatenate([x_ref[v, at, :] for v, at in pieces], axis=0)
        c = jnp.concatenate([c_ref[v, at, :] for v, at in pieces], axis=0)
        both = block_sum(jnp.concatenate([x, c], axis=0))
        centre = both[:96] * (1.0 / MEMBERS)
        c_sum = both[96:]
        a = x - centre
        a_c = halves(jnp.concatenate([a, c], axis=0))

        updates, pulls = [], []
        for q in range(2):
            at, inv, z4, forcing, half_way, mean_weight, scaled, scaled_pair, gain, state = solve(2 * p + q)
            alpha = math.sqrt(MEMBERS - 1.0) * jnp.sqrt(inv[:1])
            mine = left_half if q == 0 else jnp.logical_not(left_half)
            both = times(a_c, z4)
            moved = alpha * both[:96]
            updates.append(moved + block_sum(a * mean_weight[:1]))
            pulls.append(alpha * both[96:] + c_sum * mean_weight[:1])
            a_mine = jnp.where(mine, a, 0.0)
            g_mean = jnp.broadcast_to(jnp.sum(a_mine * c_sum, axis=0, keepdims=True), (8, width))
            g_half = one_row(g_mean, z4) * inv
            g_forcing = one_row(g_half, z4)
            left = jnp.where(row8 == 0, g_mean * inv, jnp.where(row8 == 1, g_half, 0.0))
            right = jnp.where(row8 == 0, half_way, jnp.where(row8 == 1, forcing, 0.0))
            scaled_a = a_mine * alpha
            lhs = halves(jnp.concatenate([scaled_a, c, left, right], axis=0))
            rhs = halves(jnp.concatenate([c, scaled_a, right, left], axis=0))
            full = times(lhs, rhs, dot_first)
            block = lane // MEMBERS
            e = jnp.where(
                block < 2,
                jnp.where(block == 0, full[:64], full[64:128]),
                jnp.where(block == 2, full[128:192], full[192:]),
            ) * 0.5
            g_root = pull_root(e, state)
            t0 = state[0]
            loss = jnp.sum(jnp.where(mine, c * moved, 0.0), axis=0, keepdims=True) * 0.5
            loss = loss + g_mean[:1] * mean_weight[:1] + jnp.sum(g_root * t0, axis=0, keepdims=True)
            loss = block_sum(jnp.broadcast_to(loss, (8, width)))
            g_gram = (g_root - loss[:1] * t0) * inv[:1]
            g_y = 2.0 * times(scaled_pair, block_of(halves(g_gram))) + gain * g_forcing[:1]
            g_d = scaled * g_forcing[:1]
            low = lax.broadcasted_iota(jnp.int32, (WINDOW, 128), 1) < 64
            go_ref[at, :] += jnp.where(low, fold(g_y), fold(g_d))

        update = centre + jnp.where(left_half, updates[0], updates[1])
        pull = jnp.where(left_half, pulls[0], pulls[1])
        pull = pull + (c_sum - block_sum(pull)) * (1.0 / MEMBERS)
        for n, (v, at) in enumerate(pieces):
            x_ref[v, at, :] = update[8 * n : 8 * n + 8]
            c_ref[v, at, :] = pull[8 * n : 8 * n + 8]
        return carry

    lax.fori_loop(0, QUADS // 2, pair_of_quads, 0)

    for src, dst in ((x_ref, up_ref), (c_ref, gr_ref)):

        def turn_back(v, carry, src=src, dst=dst):
            for h in range(2):
                tall = src[v, :, 128 * h : 128 * h + 128].T
                for k in range(2):
                    for s in range(8):
                        at = 64 * k + 8 * s
                        dst[s, v * 4 + 2 * h + k] = tall[at : at + 8]
            return carry

        lax.fori_loop(0, VARS, turn_back, 0)

    for o in range(4):
        got = go_ref[pl.ds(o, WINDOW, stride=4), :]
        got = got - jnp.sum(got, axis=1, keepdims=True) * (1.0 / MEMBERS)
        tall = jnp.concatenate([got, jnp.zeros((128 - WINDOW, 128), f32)], axis=0).T
        for s in range(8):
            gr_ref[s, 24 + o] = tall[8 * s : 8 * s + 8]


def ring(value, up):
    count = lax.axis_size("space")
    if up:
        pairs = [((i + 1) % count, i) for i in range(count)]
    else:
        pairs = [(i, (i + 1) % count) for i in range(count)]
    return lax.ppermute(value, "space", pairs)


def swap(value):
    return lax.all_to_all(value, "member", split_axis=0, concat_axis=0, tiled=True)


def plane_scratch(rows):
    return pltpu.VMEM((VARS, rows, PER_DEV, COLS), f32)


def shards(initial_ensemble, obs_value, obs_error, obs_location, patch_obs, cotangent):
    shape = initial_ensemble.shape
    half = (VARS * 4, PER_DEV, COLS)
    quarter = (VARS * 2, PER_DEV, COLS)
    size = 4 * PER_DEV * STRIDE * COLS

    state = initial_ensemble
    first, last = call(edge_kernel, [half, half], [], 1000, 2 * size, state)
    bot = ring(first, True)
    top = ring(last, False)

    (cot_sent,) = call(cot_kernel, [(8, 24, PER_DEV, 128)], [], 1000, 2 * size, cotangent)
    cot_owned = swap(cot_sent)

    position = lax.axis_index("member") * (NOBS // 8)
    plane = obs_location[0] // COLS
    chosen = plane.reshape(COLS, 4).T
    meta = jnp.stack([obs_value[0], (plane % ROWS).astype(f32), obs_error[0]])
    meta = jnp.concatenate([meta[:, -32:], meta, meta[:, :32]], axis=1)
    meta = lax.dynamic_slice_in_dim(meta, position, LOCAL_OBS, axis=1)
    meta = jnp.broadcast_to(meta[:, :, None], (3, LOCAL_OBS, 128))
    lists = (patch_obs[0] - position + 32) % NOBS
    lists = lists.reshape(QUADS, 256) - 16 * jnp.arange(QUADS, dtype=jnp.int32)[:, None]

    fore_sent, mid, mid_first, mid_last = call(
        forward_kernel,
        [(8, 28, PER_DEV, 128), (VARS, 12, PER_DEV, COLS), quarter, quarter],
        [plane_scratch(16), plane_scratch(ROWS)],
        10**7, 5 * size, state, top, bot, chosen,
    )
    fore_owned = swap(fore_sent)
    mid_bot = ring(mid_first, True)
    mid_top = ring(mid_last, False)

    cells = pltpu.VMEM((VARS, 128, 256), f32)
    update_sent, grad_sent = call(
        analysis_kernel,
        [(8, 24, PER_DEV, 128), (8, 28, PER_DEV, 128)],
        [
            cells, cells, pltpu.VMEM((LOCAL_OBS, 128), f32), pltpu.VMEM((LOCAL_OBS, 128), f32),
            pltpu.VMEM((LOCAL_OBS, 128), f32), pltpu.VMEM((256, 256), bf16),
        ],
        10**10, 5 * size, fore_owned, cot_owned, lists, meta,
    )
    update = swap(update_sent)
    grad = swap(grad_sent)

    g, g_first, g_last = call(
        collect_kernel, [(STRIDE, PER_DEV, COLS), half, half], [], 10**6, 3 * size, grad, chosen
    )
    g_bot = ring(g_first, True)
    g_top = ring(g_last, False)
    (analysis,) = call(place_kernel, [shape], [], 1000, 2 * size, update)
    (gradient,) = call(
        backward_kernel,
        [shape],
        [plane_scratch(16)] * 5,
        10**7, 6 * size, state, top, bot, mid, mid_top, mid_bot, g, g_top, g_bot,
    )
    return analysis, gradient


def solution(mesh):
    placed = (
        P("member", None, "space", None),
        P("space", None),
        P("space", None),
        P("space", None),
        P("space", "member", None),
        P("member", None, "space", None),
    )
    return jax.shard_map(
        shards,
        mesh=mesh,
        in_specs=placed,
        out_specs=(P("member", None, "space", None), P("member", None, "space", None)),
        check_vma=False,
    )
```

time: 603 us -> 201 us (0.33)
  the two profiles are of different devices: /device:TPU:31 before, /device:TPU:1 now
where the time goes in v1:
time: 201 us; the launch traced here: 200 us
  Pallas kernels  108 us (54%)
  waiting for transfers between devices  39 us (19%)
  starting transfers between devices  25.9 us (13%)
  blocking collectives  19.8 us (10%)
  local copies, waits for them, and re-layouts  5.91 us (3%)
    pallas_call x7, Pallas kernels, call(): pl.pallas_call(kernel, out_shape=[jax.ShapeDtypeStruct(s, f32) for s in o...  108 us
    ppermute x6, waiting for transfers between devices, ring(): return lax.ppermute(value, 'space', pairs)  28.8 us
    all_to_all x1, blocking collectives, swap(): lax.all_to_all(value, 'member', split_axis=0, concat_axis=0, tiled=True)  19.8 us
    all_to_all x3, starting transfers between devices, swap(): lax.all_to_all(value, 'member', split_axis=0, concat_axis=0, tiled=True)  15.2 us
    ppermute x6, starting transfers between devices, ring(): return lax.ppermute(value, 'space', pairs)  10.7 us
    all_to_all x3, waiting for transfers between devices, swap(): lax.all_to_all(value, 'member', split_axis=0, concat_axis=0, tiled=True)  10.2 us
    unnamed x25, local copies, waits for them, and re-layouts  5.02 us
  transfers between devices with their start and end apart: 9, of which 5 were waited for; matrix products, arithmetic and copies ran while one was open for 1% of the time, Pallas kernels for 4%

profile of v1, /device:TPU:1, one launch (start us, length us, event | category | flops | bytes accessed | tf_op | source)
XLA Modules:
  0.0 200.1 jit_solution(5158603444327893203)
XLA Ops:
  0.6 0.0 copy-start
  0.6 0.0 copy-start.2
  0.6 1.2 copy-done.2
  1.8 1.2 shard_map.79
  3.0 0.0 copy-start.8
  3.0 0.0 copy-start.9
  3.0 6.9 %all-to-all-start.1 = ((f32[8,24,8,128]{3,2,1,0:T(8,128)}), f32[8,24,8,128]{3,2,1,0:T(8,128)S(1)}, u32[]{:S(2)}, u32[]{:S(2)}) async-start(f32[8,24,8,128]{3,2,1,0:T(8,128)} %shard_map.79), calls=%async_computation.1 | async-start | bytes 1572864 | tf_op jit(solution)/shard_map/all_to_all | solution.py:516
  9.9 0.0 copy-done
  9.9 0.1 shard_map.77
  10.1 3.4 %collective-permute-start = (f32[24,8,512]{2,1,0:T(8,128)S(1)}, f32[24,8,512]{2,1,0:T(8,128)S(1)}, u32[]{:S(2)}, u32[]{:S(2)}) collective-permute-start(f32[24,8,512]{2,1,0:T(8,128)S(1)} %get-tuple-element.13), channel_id=1, source_target_pairs={{0,1},{1,2},{2,3},{3,4},{4,5},{5,6},{6,7},{7,8},{8,9},{9,10},{10,1... | collective-permute-start | bytes 1179656 | tf_op jit(solution)/shard_map/ppermute | solution.py:512
  13.4 0.0 collective-permute-start.1
  13.4 0.0 copy-done.8
  13.5 0.1 add.32
  13.5 0.5 broadcast.67
  14.0 0.0 copy-done.9
  14.0 0.7 fusion.4
  14.8 0.3 squeeze.4
  15.0 0.1 copy.8
  15.2 11.2 %collective-permute-done.top_ref = f32[24,8,512]{2,1,0:T(8,128)S(1)} collective-permute-done((f32[24,8,512]{2,1,0:T(8,128)S(1)}, f32[24,8,512]{2,1,0:T(8,128)S(1)}, u32[]{:S(2)}, u32[]{:S(2)}) %collective-permute-start) | collective-permute-done | bytes 393248 | tf_op jit(solution)/shard_map/ppermute | solution.py:512
  26.3 4.3 %collective-permute-done.1.bot_ref = f32[24,8,512]{2,1,0:T(8,128)S(1)} collective-permute-done((f32[24,8,512]{2,1,0:T(8,128)S(1)}, f32[24,8,512]{2,1,0:T(8,128)S(1)}, u32[]{:S(2)}, u32[]{:S(2)}) %collective-permute-start.1) | collective-permute-done | bytes 393248 | tf_op jit(solution)/shard_map/ppermute | solution.py:512
  30.7 5.9 %shard_map.78 = (f32[8,28,8,128]{3,2,1,0:T(8,128)}, f32[6,12,8,512]{3,2,1,0:T(8,128)S(1)}, f32[12,8,512]{2,1,0:T(8,128)S(1)}, f32[12,8,512]{2,1,0:T(8,128)S(1)}) custom-call(f32[8,6,8,512]{3,2,1,0:T(8,128)S(1)} %copy-done, f32[24,8,512]{2,1,0:T(8,128)S(1)} %collective-permute-done.top_ref, f32[24,8,512]{2,1,0:T(8,128)S(1)} %collective-permute-done.1.bot_ref, ...), custom_call_target="tpu_custom_call" | custom-call | flops 10000000 | bytes 3932160 | tf_op jit(solution)/shard_map/pallas_call | solution.py:31
  36.5 0.0 copy-start.1
  36.5 1.0 copy-done.1
  37.6 0.0 copy-start.6
  37.6 0.7 copy-done.6
  38.3 0.0 copy-start.7
  38.3 0.7 copy-done.7
  38.9 0.0 copy-start.10
  38.9 0.0 copy-start.11
  38.9 0.0 all-to-all-done.1.cot_ref
  38.9 4.7 %all-to-all-start = ((f32[8,28,8,128]{3,2,1,0:T(8,128)}), f32[8,28,8,128]{3,2,1,0:T(8,128)S(1)}, u32[]{:S(2)}, u32[]{:S(2)}) async-start(f32[8,28,8,128]{3,2,1,0:T(8,128)} %get-tuple-element.15), calls=%async_computation | async-start | bytes 1835008 | tf_op jit(solution)/shard_map/all_to_all | solution.py:516
  43.7 0.0 copy-done.10
  43.7 0.0 copy-done.11
  43.7 0.1 fusion.7
  43.8 0.1 concatenate.3
  43.9 0.1 constant_dynamic-slice_fusion
  44.0 0.1 fusion.1.list_ref
  44.1 10.1 %all-to-all-done.fore_ref = f32[8,28,8,128]{3,2,1,0:T(8,128)S(1)} async-done(((f32[8,28,8,128]{3,2,1,0:T(8,128)}), f32[8,28,8,128]{3,2,1,0:T(8,128)S(1)}, u32[]{:S(2)}, u32[]{:S(2)}) %all-to-all-start) | async-done | bytes 917536 | tf_op jit(solution)/shard_map/all_to_all | solution.py:516
  54.2 0.2 broadcast_in_dim.2.meta_ref
  54.4 89.2 %shard_map.80 = (f32[8,24,8,128]{3,2,1,0:T(8,128)S(1)}, f32[8,28,8,128]{3,2,1,0:T(8,128)S(1)}) custom-call(f32[8,28,8,128]{3,2,1,0:T(8,128)S(1)} %all-to-all-done.fore_ref, f32[8,24,8,128]{3,2,1,0:T(8,128)S(1)} %all-to-all-done.1.cot_ref, s32[16,256]{1,0:T(8,128)S(1)} %fusion.1.list_ref, f32[3,320,128]{2,1,0:T(8,128)S(1)} %broadcast_in_dim.2.meta_ref), custom_call_target="tpu_custom_call" | custom-call | flops 10000000000 | bytes 3932160 | tf_op jit(solution)/shard_map/pallas_call | solution.py:31
  143.6 0.0 copy-start.3
  143.7 19.8 %all_to_all.20.got_ref = f32[8,28,8,128]{3,2,1,0:T(8,128)S(1)} all-to-all(f32[8,28,8,128]{3,2,1,0:T(8,128)S(1)} %get-tuple-element.20), channel_id=1, replica_groups=mesh['member'=8,'space'=16] {'member'}, dimensions={0} | all-to-all | bytes 1835008 | tf_op jit(solution)/shard_map/all_to_all | solution.py:516
  163.4 0.0 copy-done.3
  163.4 3.5 %all-to-all-start.2 = ((f32[8,24,8,128]{3,2,1,0:T(8,128)}), f32[8,24,8,128]{3,2,1,0:T(8,128)S(1)}, u32[]{:S(2)}, u32[]{:S(2)}) async-start(f32[8,24,8,128]{3,2,1,0:T(8,128)} %copy-done.3), calls=%async_computation.2 | async-start | bytes 1572864 | tf_op jit(solution)/shard_map/all_to_all | solution.py:516
  167.0 1.3 shard_map.82
  168.3 0.0 copy-start.4
  168.3 0.9 copy-done.4
  169.2 0.0 copy-start.5
  169.2 3.3 %collective-permute-start.4 = (f32[24,8,512]{2,1,0:T(8,128)}, f32[24,8,512]{2,1,0:T(8,128)S(1)}, u32[]{:S(2)}, u32[]{:S(2)}) collective-permute-start(f32[24,8,512]{2,1,0:T(8,128)} %get-tuple-element.22), channel_id=1, source_target_pairs={{0,1},{1,2},{2,3},{3,4},{4,5},{5,6},{6,7},{7,8},{8,9},{9,10},{10,1... | collective-permute-start | bytes 1179656 | tf_op jit(solution)/shard_map/ppermute | solution.py:512
  172.5 0.0 collective-permute-start.5
  172.5 3.2 %collective-permute-start.2 = (f32[12,8,512]{2,1,0:T(8,128)}, f32[12,8,512]{2,1,0:T(8,128)}, u32[]{:S(2)}, u32[]{:S(2)}) collective-permute-start(f32[12,8,512]{2,1,0:T(8,128)} %copy-done.7), channel_id=1, source_target_pairs={{0,1},{1,2},{2,3},{3,4},{4,5},{5,6},{6,7},{7,8},{8,9},{9,10},{10,1... | collective-permute-start | bytes 589832 | tf_op jit(solution)/shard_map/ppermute | solution.py:512
  175.7 0.9 collective-permute-start.3
  176.6 0.0 all-to-all-done.2.got_ref
  176.6 1.2 shard_map.81
  177.8 8.9 %collective-permute-done.2.mid_top_ref = f32[12,8,512]{2,1,0:T(8,128)} collective-permute-done((f32[12,8,512]{2,1,0:T(8,128)}, f32[12,8,512]{2,1,0:T(8,128)}, u32[]{:S(2)}, u32[]{:S(2)}) %collective-permute-start.2) | collective-permute-done | bytes 196640 | tf_op jit(solution)/shard_map/ppermute | solution.py:512
  186.6 4.4 %collective-permute-done.3.mid_bot_ref = f32[12,8,512]{2,1,0:T(8,128)} collective-permute-done((f32[12,8,512]{2,1,0:T(8,128)}, f32[12,8,512]{2,1,0:T(8,128)}, u32[]{:S(2)}, u32[]{:S(2)}) %collective-permute-start.3) | collective-permute-done | bytes 196640 | tf_op jit(solution)/shard_map/ppermute | solution.py:512
  191.1 0.0 collective-permute-done.4.g_top_ref
  191.1 0.0 collective-permute-done.5.g_bot_ref
  191.1 0.0 copy-done.5
  191.1 9.0 %shard_map.83 = f32[8,6,8,512]{3,2,1,0:T(8,128)} custom-call(f32[8,6,8,512]{3,2,1,0:T(8,128)S(1)} %copy-done, f32[24,8,512]{2,1,0:T(8,128)S(1)} %collective-permute-done.top_ref, f32[24,8,512]{2,1,0:T(8,128)S(1)} %collective-permute-done.1.bot_ref, f32[6,12,8,512]{3,2,1,0:T(8,128)} %copy-done.1, f32[12,8,512]{2,1,0:T(8,128)} %collective-permute-done.2.mid_top_ref, ...), custom_call_target="tpu_custom_call" | custom-call | flops 10000000 | bytes 4718592 | tf_op jit(solution)/shard_map/pallas_call | solution.py:31
  (4 shorter events, 0.1 us)
Async XLA Ops:
  0.6 9.3 %copy-start = (f32[8,6,8,512]{3,2,1,0:T(8,128)S(1)}, f32[8,6,8,512]{3,2,1,0:T(8,128)}, u32[]{:S(2)}) copy-start(f32[8,6,8,512]{3,2,1,0:T(8,128)} %x_ref.7) | copy-start | bytes 2359300
  0.6 1.2 copy-start.2
  3.0 10.4 %copy-start.8 = (s32[1,64,64]{2,1,0:T(8,128)S(1)}, s32[1,64,64]{2,1,0:T(8,128)}, u32[]{:S(2)}) copy-start(s32[1,64,64]{2,1,0:T(8,128)} %param.10) | copy-start | bytes 49156
  3.0 11.0 %copy-start.9 = (s32[1,2048]{1,0:T(1,128)S(1)}, s32[1,2048]{1,0:T(1,128)}, u32[]{:S(2)}) copy-start(s32[1,2048]{1,0:T(1,128)} %param.9) | copy-start | bytes 24580
  3.0 35.9 %all-to-all-start.1 = ((f32[8,24,8,128]{3,2,1,0:T(8,128)}), f32[8,24,8,128]{3,2,1,0:T(8,128)S(1)}, u32[]{:S(2)}, u32[]{:S(2)}) async-start(f32[8,24,8,128]{3,2,1,0:T(8,128)} %shard_map.79), calls=%async_computation.1 | async-start | bytes 1572864 | tf_op jit(solution)/shard_map/all_to_all | solution.py:516
  10.1 16.3 %collective-permute-start = (f32[24,8,512]{2,1,0:T(8,128)S(1)}, f32[24,8,512]{2,1,0:T(8,128)S(1)}, u32[]{:S(2)}, u32[]{:S(2)}) collective-permute-start(f32[24,8,512]{2,1,0:T(8,128)S(1)} %get-tuple-element.13), channel_id=1, source_target_pairs={{0,1},{1,2},{2,3},{3,4},{4,5},{5,6},{6,7},{7,8},{8,9},{9,10},{10,1... | collective-permute-start | bytes 1179656 | tf_op jit(solution)/shard_map/ppermute | solution.py:512
  13.4 17.2 %collective-permute-start.1 = (f32[24,8,512]{2,1,0:T(8,128)S(1)}, f32[24,8,512]{2,1,0:T(8,128)S(1)}, u32[]{:S(2)}, u32[]{:S(2)}) collective-permute-start(f32[24,8,512]{2,1,0:T(8,128)S(1)} %get-tuple-element.14), channel_id=1, source_target_pairs={{1,0},{2,1},{3,2},{4,3},{5,4},{6,5},{7,6},{8,7},{9,8},{10,9},{11,1... | collective-permute-start | bytes 1179656 | tf_op jit(solution)/shard_map/ppermute | solution.py:512
  36.5 1.0 copy-start.1
  37.6 0.7 copy-start.6
  38.3 0.7 copy-start.7
  38.9 4.7 %copy-start.10 = (f32[1,2048]{1,0:T(1,128)S(1)}, f32[1,2048]{1,0:T(1,128)}, u32[]{:S(2)}) copy-start(f32[1,2048]{1,0:T(1,128)} %param.8) | copy-start | bytes 24580
  38.9 4.7 %copy-start.11 = (f32[1,2048]{1,0:T(1,128)S(1)}, f32[1,2048]{1,0:T(1,128)}, u32[]{:S(2)}) copy-start(f32[1,2048]{1,0:T(1,128)} %param.7) | copy-start | bytes 24580
  38.9 15.3 %all-to-all-start = ((f32[8,28,8,128]{3,2,1,0:T(8,128)}), f32[8,28,8,128]{3,2,1,0:T(8,128)S(1)}, u32[]{:S(2)}, u32[]{:S(2)}) async-start(f32[8,28,8,128]{3,2,1,0:T(8,128)} %get-tuple-element.15), calls=%async_computation | async-start | bytes 1835008 | tf_op jit(solution)/shard_map/all_to_all | solution.py:516
  143.6 19.8 %copy-start.3 = (f32[8,24,8,128]{3,2,1,0:T(8,128)}, f32[8,24,8,128]{3,2,1,0:T(8,128)S(1)}, u32[]{:S(2)}) copy-start(f32[8,24,8,128]{3,2,1,0:T(8,128)S(1)} %get-tuple-element.16) | copy-start | bytes 2359300
  163.4 13.2 %all-to-all-start.2 = ((f32[8,24,8,128]{3,2,1,0:T(8,128)}), f32[8,24,8,128]{3,2,1,0:T(8,128)S(1)}, u32[]{:S(2)}, u32[]{:S(2)}) async-start(f32[8,24,8,128]{3,2,1,0:T(8,128)} %copy-done.3), calls=%async_computation.2 | async-start | bytes 1572864 | tf_op jit(solution)/shard_map/all_to_all | solution.py:516
  168.3 0.9 copy-start.4
  169.2 21.9 %copy-start.5 = (f32[48,8,512]{2,1,0:T(8,128)S(1)}, f32[48,8,512]{2,1,0:T(8,128)}, u32[]{:S(2)}) copy-start(f32[48,8,512]{2,1,0:T(8,128)} %copy-done.4) | copy-start | bytes 2359300
  169.2 21.9 %collective-permute-start.4 = (f32[24,8,512]{2,1,0:T(8,128)}, f32[24,8,512]{2,1,0:T(8,128)S(1)}, u32[]{:S(2)}, u32[]{:S(2)}) collective-permute-start(f32[24,8,512]{2,1,0:T(8,128)} %get-tuple-element.22), channel_id=1, source_target_pairs={{0,1},{1,2},{2,3},{3,4},{4,5},{5,6},{6,7},{7,8},{8,9},{9,10},{10,1... | collective-permute-start | bytes 1179656 | tf_op jit(solution)/shard_map/ppermute | solution.py:512
  172.5 18.6 %collective-permute-start.5 = (f32[24,8,512]{2,1,0:T(8,128)}, f32[24,8,512]{2,1,0:T(8,128)}, u32[]{:S(2)}, u32[]{:S(2)}) collective-permute-start(f32[24,8,512]{2,1,0:T(8,128)} %get-tuple-element.23), channel_id=1, source_target_pairs={{1,0},{2,1},{3,2},{4,3},{5,4},{6,5},{7,6},{8,7},{9,8},{10,9},{11,1... | collective-permute-start | bytes 1179656 | tf_op jit(solution)/shard_map/ppermute | solution.py:512
  172.5 14.2 %collective-permute-start.2 = (f32[12,8,512]{2,1,0:T(8,128)}, f32[12,8,512]{2,1,0:T(8,128)}, u32[]{:S(2)}, u32[]{:S(2)}) collective-permute-start(f32[12,8,512]{2,1,0:T(8,128)} %copy-done.7), channel_id=1, source_target_pairs={{0,1},{1,2},{2,3},{3,4},{4,5},{5,6},{6,7},{7,8},{8,9},{9,10},{10,1... | collective-permute-start | bytes 589832 | tf_op jit(solution)/shard_map/ppermute | solution.py:512
  175.7 15.4 %collective-permute-start.3 = (f32[12,8,512]{2,1,0:T(8,128)}, f32[12,8,512]{2,1,0:T(8,128)}, u32[]{:S(2)}, u32[]{:S(2)}) collective-permute-start(f32[12,8,512]{2,1,0:T(8,128)} %copy-done.6), channel_id=1, source_target_pairs={{1,0},{2,1},{3,2},{4,3},{5,4},{6,5},{7,6},{8,7},{9,8},{10,9},{11,1... | collective-permute-start | bytes 589832 | tf_op jit(solution)/shard_map/ppermute | solution.py:512

commit v2 on v1

--- a/solution.py
+++ b/solution.py
@@ -18,6 +18,8 @@
 WINDOW = 80
 LOCAL_OBS = 320
 QUADS = 16
+HALO = 6
+PAIRS = 4
 LOC_R = 8
 
 time_step = 0.2
@@ -74,8 +76,8 @@
 def edge_kernel(x_ref, first_ref, last_ref):
     for v in range(VARS):
         planes = planes_of(x_ref, v)
-        first_ref[4 * v : 4 * v + 4] = planes[:4]
-        last_ref[4 * v : 4 * v + 4] = planes[4:]
+        first_ref[HALO * v : HALO * v + HALO] = planes[:HALO]
+        last_ref[HALO * v : HALO * v + HALO] = planes[ROWS - HALO :]
 
 
 def pack_planes(even, odd, store):
@@ -109,15 +111,13 @@
 
 def load_state(s_ref, x_ref, top_ref, bot_ref):
     for v in range(VARS):
-        s_ref[v, 4:12] = planes_of(x_ref, v)
-        for r in range(4):
-            s_ref[v, r] = top_ref[v * 4 + r]
-            s_ref[v, 12 + r] = bot_ref[v * 4 + r]
-
-
-def forward_kernel(
-    x_ref, top_ref, bot_ref, sel_ref, out_ref, mid_ref, first_ref, last_ref, s_ref, fore_ref
-):
+        s_ref[v, HALO : HALO + ROWS] = planes_of(x_ref, v)
+        for r in range(HALO):
+            s_ref[v, r] = top_ref[v * HALO + r]
+            s_ref[v, HALO + ROWS + r] = bot_ref[v * HALO + r]
+
+
+def forward_kernel(x_ref, top_ref, bot_ref, sel_ref, out_ref, mid_ref, s_ref, fore_ref):
     load_state(s_ref, x_ref, top_ref, bot_ref)
 
     def middle(i, carry):
@@ -126,20 +126,15 @@
             mid_ref[v, i] = s_ref[v, i + 2] + time_step * rates[v]
         return carry
 
-    lax.fori_loop(0, 12, middle, 0)
+    lax.fori_loop(0, 16, middle, 0)
 
     def finish(i, carry):
-        rates = tendency(mid_ref, i + 2)
+        rates = tendency(mid_ref, i + 4)
         for v in range(VARS):
-            fore_ref[v, i] = 0.5 * (s_ref[v, i + 4] + mid_ref[v, i + 2]) + 0.5 * time_step * rates[v]
+            fore_ref[v, i] = 0.5 * (s_ref[v, i + HALO] + mid_ref[v, i + 4]) + 0.5 * time_step * rates[v]
         return carry
 
     lax.fori_loop(0, ROWS, finish, 0)
-
-    for v in range(VARS):
-        for r in range(2):
-            first_ref[v * 2 + r] = mid_ref[v, 4 + r]
-            last_ref[v * 2 + r] = mid_ref[v, 6 + r]
 
     def pack(v, carry):
         for r in range(4):
@@ -200,10 +195,10 @@
         out_ref[:, v] = jnp.swapaxes(jnp.stack(planes), 0, 1)
 
 
-def pull_products(s_ref, g_ref, prod_ref, start, stop):
+def pull_products(s_ref, g_ref, prod_ref, start, stop, shift):
     def body(i, carry):
         for l in range(2):
-            u = s_ref[l, i]
+            u = s_ref[l, i + shift]
             gu, gv, gb = g_ref[l, i], g_ref[2 + l, i], g_ref[4 + l, i]
             prod_ref[l, i] = u * gu + gb
             prod_ref[2 + l, i] = u * gv
@@ -213,12 +208,12 @@
     lax.fori_loop(start, stop, body, 0)
 
 
-def pull_row(s_ref, g_ref, prod_ref, i):
+def pull_row(s_ref, g_ref, prod_ref, i, shift):
     out = [None] * VARS
     for l in range(2):
-        u, v, b = s_ref[l, i], s_ref[2 + l, i], s_ref[4 + l, i]
+        u, v, b = (s_ref[k + l, i + shift] for k in (0, 2, 4))
         gu, gv, gb = g_ref[l, i], g_ref[2 + l, i], g_ref[4 + l, i]
-        ru, rv, rb = (row_diff(s_ref, k + l, i) for k in (0, 2, 4))
+        ru, rv, rb = (row_diff(s_ref, k + l, i + shift) for k in (0, 2, 4))
         cu, cv, cb = col_diff(u), col_diff(v), col_diff(b)
         out[l] = (
             row_diff(prod_ref, l, i) + col_diff(v * gu)
@@ -235,26 +230,21 @@
 
 
 def backward_kernel(
-    x_ref, top_ref, bot_ref, mid_ref, mid_top_ref, mid_bot_ref, g_ref, g_top_ref, g_bot_ref,
-    out_ref, s_ref, m_ref, c_ref, prod_ref, gm_ref,
+    x_ref, top_ref, bot_ref, mid_ref, g_ref, g_top_ref, g_bot_ref,
+    out_ref, s_ref, c_ref, prod_ref, gm_ref,
 ):
     load_state(s_ref, x_ref, top_ref, bot_ref)
     for v in range(VARS):
-        for r in range(2):
-            m_ref[v, r] = mid_top_ref[v * 2 + r]
-            m_ref[v, 14 + r] = mid_bot_ref[v * 2 + r]
-        for r in range(12):
-            m_ref[v, 2 + r] = mid_ref[v, r]
         for r in range(ROWS):
             c_ref[v, 4 + r] = g_ref[v * ROWS + r]
         for r in range(4):
             c_ref[v, r] = g_top_ref[v * 4 + r]
             c_ref[v, 12 + r] = g_bot_ref[v * 4 + r]
 
-    pull_products(m_ref, c_ref, prod_ref, 0, 16)
+    pull_products(mid_ref, c_ref, prod_ref, 0, 16, 0)
 
     def second(i, carry):
-        got = pull_row(m_ref, c_ref, prod_ref, i)
+        got = pull_row(mid_ref, c_ref, prod_ref, i, 0)
         for v in range(VARS):
             gm_ref[v, i] = 0.5 * time_step * got[v]
         return carry
@@ -269,10 +259,10 @@
         return carry
 
     lax.fori_loop(2, 14, combine, 0)
-    pull_products(s_ref, c_ref, prod_ref, 2, 14)
+    pull_products(s_ref, c_ref, prod_ref, 2, 14, HALO - 4)
 
     def first(i, carry):
-        got = pull_row(s_ref, c_ref, prod_ref, i)
+        got = pull_row(s_ref, c_ref, prod_ref, i, HALO - 4)
         for v in range(VARS):
             gm_ref[v, i] = gm_ref[v, i] + got[v]
         return carry
@@ -298,7 +288,26 @@
 def times(left, right, product=dot):
     lh, ll = left
     rh, rl = right
-    return product(lh, rh) + (product(lh, rl) + product(ll, rh))
+    if product is dot_first:
+        return product(lh, rh) + (product(lh, rl) + product(ll, rh))
+    n = lh.shape[0]
+    if n % 16:
+        return product(lh, rh) + (product(lh, rl) + product(ll, rh))
+    both = product(jnp.concatenate([lh, ll], axis=0), rh)
+    return both[:n] + (both[n:] + product(lh, rl))
+
+
+def in_step(jobs):
+    results = [None] * len(jobs)
+    left = list(range(len(jobs)))
+    while left:
+        for n in list(left):
+            try:
+                next(jobs[n])
+            except StopIteration as done:
+                results[n] = done.value
+                left.remove(n)
+    return results
 
 
 def stack(*parts):
@@ -362,6 +371,7 @@
         lists = list_ref[pl.ds(quad, 1), :]
         hits = jnp.where(jnp.broadcast_to(lists, (WINDOW, width)) == entry, 1.0, 0.0).astype(bf16)
         count = dot(hits, block_ref[...])
+        yield
         obs_row = jnp.concatenate([meta_ref[1, at, :]] * 2, axis=1)
         error = jnp.concatenate([meta_ref[2, at, :]] * 2, axis=1)
         row_gap = obs_row - 2.0 * patch_row - 0.5
@@ -372,7 +382,9 @@
         gain = weight * jnp.concatenate([d, d], axis=1)
         scaled_pair = halves(scaled)
         gram = times(halves(y[:, :MEMBERS]), scaled_pair, dot_first) + (MEMBERS - 1.0) * identity
+        yield
         inv = lax.rsqrt(row_sum(gram * gram))
+        yield
         t0 = gram * inv[:1]
         forcing = jnp.sum(scaled * jnp.concatenate([d, d], axis=1), axis=0, keepdims=True)
         forcing = jnp.broadcast_to(forcing, (8, width))
@@ -382,21 +394,30 @@
         r0 = block_of(z1)
         t0p = halves(t0)
         u0 = halves(times(t0p, r0))
+        yield
         t1f = times(u0, r0)
+        yield
         t1 = halves(t1f)
         r1 = block_of(halves(1.5 * identity - 0.5 * t1f))
         both = times(stack(z1, t1), r1)
+        yield
         z2, u1 = halves(both[:MEMBERS]), halves(both[MEMBERS:])
         t2f = times(u1, r1)
+        yield
         t2 = halves(t2f)
         r2 = block_of(halves(1.5 * identity - 0.5 * t2f))
         both = times(stack(z2, t2), r2)
+        yield
         z3, u2 = halves(both[:MEMBERS]), halves(both[MEMBERS:])
         t3f = times(u2, r2)
+        yield
         r3 = block_of(halves(1.5 * identity - 0.5 * t3f))
         z4 = block_of(halves(times(z3, r3)))
+        yield
         half_way = one_row(forcing, z4)
+        yield
         mean_weight = one_row(half_way, z4) * inv
+        yield
         state = (t0, t0p, u0, t1, u1, t2, u2, z1, z2, z3, r0, r1, r2, r3)
         return at, inv, z4, forcing, half_way, mean_weight, scaled, scaled_pair, gain, state
 
@@ -406,25 +427,33 @@
         dm = halves(-0.5 * e)
         s0 = block_of(dm)
         du0 = halves(times(dt0, r0) + times(t0p, s0))
+        yield
         dt1f = times(du0, r0) + times(u0, s0)
+        yield
         dt1 = halves(dt1f)
         s1 = block_of(halves(-0.5 * dt1f))
         both = times(stack(dm, dt1), r1) + times(stack(z1, t1), s1)
+        yield
         dz2, du1 = halves(both[:MEMBERS]), halves(both[MEMBERS:])
         dt2f = times(du1, r1) + times(u1, s1)
+        yield
         dt2 = halves(dt2f)
         s2 = block_of(halves(-0.5 * dt2f))
         both = times(stack(dz2, dt2), r2) + times(stack(z2, t2), s2)
+        yield
         dz3, du2 = halves(both[:MEMBERS]), halves(both[MEMBERS:])
         dt3f = times(du2, r2) + times(u2, s2)
+        yield
         s3 = block_of(halves(-0.5 * dt3f))
-        return times(dz3, r3) + times(z3, s3)
+        got = times(dz3, r3) + times(z3, s3)
+        yield
+        return got
 
     def fold(x):
         x = x[:, :128] + x[:, 128:]
         return x + pltpu.roll(x, 64, 1)
 
-    def pair_of_quads(p, carry):
+    def open_pair(p):
         pieces = [
             (v, pl.ds(pl.multiple_of(64 * k + 8 * p, 8), 8)) for v in range(VARS) for k in range(2)
         ]
@@ -436,51 +465,70 @@
         a = x - centre
         a_c = halves(jnp.concatenate([a, c], axis=0))
 
-        updates, pulls = [], []
-        for q in range(2):
-            at, inv, z4, forcing, half_way, mean_weight, scaled, scaled_pair, gain, state = solve(2 * p + q)
-            alpha = math.sqrt(MEMBERS - 1.0) * jnp.sqrt(inv[:1])
-            mine = left_half if q == 0 else jnp.logical_not(left_half)
-            both = times(a_c, z4)
-            moved = alpha * both[:96]
-            updates.append(moved + block_sum(a * mean_weight[:1]))
-            pulls.append(alpha * both[96:] + c_sum * mean_weight[:1])
-            a_mine = jnp.where(mine, a, 0.0)
-            g_mean = jnp.broadcast_to(jnp.sum(a_mine * c_sum, axis=0, keepdims=True), (8, width))
-            g_half = one_row(g_mean, z4) * inv
-            g_forcing = one_row(g_half, z4)
-            left = jnp.where(row8 == 0, g_mean * inv, jnp.where(row8 == 1, g_half, 0.0))
-            right = jnp.where(row8 == 0, half_way, jnp.where(row8 == 1, forcing, 0.0))
-            scaled_a = a_mine * alpha
-            lhs = halves(jnp.concatenate([scaled_a, c, left, right], axis=0))
-            rhs = halves(jnp.concatenate([c, scaled_a, right, left], axis=0))
-            full = times(lhs, rhs, dot_first)
-            block = lane // MEMBERS
-            e = jnp.where(
-                block < 2,
-                jnp.where(block == 0, full[:64], full[64:128]),
-                jnp.where(block == 2, full[128:192], full[192:]),
-            ) * 0.5
-            g_root = pull_root(e, state)
-            t0 = state[0]
-            loss = jnp.sum(jnp.where(mine, c * moved, 0.0), axis=0, keepdims=True) * 0.5
-            loss = loss + g_mean[:1] * mean_weight[:1] + jnp.sum(g_root * t0, axis=0, keepdims=True)
-            loss = block_sum(jnp.broadcast_to(loss, (8, width)))
-            g_gram = (g_root - loss[:1] * t0) * inv[:1]
-            g_y = 2.0 * times(scaled_pair, block_of(halves(g_gram))) + gain * g_forcing[:1]
-            g_d = scaled * g_forcing[:1]
-            low = lax.broadcasted_iota(jnp.int32, (WINDOW, 128), 1) < 64
-            go_ref[at, :] += jnp.where(low, fold(g_y), fold(g_d))
-
+        return pieces, centre, c_sum, a, c, a_c
+
+    def one_quad(p, q, opened):
+        pieces, centre, c_sum, a, c, a_c = opened
+        at, inv, z4, forcing, half_way, mean_weight, scaled, scaled_pair, gain, state = yield from solve(2 * p + q)
+        alpha = math.sqrt(MEMBERS - 1.0) * jnp.sqrt(inv[:1])
+        mine = left_half if q == 0 else jnp.logical_not(left_half)
+        both = times(a_c, z4)
+        yield
+        moved = alpha * both[:96]
+        update = moved + block_sum(a * mean_weight[:1])
+        yield
+        pull = alpha * both[96:] + c_sum * mean_weight[:1]
+        a_mine = jnp.where(mine, a, 0.0)
+        g_mean = jnp.broadcast_to(jnp.sum(a_mine * c_sum, axis=0, keepdims=True), (8, width))
+        g_half = one_row(g_mean, z4) * inv
+        yield
+        g_forcing = one_row(g_half, z4)
+        yield
+        left = jnp.where(row8 == 0, g_mean * inv, jnp.where(row8 == 1, g_half, 0.0))
+        right = jnp.where(row8 == 0, half_way, jnp.where(row8 == 1, forcing, 0.0))
+        scaled_a = a_mine * alpha
+        lhs = halves(jnp.concatenate([scaled_a, c, left, right], axis=0))
+        rhs = halves(jnp.concatenate([c, scaled_a, right, left], axis=0))
+        full = times(lhs, rhs, dot_first)
+        yield
+        block = lane // MEMBERS
+        e = jnp.where(
+            block < 2,
+            jnp.where(block == 0, full[:64], full[64:128]),
+            jnp.where(block == 2, full[128:192], full[192:]),
+        ) * 0.5
+        g_root = yield from pull_root(e, state)
+        t0 = state[0]
+        loss = jnp.sum(jnp.where(mine, c * moved, 0.0), axis=0, keepdims=True) * 0.5
+        loss = loss + g_mean[:1] * mean_weight[:1] + jnp.sum(g_root * t0, axis=0, keepdims=True)
+        loss = block_sum(jnp.broadcast_to(loss, (8, width)))
+        yield
+        g_gram = (g_root - loss[:1] * t0) * inv[:1]
+        g_y = 2.0 * times(scaled_pair, block_of(halves(g_gram))) + gain * g_forcing[:1]
+        yield
+        g_d = scaled * g_forcing[:1]
+        low = lax.broadcasted_iota(jnp.int32, (WINDOW, 128), 1) < 64
+        go_ref[at, :] += jnp.where(low, fold(g_y), fold(g_d))
+        return update, pull
+
+    def close_pair(opened, updates, pulls):
+        pieces, centre, c_sum = opened[:3]
         update = centre + jnp.where(left_half, updates[0], updates[1])
         pull = jnp.where(left_half, pulls[0], pulls[1])
         pull = pull + (c_sum - block_sum(pull)) * (1.0 / MEMBERS)
         for n, (v, at) in enumerate(pieces):
             x_ref[v, at, :] = update[8 * n : 8 * n + 8]
             c_ref[v, at, :] = pull[8 * n : 8 * n + 8]
-        return carry
-
-    lax.fori_loop(0, QUADS // 2, pair_of_quads, 0)
+
+    def group_of_pairs(g, carry):
+        pairs = [PAIRS * g + k for k in range(PAIRS)]
+        opened = [open_pair(p) for p in pairs]
+        done = in_step([one_quad(p, q, o) for p, o in zip(pairs, opened) for q in range(2)])
+        for k, o in enumerate(opened):
+            close_pair(o, *zip(*done[2 * k : 2 * k + 2]))
+        return carry
+
+    lax.fori_loop(0, QUADS // (2 * PAIRS), group_of_pairs, 0)
 
     for src, dst in ((x_ref, up_ref), (c_ref, gr_ref)):
 
@@ -522,12 +570,13 @@
 
 def shards(initial_ensemble, obs_value, obs_error, obs_location, patch_obs, cotangent):
     shape = initial_ensemble.shape
+    edge = (VARS * HALO, PER_DEV, COLS)
     half = (VARS * 4, PER_DEV, COLS)
-    quarter = (VARS * 2, PER_DEV, COLS)
     size = 4 * PER_DEV * STRIDE * COLS
 
     state = initial_ensemble
-    first, last = call(edge_kernel, [half, half], [], 1000, 2 * size, state)
+    first, last = call(edge_kernel, [edge, edge], [], 1000, 2 * size, state)
+    first, last, cotangent = lax.optimization_barrier((first, last, cotangent))
     bot = ring(first, True)
     top = ring(last, False)
 
@@ -544,15 +593,13 @@
     lists = (patch_obs[0] - position + 32) % NOBS
     lists = lists.reshape(QUADS, 256) - 16 * jnp.arange(QUADS, dtype=jnp.int32)[:, None]
 
-    fore_sent, mid, mid_first, mid_last = call(
+    fore_sent, mid = call(
         forward_kernel,
-        [(8, 28, PER_DEV, 128), (VARS, 12, PER_DEV, COLS), quarter, quarter],
-        [plane_scratch(16), plane_scratch(ROWS)],
+        [(8, 28, PER_DEV, 128), (VARS, 16, PER_DEV, COLS)],
+        [plane_scratch(ROWS + 2 * HALO), plane_scratch(ROWS)],
         10**7, 5 * size, state, top, bot, chosen,
     )
     fore_owned = swap(fore_sent)
-    mid_bot = ring(mid_first, True)
-    mid_top = ring(mid_last, False)
 
     cells = pltpu.VMEM((VARS, 128, 256), f32)
     update_sent, grad_sent = call(
@@ -576,8 +623,8 @@
     (gradient,) = call(
         backward_kernel,
         [shape],
-        [plane_scratch(16)] * 5,
-        10**7, 6 * size, state, top, bot, mid, mid_top, mid_bot, g, g_top, g_bot,
+        [plane_scratch(ROWS + 2 * HALO)] + [plane_scratch(16)] * 3,
+        10**7, 6 * size, state, top, bot, mid, g, g_top, g_bot,
     )
     return analysis, gradient
 

time: 201 us -> 144 us (0.72)
  Pallas kernels: 108 us -> 51.4 us
  starting transfers between devices: 25.9 us -> 21.5 us
  waiting for transfers between devices: 39 us -> 43.3 us
    pallas_call x7, Pallas kernels: 108 us -> 51.4 us  [call(): pl.pallas_call(kernel, out_shape=[jax.ShapeDtypeStruct(s, f32) for s in o...]
    ppermute x6 -> x4, starting transfers between devices: 10.7 us -> 6.54 us  [ring(): return lax.ppermute(value, 'space', pairs)]
    all_to_all x3, waiting for transfers between devices: 10.2 us -> 13.6 us  [swap(): lax.all_to_all(value, 'member', split_axis=0, concat_axis=0, tiled=True)]
    ppermute x6 -> x4, waiting for transfers between devices: 28.8 us -> 29.7 us  [ring(): return lax.ppermute(value, 'space', pairs)]
    unnamed x25 -> x27, local copies, waits for them, and re-layouts: 5.02 us -> 4.65 us
  transfers between devices with their start and end apart: 9 -> 7, of which waited for: 5 -> 6; matrix products, arithmetic and copies ran while one was open for 1% -> 1% of each run, Pallas kernels for 4% -> 6%
where the time goes in v2:
time: 144 us; the launch traced here: 143 us
  Pallas kernels  51.4 us (36%)
  waiting for transfers between devices  43.3 us (30%)
  starting transfers between devices  21.5 us (15%)
  blocking collectives  20 us (14%)
  local copies, waits for them, and re-layouts  5.53 us (4%)
    pallas_call x7, Pallas kernels, call(): pl.pallas_call(kernel, out_shape=[jax.ShapeDtypeStruct(s, f32) for s in o...  51.4 us
    ppermute x4, waiting for transfers between devices, ring(): return lax.ppermute(value, 'space', pairs)  29.7 us
    all_to_all x1, blocking collectives, swap(): lax.all_to_all(value, 'member', split_axis=0, concat_axis=0, tiled=True)  20 us
    all_to_all x3, starting transfers between devices, swap(): lax.all_to_all(value, 'member', split_axis=0, concat_axis=0, tiled=True)  14.9 us
    all_to_all x3, waiting for transfers between devices, swap(): lax.all_to_all(value, 'member', split_axis=0, concat_axis=0, tiled=True)  13.6 us
    ppermute x4, starting transfers between devices, ring(): return lax.ppermute(value, 'space', pairs)  6.54 us
    unnamed x27, local copies, waits for them, and re-layouts  4.65 us
  transfers between devices with their start and end apart: 7, of which 6 were waited for; matrix products, arithmetic and copies ran while one was open for 1% of the time, Pallas kernels for 6%

profile of v2, /device:TPU:1, one launch (start us, length us, event | category | flops | bytes accessed | tf_op | source)
XLA Modules:
  0.0 143.3 jit_solution(13935341657699726733)
XLA Ops:
  0.6 0.0 copy-start
  0.6 1.1 copy-done
  1.8 0.9 shard_map.77
  2.7 0.0 copy-start.5
  2.7 1.1 copy-done.5
  3.8 0.0 copy-start.9
  3.8 0.0 copy-start.10
  3.8 0.0 copy-start.1
  3.9 1.2 shard_map.79
  5.0 6.8 %all-to-all-start.1 = ((f32[8,24,8,128]{3,2,1,0:T(8,128)}), f32[8,24,8,128]{3,2,1,0:T(8,128)}, u32[]{:S(2)}, u32[]{:S(2)}) async-start(f32[8,24,8,128]{3,2,1,0:T(8,128)} %shard_map.79), calls=%async_computation.1 | async-start | bytes 1572864 | tf_op jit(solution)/shard_map/all_to_all | solution.py:564
  11.8 3.3 %collective-permute-start = (f32[36,8,512]{2,1,0:T(8,128)}, f32[36,8,512]{2,1,0:T(8,128)S(1)}, u32[]{:S(2)}, u32[]{:S(2)}) collective-permute-start(f32[36,8,512]{2,1,0:T(8,128)} %get-tuple-element.16), channel_id=1, source_target_pairs={{0,1},{1,2},{2,3},{3,4},{4,5},{5,6},{6,7},{7,8},{8,9},{9,10},{10,1... | collective-permute-start | bytes 1769480 | tf_op jit(solution)/shard_map/ppermute | solution.py:560
  15.1 0.0 collective-permute-start.1
  15.1 0.0 copy-done.9
  15.1 0.1 add.32
  15.2 0.5 broadcast.67
  15.7 0.0 copy-done.10
  15.7 0.7 fusion.4
  16.4 0.3 squeeze.4
  16.6 0.1 copy.8
  16.8 0.0 copy-start.11
  16.8 0.0 copy-start.12
  16.8 15.7 %collective-permute-done.top_ref = f32[36,8,512]{2,1,0:T(8,128)S(1)} collective-permute-done((f32[36,8,512]{2,1,0:T(8,128)}, f32[36,8,512]{2,1,0:T(8,128)S(1)}, u32[]{:S(2)}, u32[]{:S(2)}) %collective-permute-start) | collective-permute-done | bytes 589856 | tf_op jit(solution)/shard_map/ppermute | solution.py:560
  32.5 4.2 %collective-permute-done.1.bot_ref = f32[36,8,512]{2,1,0:T(8,128)S(1)} collective-permute-done((f32[36,8,512]{2,1,0:T(8,128)S(1)}, f32[36,8,512]{2,1,0:T(8,128)S(1)}, u32[]{:S(2)}, u32[]{:S(2)}) %collective-permute-start.1) | collective-permute-done | bytes 589856 | tf_op jit(solution)/shard_map/ppermute | solution.py:560
  36.8 0.0 copy-done.1
  36.8 0.0 copy-start.2
  36.8 6.8 %shard_map.78 = (f32[8,28,8,128]{3,2,1,0:T(8,128)S(1)}, f32[6,16,8,512]{3,2,1,0:T(8,128)}) custom-call(f32[8,6,8,512]{3,2,1,0:T(8,128)S(1)} %copy-done.1, f32[36,8,512]{2,1,0:T(8,128)S(1)} %collective-permute-done.top_ref, f32[36,8,512]{2,1,0:T(8,128)S(1)} %collective-permute-done.1.bot_ref, s32[4,512]{1,0:T(4,128)S(1)} %fusion.3.sel_ref), custom_call_target="tpu_custom_call" | custom-call | flops 10000000 | bytes 3932160 | tf_op jit(solution)/shard_map/pallas_call | solution.py:33
  43.5 0.0 copy-start.4
  43.5 0.0 all-to-all-done.1.cot_ref
  43.5 0.9 copy-done.4
  44.5 0.0 copy-done.2
  44.5 4.6 %all-to-all-start = ((f32[8,28,8,128]{3,2,1,0:T(8,128)}), f32[8,28,8,128]{3,2,1,0:T(8,128)S(1)}, u32[]{:S(2)}, u32[]{:S(2)}) async-start(f32[8,28,8,128]{3,2,1,0:T(8,128)} %copy-done.4), calls=%async_computation | async-start | bytes 1835008 | tf_op jit(solution)/shard_map/all_to_all | solution.py:564
  49.1 0.0 copy-done.11
  49.1 0.0 copy-done.12
  49.1 0.1 fusion.7
  49.2 0.1 concatenate.3
  49.3 0.1 constant_dynamic-slice_fusion
  49.4 0.1 fusion.1.list_ref
  49.5 10.1 %all-to-all-done.fore_ref = f32[8,28,8,128]{3,2,1,0:T(8,128)S(1)} async-done(((f32[8,28,8,128]{3,2,1,0:T(8,128)}), f32[8,28,8,128]{3,2,1,0:T(8,128)S(1)}, u32[]{:S(2)}, u32[]{:S(2)}) %all-to-all-start) | async-done | bytes 917536 | tf_op jit(solution)/shard_map/all_to_all | solution.py:564
  59.6 0.2 broadcast_in_dim.2.meta_ref
  59.8 31.3 %shard_map.80 = (f32[8,24,8,128]{3,2,1,0:T(8,128)S(1)}, f32[8,28,8,128]{3,2,1,0:T(8,128)S(1)}) custom-call(f32[8,28,8,128]{3,2,1,0:T(8,128)S(1)} %all-to-all-done.fore_ref, f32[8,24,8,128]{3,2,1,0:T(8,128)} %all-to-all-done.1.cot_ref, s32[16,256]{1,0:T(8,128)S(1)} %fusion.1.list_ref, f32[3,320,128]{2,1,0:T(8,128)S(1)} %broadcast_in_dim.2.meta_ref), custom_call_target="tpu_custom_call" | custom-call | flops 10000000000 | bytes 3932160 | tf_op jit(solution)/shard_map/pallas_call | solution.py:33
  91.1 0.0 copy-start.6
  91.1 20.0 %all_to_all.20.got_ref = f32[8,28,8,128]{3,2,1,0:T(8,128)S(1)} all-to-all(f32[8,28,8,128]{3,2,1,0:T(8,128)S(1)} %get-tuple-element.22), channel_id=1, replica_groups=mesh['member'=8,'space'=16] {'member'}, dimensions={0} | all-to-all | bytes 1835008 | tf_op jit(solution)/shard_map/all_to_all | solution.py:564
  111.1 0.0 copy-done.6
  111.1 3.5 %all-to-all-start.2 = ((f32[8,24,8,128]{3,2,1,0:T(8,128)}), f32[8,24,8,128]{3,2,1,0:T(8,128)S(1)}, u32[]{:S(2)}, u32[]{:S(2)}) async-start(f32[8,24,8,128]{3,2,1,0:T(8,128)} %copy-done.6), calls=%async_computation.2 | async-start | bytes 1572864 | tf_op jit(solution)/shard_map/all_to_all | solution.py:564
  114.7 1.3 shard_map.82
  116.0 0.0 copy-start.7
  116.0 0.9 copy-done.7
  116.9 0.0 copy-start.3
  116.9 3.2 %collective-permute-start.2 = (f32[24,8,512]{2,1,0:T(8,128)}, f32[24,8,512]{2,1,0:T(8,128)S(1)}, u32[]{:S(2)}, u32[]{:S(2)}) collective-permute-start(f32[24,8,512]{2,1,0:T(8,128)} %get-tuple-element.24), channel_id=1, source_target_pairs={{0,1},{1,2},{2,3},{3,4},{4,5},{5,6},{6,7},{7,8},{8,9},{9,10},{10,1... | collective-permute-start | bytes 1179656 | tf_op jit(solution)/shard_map/ppermute | solution.py:560
  120.1 0.0 collective-permute-start.3
  120.1 3.4 %all-to-all-done.2.got_ref = f32[8,24,8,128]{3,2,1,0:T(8,128)S(1)} async-done(((f32[8,24,8,128]{3,2,1,0:T(8,128)}), f32[8,24,8,128]{3,2,1,0:T(8,128)S(1)}, u32[]{:S(2)}, u32[]{:S(2)}) %all-to-all-start.2) | async-done | bytes 786464 | tf_op jit(solution)/shard_map/all_to_all | solution.py:564
  123.5 0.0 copy-start.8
  123.5 1.2 shard_map.81
  124.7 5.5 %collective-permute-done.2.g_top_ref = f32[24,8,512]{2,1,0:T(8,128)S(1)} collective-permute-done((f32[24,8,512]{2,1,0:T(8,128)}, f32[24,8,512]{2,1,0:T(8,128)S(1)}, u32[]{:S(2)}, u32[]{:S(2)}) %collective-permute-start.2) | collective-permute-done | bytes 393248 | tf_op jit(solution)/shard_map/ppermute | solution.py:560
  130.1 4.3 %collective-permute-done.3.g_bot_ref = f32[24,8,512]{2,1,0:T(8,128)} collective-permute-done((f32[24,8,512]{2,1,0:T(8,128)}, f32[24,8,512]{2,1,0:T(8,128)}, u32[]{:S(2)}, u32[]{:S(2)}) %collective-permute-start.3) | collective-permute-done | bytes 393248 | tf_op jit(solution)/shard_map/ppermute | solution.py:560
  134.4 0.0 copy-done.3
  134.4 0.0 copy-done.8
  134.4 8.8 %shard_map.83 = f32[8,6,8,512]{3,2,1,0:T(8,128)} custom-call(f32[8,6,8,512]{3,2,1,0:T(8,128)S(1)} %copy-done.1, f32[36,8,512]{2,1,0:T(8,128)S(1)} %collective-permute-done.top_ref, f32[36,8,512]{2,1,0:T(8,128)S(1)} %copy-done.3, f32[6,16,8,512]{3,2,1,0:T(8,128)} %get-tuple-element.21.mid_ref, f32[48,8,512]{2,1,0:T(8,128)S(1)} %copy-done.8, ...), custom_call_target="tpu_custom_call" | custom-call | flops 10000000 | bytes 4718592 | tf_op jit(solution)/shard_map/pallas_call | solution.py:33
  (4 shorter events, 0.1 us)
Async XLA Ops:
  0.6 1.1 copy-start
  2.7 1.1 copy-start.5
  3.8 11.3 %copy-start.9 = (s32[1,64,64]{2,1,0:T(8,128)S(1)}, s32[1,64,64]{2,1,0:T(8,128)}, u32[]{:S(2)}) copy-start(s32[1,64,64]{2,1,0:T(8,128)} %param.10) | copy-start | bytes 49156
  3.8 11.9 %copy-start.10 = (s32[1,2048]{1,0:T(1,128)S(1)}, s32[1,2048]{1,0:T(1,128)}, u32[]{:S(2)}) copy-start(s32[1,2048]{1,0:T(1,128)} %param.9) | copy-start | bytes 24580
  3.8 32.9 %copy-start.1 = (f32[8,6,8,512]{3,2,1,0:T(8,128)S(1)}, f32[8,6,8,512]{3,2,1,0:T(8,128)}, u32[]{:S(2)}) copy-start(f32[8,6,8,512]{3,2,1,0:T(8,128)} %x_ref.6) | copy-start | bytes 2359300
  5.0 38.5 %all-to-all-start.1 = ((f32[8,24,8,128]{3,2,1,0:T(8,128)}), f32[8,24,8,128]{3,2,1,0:T(8,128)}, u32[]{:S(2)}, u32[]{:S(2)}) async-start(f32[8,24,8,128]{3,2,1,0:T(8,128)} %shard_map.79), calls=%async_computation.1 | async-start | bytes 1572864 | tf_op jit(solution)/shard_map/all_to_all | solution.py:564
  11.8 20.7 %collective-permute-start = (f32[36,8,512]{2,1,0:T(8,128)}, f32[36,8,512]{2,1,0:T(8,128)S(1)}, u32[]{:S(2)}, u32[]{:S(2)}) collective-permute-start(f32[36,8,512]{2,1,0:T(8,128)} %get-tuple-element.16), channel_id=1, source_target_pairs={{0,1},{1,2},{2,3},{3,4},{4,5},{5,6},{6,7},{7,8},{8,9},{9,10},{10,1... | collective-permute-start | bytes 1769480 | tf_op jit(solution)/shard_map/ppermute | solution.py:560
  15.1 21.7 %collective-permute-start.1 = (f32[36,8,512]{2,1,0:T(8,128)S(1)}, f32[36,8,512]{2,1,0:T(8,128)S(1)}, u32[]{:S(2)}, u32[]{:S(2)}) collective-permute-start(f32[36,8,512]{2,1,0:T(8,128)S(1)} %get-tuple-element.17), channel_id=1, source_target_pairs={{1,0},{2,1},{3,2},{4,3},{5,4},{6,5},{7,6},{8,7},{9,8},{10,9},{11,1... | collective-permute-start | bytes 1769480 | tf_op jit(solution)/shard_map/ppermute | solution.py:560
  16.8 32.3 %copy-start.11 = (f32[1,2048]{1,0:T(1,128)S(1)}, f32[1,2048]{1,0:T(1,128)}, u32[]{:S(2)}) copy-start(f32[1,2048]{1,0:T(1,128)} %param.8) | copy-start | bytes 24580
  16.8 32.3 %copy-start.12 = (f32[1,2048]{1,0:T(1,128)S(1)}, f32[1,2048]{1,0:T(1,128)}, u32[]{:S(2)}) copy-start(f32[1,2048]{1,0:T(1,128)} %param.7) | copy-start | bytes 24580
  36.8 7.7 %copy-start.2 = (f32[36,8,512]{2,1,0:T(8,128)}, f32[36,8,512]{2,1,0:T(8,128)S(1)}, u32[]{:S(2)}) copy-start(f32[36,8,512]{2,1,0:T(8,128)S(1)} %collective-permute-done.1.bot_ref) | copy-start | bytes 1769476
  43.5 0.9 copy-start.4
  44.5 15.1 %all-to-all-start = ((f32[8,28,8,128]{3,2,1,0:T(8,128)}), f32[8,28,8,128]{3,2,1,0:T(8,128)S(1)}, u32[]{:S(2)}, u32[]{:S(2)}) async-start(f32[8,28,8,128]{3,2,1,0:T(8,128)} %copy-done.4), calls=%async_computation | async-start | bytes 1835008 | tf_op jit(solution)/shard_map/all_to_all | solution.py:564
  91.1 20.0 %copy-start.6 = (f32[8,24,8,128]{3,2,1,0:T(8,128)}, f32[8,24,8,128]{3,2,1,0:T(8,128)S(1)}, u32[]{:S(2)}) copy-start(f32[8,24,8,128]{3,2,1,0:T(8,128)S(1)} %get-tuple-element.20) | copy-start | bytes 2359300
  111.1 12.4 %all-to-all-start.2 = ((f32[8,24,8,128]{3,2,1,0:T(8,128)}), f32[8,24,8,128]{3,2,1,0:T(8,128)S(1)}, u32[]{:S(2)}, u32[]{:S(2)}) async-start(f32[8,24,8,128]{3,2,1,0:T(8,128)} %copy-done.6), calls=%async_computation.2 | async-start | bytes 1572864 | tf_op jit(solution)/shard_map/all_to_all | solution.py:564
  116.0 0.9 copy-start.7
  116.9 17.6 %copy-start.3 = (f32[36,8,512]{2,1,0:T(8,128)S(1)}, f32[36,8,512]{2,1,0:T(8,128)}, u32[]{:S(2)}) copy-start(f32[36,8,512]{2,1,0:T(8,128)} %copy-done.2) | copy-start | bytes 1769476
  116.9 13.3 %collective-permute-start.2 = (f32[24,8,512]{2,1,0:T(8,128)}, f32[24,8,512]{2,1,0:T(8,128)S(1)}, u32[]{:S(2)}, u32[]{:S(2)}) collective-permute-start(f32[24,8,512]{2,1,0:T(8,128)} %get-tuple-element.24), channel_id=1, source_target_pairs={{0,1},{1,2},{2,3},{3,4},{4,5},{5,6},{6,7},{7,8},{8,9},{9,10},{10,1... | collective-permute-start | bytes 1179656 | tf_op jit(solution)/shard_map/ppermute | solution.py:560
  120.1 14.3 %collective-permute-start.3 = (f32[24,8,512]{2,1,0:T(8,128)}, f32[24,8,512]{2,1,0:T(8,128)}, u32[]{:S(2)}, u32[]{:S(2)}) collective-permute-start(f32[24,8,512]{2,1,0:T(8,128)} %get-tuple-element.25), channel_id=1, source_target_pairs={{1,0},{2,1},{3,2},{4,3},{5,4},{6,5},{7,6},{8,7},{9,8},{10,9},{11,1... | collective-permute-start | bytes 1179656 | tf_op jit(solution)/shard_map/ppermute | solution.py:560
  123.5 10.9 %copy-start.8 = (f32[48,8,512]{2,1,0:T(8,128)S(1)}, f32[48,8,512]{2,1,0:T(8,128)}, u32[]{:S(2)}) copy-start(f32[48,8,512]{2,1,0:T(8,128)} %copy-done.7) | copy-start | bytes 2359300

commit v3 on v2

--- a/solution.py
+++ b/solution.py
@@ -126,7 +126,7 @@
             mid_ref[v, i] = s_ref[v, i + 2] + time_step * rates[v]
         return carry
 
-    lax.fori_loop(0, 16, middle, 0)
+    lax.fori_loop(0, 16, middle, 0, unroll=4)
 
     def finish(i, carry):
         rates = tendency(mid_ref, i + 4)
@@ -134,7 +134,7 @@
             fore_ref[v, i] = 0.5 * (s_ref[v, i + HALO] + mid_ref[v, i + 4]) + 0.5 * time_step * rates[v]
         return carry
 
-    lax.fori_loop(0, ROWS, finish, 0)
+    lax.fori_loop(0, ROWS, finish, 0, unroll=4)
 
     def pack(v, carry):
         for r in range(4):
@@ -145,7 +145,7 @@
             pack_planes(fore_ref[v, 2 * r], fore_ref[v, 2 * r + 1], store)
         return carry
 
-    lax.fori_loop(0, VARS, pack, 0)
+    lax.fori_loop(0, VARS, pack, 0, unroll=2)
 
     for o in range(4):
         chosen = jnp.broadcast_to(sel_ref[o : o + 1, :], (PER_DEV, COLS))
@@ -155,7 +155,7 @@
                 acc = jnp.where(chosen == v * ROWS + r, fore_ref[v, r], acc)
             return acc
 
-        seen = lax.fori_loop(0, VARS, pick, jnp.zeros((PER_DEV, COLS), f32))
+        seen = lax.fori_loop(0, VARS, pick, jnp.zeros((PER_DEV, COLS), f32), unroll=2)
         for d in range(8):
             out_ref[d, 24 + o] = lane_shift(seen, 8 - 64 * d)[:, :128]
 
@@ -205,7 +205,7 @@
             prod_ref[4 + l, i] = u * gb + gu
         return carry
 
-    lax.fori_loop(start, stop, body, 0)
+    lax.fori_loop(start, stop, body, 0, unroll=2)
 
 
 def pull_row(s_ref, g_ref, prod_ref, i, shift):
@@ -249,7 +249,7 @@
             gm_ref[v, i] = 0.5 * time_step * got[v]
         return carry
 
-    lax.fori_loop(2, 14, second, 0)
+    lax.fori_loop(2, 14, second, 0, unroll=4)
 
     def combine(i, carry):
         for v in range(VARS):
@@ -258,7 +258,7 @@
             gm_ref[v, i] = g + gm
         return carry
 
-    lax.fori_loop(2, 14, combine, 0)
+    lax.fori_loop(2, 14, combine, 0, unroll=2)
     pull_products(s_ref, c_ref, prod_ref, 2, 14, HALO - 4)
 
     def first(i, carry):
@@ -267,7 +267,7 @@
             gm_ref[v, i] = gm_ref[v, i] + got[v]
         return carry
 
-    lax.fori_loop(4, 12, first, 0)
+    lax.fori_loop(4, 12, first, 0, unroll=4)
     for v in range(VARS):
         out_ref[:, v] = jnp.swapaxes(gm_ref[v, 4:12], 0, 1)
 
@@ -576,12 +576,12 @@
 
     state = initial_ensemble
     first, last = call(edge_kernel, [edge, edge], [], 1000, 2 * size, state)
-    first, last, cotangent = lax.optimization_barrier((first, last, cotangent))
     bot = ring(first, True)
     top = ring(last, False)
-
     (cot_sent,) = call(cot_kernel, [(8, 24, PER_DEV, 128)], [], 1000, 2 * size, cotangent)
+    top, bot, cot_sent = lax.optimization_barrier((top, bot, cot_sent))
     cot_owned = swap(cot_sent)
+
 
     position = lax.axis_index("member") * (NOBS // 8)
     plane = obs_location[0] // COLS
@@ -611,7 +611,6 @@
         ],
         10**10, 5 * size, fore_owned, cot_owned, lists, meta,
     )
-    update = swap(update_sent)
     grad = swap(grad_sent)
 
     g, g_first, g_last = call(
@@ -619,6 +618,8 @@
     )
     g_bot = ring(g_first, True)
     g_top = ring(g_last, False)
+    g_top, g_bot, update_sent = lax.optimization_barrier((g_top, g_bot, update_sent))
+    update = swap(update_sent)
     (analysis,) = call(place_kernel, [shape], [], 1000, 2 * size, update)
     (gradient,) = call(
         backward_kernel,

time: 144 us -> 140 us (0.972)
  Pallas kernels: 51.4 us -> 47.8 us
  blocking collectives: 20 us -> 16.9 us
  local copies, waits for them, and re-layouts: 5.53 us -> 7.27 us
    all_to_all x3, waiting for transfers between devices: 13.6 us -> 20.3 us  [swap(): lax.all_to_all(value, 'member', split_axis=0, concat_axis=0, tiled=True)]
    ppermute x4, waiting for transfers between devices: 29.7 us -> 23.7 us  [ring(): return lax.ppermute(value, 'space', pairs)]
    pallas_call x7, Pallas kernels: 51.4 us -> 47.8 us  [call(): pl.pallas_call(kernel, out_shape=[jax.ShapeDtypeStruct(s, f32) for s in o...]
    all_to_all x1, blocking collectives: 20 us -> 16.9 us  [swap(): lax.all_to_all(value, 'member', split_axis=0, concat_axis=0, tiled=True)]
    unnamed x27 -> x23, local copies, waits for them, and re-layouts: 4.65 us -> 6.39 us
  transfers between devices with their start and end apart: 7 -> 7, of which waited for: 6 -> 7; matrix products, arithmetic and copies ran while one was open for 1% -> 1% of each run, Pallas kernels for 6% -> 10%
where the time goes in v3:
time: 140 us; the launch traced here: 139 us
  Pallas kernels  47.8 us (34%)
  waiting for transfers between devices  44 us (31%)
  starting transfers between devices  21.5 us (15%)
  blocking collectives  16.9 us (12%)
  local copies, waits for them, and re-layouts  7.27 us (5%)
    pallas_call x7, Pallas kernels, call(): pl.pallas_call(kernel, out_shape=[jax.ShapeDtypeStruct(s, f32) for s in o...  47.8 us
    ppermute x4, waiting for transfers between devices, ring(): return lax.ppermute(value, 'space', pairs)  23.7 us
    all_to_all x3, waiting for transfers between devices, swap(): lax.all_to_all(value, 'member', split_axis=0, concat_axis=0, tiled=True)  20.3 us
    all_to_all x1, blocking collectives, swap(): lax.all_to_all(value, 'member', split_axis=0, concat_axis=0, tiled=True)  16.9 us
    all_to_all x3, starting transfers between devices, swap(): lax.all_to_all(value, 'member', split_axis=0, concat_axis=0, tiled=True)  13.7 us
    ppermute x4, starting transfers between devices, ring(): return lax.ppermute(value, 'space', pairs)  7.8 us
    unnamed x23, local copies, waits for them, and re-layouts  6.39 us
  transfers between devices with their start and end apart: 7, of which 7 were waited for; matrix products, arithmetic and copies ran while one was open for 1% of the time, Pallas kernels for 10%

profile of v3, /device:TPU:1, one launch (start us, length us, event | category | flops | bytes accessed | tf_op | source)
XLA Modules:
  0.0 139.2 jit_solution(17099913812535242595)
XLA Ops:
  0.6 0.0 copy-start
  0.6 1.1 copy-done
  1.8 0.1 shard_map.77
  1.9 4.2 %collective-permute-start = (f32[36,8,512]{2,1,0:T(8,128)S(1)}, f32[36,8,512]{2,1,0:T(8,128)S(1)}, u32[]{:S(2)}, u32[]{:S(2)}) collective-permute-start(f32[36,8,512]{2,1,0:T(8,128)S(1)} %get-tuple-element.17), channel_id=1, source_target_pairs={{0,1},{1,2},{2,3},{3,4},{4,5},{5,6},{6,7},{7,8},{8,9},{9,10},{10,1... | collective-permute-start | bytes 1769480 | tf_op jit(solution)/shard_map/ppermute | solution.py:560
  6.1 0.0 copy-start.1
  6.1 0.0 collective-permute-start.1
  6.1 0.0 copy-start.2
  6.1 1.2 copy-done.2
  7.3 0.0 copy-start.7
  7.3 0.0 copy-start.8
  7.3 1.2 shard_map.78
  8.5 7.9 %collective-permute-done.top_ref = f32[36,8,512]{2,1,0:T(8,128)S(1)} collective-permute-done((f32[36,8,512]{2,1,0:T(8,128)S(1)}, f32[36,8,512]{2,1,0:T(8,128)S(1)}, u32[]{:S(2)}, u32[]{:S(2)}) %collective-permute-start) | collective-permute-done | bytes 589856 | tf_op jit(solution)/shard_map/ppermute | solution.py:560
  16.4 4.6 %collective-permute-done.1.bot_ref = f32[36,8,512]{2,1,0:T(8,128)S(1)} collective-permute-done((f32[36,8,512]{2,1,0:T(8,128)S(1)}, f32[36,8,512]{2,1,0:T(8,128)S(1)}, u32[]{:S(2)}, u32[]{:S(2)}) %collective-permute-start.1) | collective-permute-done | bytes 589856 | tf_op jit(solution)/shard_map/ppermute | solution.py:560
  20.9 6.0 %all-to-all-start.1 = ((f32[8,24,8,128]{3,2,1,0:T(8,128)}), f32[8,24,8,128]{3,2,1,0:T(8,128)S(1)}, u32[]{:S(2)}, u32[]{:S(2)}) async-start(f32[8,24,8,128]{3,2,1,0:T(8,128)} %shard_map.78), calls=%async_computation.1 | async-start | bytes 1572864 | tf_op jit(solution)/shard_map/all_to_all | solution.py:564
  26.9 0.0 copy-done.7
  26.9 0.1 add.32
  27.0 0.5 broadcast.67
  27.5 0.0 copy-done.8
  27.5 0.7 fusion.4
  28.3 0.3 squeeze.4
  28.5 0.1 copy.8
  28.7 0.0 copy-done.1
  28.7 0.0 copy-start.9
  28.7 0.0 copy-start.10
  28.7 5.4 %shard_map.79 = (f32[8,28,8,128]{3,2,1,0:T(8,128)}, f32[6,16,8,512]{3,2,1,0:T(8,128)}) custom-call(f32[8,6,8,512]{3,2,1,0:T(8,128)S(1)} %copy-done.1, f32[36,8,512]{2,1,0:T(8,128)S(1)} %collective-permute-done.top_ref, f32[36,8,512]{2,1,0:T(8,128)S(1)} %collective-permute-done.1.bot_ref, s32[4,512]{1,0:T(4,128)S(1)} %fusion.3.sel_ref), custom_call_target="tpu_custom_call" | custom-call | flops 10000000 | bytes 3932160 | tf_op jit(solution)/shard_map/pallas_call | solution.py:33
  34.1 4.8 %all-to-all-done.1.cot_ref = f32[8,24,8,128]{3,2,1,0:T(8,128)S(1)} async-done(((f32[8,24,8,128]{3,2,1,0:T(8,128)}), f32[8,24,8,128]{3,2,1,0:T(8,128)S(1)}, u32[]{:S(2)}, u32[]{:S(2)}) %all-to-all-start.1) | async-done | bytes 786464 | tf_op jit(solution)/shard_map/all_to_all | solution.py:564
  38.9 4.2 %all-to-all-start = ((f32[8,28,8,128]{3,2,1,0:T(8,128)}), f32[8,28,8,128]{3,2,1,0:T(8,128)}, u32[]{:S(2)}, u32[]{:S(2)}) async-start(f32[8,28,8,128]{3,2,1,0:T(8,128)} %get-tuple-element.21), calls=%async_computation | async-start | bytes 1835008 | tf_op jit(solution)/shard_map/all_to_all | solution.py:564
  43.1 0.0 copy-done.9
  43.1 0.0 copy-done.10
  43.2 0.1 fusion.7
  43.2 0.1 concatenate.3
  43.4 0.1 constant_dynamic-slice_fusion
  43.4 0.1 fusion.1.list_ref
  43.5 13.2 %all-to-all-done.fore_ref = f32[8,28,8,128]{3,2,1,0:T(8,128)} async-done(((f32[8,28,8,128]{3,2,1,0:T(8,128)}), f32[8,28,8,128]{3,2,1,0:T(8,128)}, u32[]{:S(2)}, u32[]{:S(2)}) %all-to-all-start) | async-done | bytes 917536 | tf_op jit(solution)/shard_map/all_to_all | solution.py:564
  56.7 0.2 broadcast_in_dim.2.meta_ref
  56.9 32.0 %shard_map.80 = (f32[8,24,8,128]{3,2,1,0:T(8,128)}, f32[8,28,8,128]{3,2,1,0:T(8,128)S(1)}) custom-call(f32[8,28,8,128]{3,2,1,0:T(8,128)} %all-to-all-done.fore_ref, f32[8,24,8,128]{3,2,1,0:T(8,128)S(1)} %all-to-all-done.1.cot_ref, s32[16,256]{1,0:T(8,128)S(1)} %fusion.1.list_ref, f32[3,320,128]{2,1,0:T(8,128)S(1)} %broadcast_in_dim.2.meta_ref), custom_call_target="tpu_custom_call" | custom-call | flops 10000000000 | bytes 3932160 | tf_op jit(solution)/shard_map/pallas_call | solution.py:33
  88.8 16.9 %all_to_all.20.got_ref = f32[8,28,8,128]{3,2,1,0:T(8,128)S(1)} all-to-all(f32[8,28,8,128]{3,2,1,0:T(8,128)S(1)} %get-tuple-element.23), channel_id=1, replica_groups=mesh['member'=8,'space'=16] {'member'}, dimensions={0} | all-to-all | bytes 1835008 | tf_op jit(solution)/shard_map/all_to_all | solution.py:564
  105.8 0.4 shard_map.81
  106.2 3.6 %collective-permute-start.2 = (f32[24,8,512]{2,1,0:T(8,128)S(1)}, f32[24,8,512]{2,1,0:T(8,128)S(1)}, u32[]{:S(2)}, u32[]{:S(2)}) collective-permute-start(f32[24,8,512]{2,1,0:T(8,128)S(1)} %get-tuple-element.24), channel_id=1, source_target_pairs={{0,1},{1,2},{2,3},{3,4},{4,5},{5,6},{6,7},{7,8},{8,9},{9,10},{10,1... | collective-permute-start | bytes 1179656 | tf_op jit(solution)/shard_map/ppermute | solution.py:560
  109.8 0.0 collective-permute-start.3
  109.8 4.7 %collective-permute-done.2.g_top_ref = f32[24,8,512]{2,1,0:T(8,128)S(1)} collective-permute-done((f32[24,8,512]{2,1,0:T(8,128)S(1)}, f32[24,8,512]{2,1,0:T(8,128)S(1)}, u32[]{:S(2)}, u32[]{:S(2)}) %collective-permute-start.2) | collective-permute-done | bytes 393248 | tf_op jit(solution)/shard_map/ppermute | solution.py:560
  114.5 0.0 copy-start.3
  114.5 0.7 copy-done.3
  115.3 6.6 %collective-permute-done.3.g_bot_ref = f32[24,8,512]{2,1,0:T(8,128)S(1)} collective-permute-done((f32[24,8,512]{2,1,0:T(8,128)S(1)}, f32[24,8,512]{2,1,0:T(8,128)S(1)}, u32[]{:S(2)}, u32[]{:S(2)}) %collective-permute-start.3) | collective-permute-done | bytes 393248 | tf_op jit(solution)/shard_map/ppermute | solution.py:560
  121.8 0.0 copy-start.5
  121.8 0.8 copy-done.5
  122.6 3.5 %all-to-all-start.3 = ((f32[8,24,8,128]{3,2,1,0:T(8,128)}), f32[8,24,8,128]{3,2,1,0:T(8,128)S(1)}, u32[]{:S(2)}, u32[]{:S(2)}) async-start(f32[8,24,8,128]{3,2,1,0:T(8,128)} %get-tuple-element.27), calls=%async_computation.3 | async-start | bytes 1572864 | tf_op jit(solution)/shard_map/all_to_all | solution.py:564
  126.2 0.0 copy-start.4
  126.2 1.0 copy-done.4
  127.2 0.0 copy-start.6
  127.2 1.0 copy-done.6
  128.1 7.6 %shard_map.83 = f32[8,6,8,512]{3,2,1,0:T(8,128)} custom-call(f32[8,6,8,512]{3,2,1,0:T(8,128)S(1)} %copy-done.1, f32[36,8,512]{2,1,0:T(8,128)S(1)} %collective-permute-done.top_ref, f32[36,8,512]{2,1,0:T(8,128)S(1)} %collective-permute-done.1.bot_ref, f32[6,16,8,512]{3,2,1,0:T(8,128)} %get-tuple-element.28.mid_ref, ...), custom_call_target="tpu_custom_call" | custom-call | flops 10000000 | bytes 4718592 | tf_op jit(solution)/shard_map/pallas_call | solution.py:33
  135.7 2.3 %all-to-all-done.3.got_ref = f32[8,24,8,128]{3,2,1,0:T(8,128)S(1)} async-done(((f32[8,24,8,128]{3,2,1,0:T(8,128)}), f32[8,24,8,128]{3,2,1,0:T(8,128)S(1)}, u32[]{:S(2)}, u32[]{:S(2)}) %all-to-all-start.3) | async-done | bytes 786464 | tf_op jit(solution)/shard_map/all_to_all | solution.py:564
  138.1 1.2 shard_map.82
  (4 shorter events, 0.1 us)
Async XLA Ops:
  0.6 1.1 copy-start
  1.9 14.5 %collective-permute-start = (f32[36,8,512]{2,1,0:T(8,128)S(1)}, f32[36,8,512]{2,1,0:T(8,128)S(1)}, u32[]{:S(2)}, u32[]{:S(2)}) collective-permute-start(f32[36,8,512]{2,1,0:T(8,128)S(1)} %get-tuple-element.17), channel_id=1, source_target_pairs={{0,1},{1,2},{2,3},{3,4},{4,5},{5,6},{6,7},{7,8},{8,9},{9,10},{10,1... | collective-permute-start | bytes 1769480 | tf_op jit(solution)/shard_map/ppermute | solution.py:560
  6.1 22.5 %copy-start.1 = (f32[8,6,8,512]{3,2,1,0:T(8,128)S(1)}, f32[8,6,8,512]{3,2,1,0:T(8,128)}, u32[]{:S(2)}) copy-start(f32[8,6,8,512]{3,2,1,0:T(8,128)} %x_ref.7) | copy-start | bytes 2359300
  6.1 14.8 %collective-permute-start.1 = (f32[36,8,512]{2,1,0:T(8,128)S(1)}, f32[36,8,512]{2,1,0:T(8,128)S(1)}, u32[]{:S(2)}, u32[]{:S(2)}) collective-permute-start(f32[36,8,512]{2,1,0:T(8,128)S(1)} %get-tuple-element.18), channel_id=1, source_target_pairs={{1,0},{2,1},{3,2},{4,3},{5,4},{6,5},{7,6},{8,7},{9,8},{10,9},{11,1... | collective-permute-start | bytes 1769480 | tf_op jit(solution)/shard_map/ppermute | solution.py:560
  6.1 1.2 copy-start.2
  7.3 19.6 %copy-start.7 = (s32[1,64,64]{2,1,0:T(8,128)S(1)}, s32[1,64,64]{2,1,0:T(8,128)}, u32[]{:S(2)}) copy-start(s32[1,64,64]{2,1,0:T(8,128)} %param.10) | copy-start | bytes 49156
  7.3 20.2 %copy-start.8 = (s32[1,2048]{1,0:T(1,128)S(1)}, s32[1,2048]{1,0:T(1,128)}, u32[]{:S(2)}) copy-start(s32[1,2048]{1,0:T(1,128)} %param.9) | copy-start | bytes 24580
  20.9 17.9 %all-to-all-start.1 = ((f32[8,24,8,128]{3,2,1,0:T(8,128)}), f32[8,24,8,128]{3,2,1,0:T(8,128)S(1)}, u32[]{:S(2)}, u32[]{:S(2)}) async-start(f32[8,24,8,128]{3,2,1,0:T(8,128)} %shard_map.78), calls=%async_computation.1 | async-start | bytes 1572864 | tf_op jit(solution)/shard_map/all_to_all | solution.py:564
  28.7 14.4 %copy-start.9 = (f32[1,2048]{1,0:T(1,128)S(1)}, f32[1,2048]{1,0:T(1,128)}, u32[]{:S(2)}) copy-start(f32[1,2048]{1,0:T(1,128)} %param.8) | copy-start | bytes 24580
  28.7 14.4 %copy-start.10 = (f32[1,2048]{1,0:T(1,128)S(1)}, f32[1,2048]{1,0:T(1,128)}, u32[]{:S(2)}) copy-start(f32[1,2048]{1,0:T(1,128)} %param.7) | copy-start | bytes 24580
  38.9 17.8 %all-to-all-start = ((f32[8,28,8,128]{3,2,1,0:T(8,128)}), f32[8,28,8,128]{3,2,1,0:T(8,128)}, u32[]{:S(2)}, u32[]{:S(2)}) async-start(f32[8,28,8,128]{3,2,1,0:T(8,128)} %get-tuple-element.21), calls=%async_computation | async-start | bytes 1835008 | tf_op jit(solution)/shard_map/all_to_all | solution.py:564
  106.2 8.3 %collective-permute-start.2 = (f32[24,8,512]{2,1,0:T(8,128)S(1)}, f32[24,8,512]{2,1,0:T(8,128)S(1)}, u32[]{:S(2)}, u32[]{:S(2)}) collective-permute-start(f32[24,8,512]{2,1,0:T(8,128)S(1)} %get-tuple-element.24), channel_id=1, source_target_pairs={{0,1},{1,2},{2,3},{3,4},{4,5},{5,6},{6,7},{7,8},{8,9},{9,10},{10,1... | collective-permute-start | bytes 1179656 | tf_op jit(solution)/shard_map/ppermute | solution.py:560
  109.8 12.0 %collective-permute-start.3 = (f32[24,8,512]{2,1,0:T(8,128)S(1)}, f32[24,8,512]{2,1,0:T(8,128)S(1)}, u32[]{:S(2)}, u32[]{:S(2)}) collective-permute-start(f32[24,8,512]{2,1,0:T(8,128)S(1)} %get-tuple-element.25), channel_id=1, source_target_pairs={{1,0},{2,1},{3,2},{4,3},{5,4},{6,5},{7,6},{8,7},{9,8},{10,9},{11,1... | collective-permute-start | bytes 1179656 | tf_op jit(solution)/shard_map/ppermute | solution.py:560
  114.5 0.7 copy-start.3
  121.8 0.8 copy-start.5
  122.6 15.5 %all-to-all-start.3 = ((f32[8,24,8,128]{3,2,1,0:T(8,128)}), f32[8,24,8,128]{3,2,1,0:T(8,128)S(1)}, u32[]{:S(2)}, u32[]{:S(2)}) async-start(f32[8,24,8,128]{3,2,1,0:T(8,128)} %get-tuple-element.27), calls=%async_computation.3 | async-start | bytes 1572864 | tf_op jit(solution)/shard_map/all_to_all | solution.py:564
  126.2 1.0 copy-start.4
  127.2 1.0 copy-start.6

commit v4 on v3

--- a/solution.py
+++ b/solution.py
@@ -117,7 +117,9 @@
             s_ref[v, HALO + ROWS + r] = bot_ref[v * HALO + r]
 
 
-def forward_kernel(x_ref, top_ref, bot_ref, sel_ref, out_ref, mid_ref, s_ref, fore_ref):
+def forward_kernel(x_ref, top_ref, bot_ref, sel_ref, cot_ref, out_ref, mid_ref, s_ref, fore_ref):
+    for d in range(8):
+        out_ref[d, 28:] = cot_ref[d]
     load_state(s_ref, x_ref, top_ref, bot_ref)
 
     def middle(i, carry):
@@ -191,7 +193,7 @@
     for v in range(VARS):
         planes = []
         for r in range(4):
-            planes.extend(unpack_planes(lambda d: got_ref[d, v * 4 + r]))
+            planes.extend(unpack_planes(lambda d: got_ref[d, 28 + v * 4 + r]))
         out_ref[:, v] = jnp.swapaxes(jnp.stack(planes), 0, 1)
 
 
@@ -315,25 +317,25 @@
 
 
 def analysis_kernel(
-    fore_ref, cot_ref, list_ref, meta_ref, up_ref, gr_ref, x_ref, c_ref, y_ref, d_ref, go_ref, block_ref
+    got_ref, list_ref, meta_ref, out_ref, x_ref, c_ref, y_ref, d_ref, go_ref, block_ref
 ):
     width = 4 * MEMBERS
     block_row = lax.broadcasted_iota(jnp.int32, (width, width), 0) // MEMBERS
     block_col = lax.broadcasted_iota(jnp.int32, (width, width), 1) // MEMBERS
     block_ref[...] = jnp.where(block_row == block_col, 1.0, 0.0).astype(bf16)
 
-    for src, dst in ((fore_ref, x_ref), (cot_ref, c_ref)):
-
-        def turn(v, carry, src=src, dst=dst):
+    for first, dst in ((0, x_ref), (28, c_ref)):
+
+        def turn(v, carry, first=first, dst=dst):
             for h in range(2):
-                tall = [src[s, v * 4 + 2 * h + k] for k in range(2) for s in range(8)]
+                tall = [got_ref[s, first + v * 4 + 2 * h + k] for k in range(2) for s in range(8)]
                 dst[v, :, 128 * h : 128 * h + 128] = jnp.concatenate(tall, axis=0).T
             return carry
 
         lax.fori_loop(0, VARS, turn, 0)
 
     for o in range(4):
-        tall = [fore_ref[s, 24 + o] for s in range(8)]
+        tall = [got_ref[s, 24 + o] for s in range(8)]
         seen = jnp.concatenate(tall + tall, axis=0).T[:WINDOW]
         mean = jnp.sum(seen, axis=1, keepdims=True) * (1.0 / 128.0)
         spread = seen - mean
@@ -530,15 +532,15 @@
 
     lax.fori_loop(0, QUADS // (2 * PAIRS), group_of_pairs, 0)
 
-    for src, dst in ((x_ref, up_ref), (c_ref, gr_ref)):
-
-        def turn_back(v, carry, src=src, dst=dst):
+    for src, first in ((x_ref, 28), (c_ref, 0)):
+
+        def turn_back(v, carry, src=src, first=first):
             for h in range(2):
                 tall = src[v, :, 128 * h : 128 * h + 128].T
                 for k in range(2):
                     for s in range(8):
                         at = 64 * k + 8 * s
-                        dst[s, v * 4 + 2 * h + k] = tall[at : at + 8]
+                        out_ref[s, first + v * 4 + 2 * h + k] = tall[at : at + 8]
             return carry
 
         lax.fori_loop(0, VARS, turn_back, 0)
@@ -548,7 +550,7 @@
         got = got - jnp.sum(got, axis=1, keepdims=True) * (1.0 / MEMBERS)
         tall = jnp.concatenate([got, jnp.zeros((128 - WINDOW, 128), f32)], axis=0).T
         for s in range(8):
-            gr_ref[s, 24 + o] = tall[8 * s : 8 * s + 8]
+            out_ref[s, 24 + o] = tall[8 * s : 8 * s + 8]
 
 
 def ring(value, up):
@@ -578,10 +580,6 @@
     first, last = call(edge_kernel, [edge, edge], [], 1000, 2 * size, state)
     bot = ring(first, True)
     top = ring(last, False)
-    (cot_sent,) = call(cot_kernel, [(8, 24, PER_DEV, 128)], [], 1000, 2 * size, cotangent)
-    top, bot, cot_sent = lax.optimization_barrier((top, bot, cot_sent))
-    cot_owned = swap(cot_sent)
-
 
     position = lax.axis_index("member") * (NOBS // 8)
     plane = obs_location[0] // COLS
@@ -592,35 +590,35 @@
     meta = jnp.broadcast_to(meta[:, :, None], (3, LOCAL_OBS, 128))
     lists = (patch_obs[0] - position + 32) % NOBS
     lists = lists.reshape(QUADS, 256) - 16 * jnp.arange(QUADS, dtype=jnp.int32)[:, None]
-
-    fore_sent, mid = call(
+    chosen, meta, lists, cotangent = lax.optimization_barrier((chosen, meta, lists, cotangent))
+    (cot_sent,) = call(cot_kernel, [(8, 24, PER_DEV, 128)], [], 1000, 2 * size, cotangent)
+
+    sent, mid = call(
         forward_kernel,
-        [(8, 28, PER_DEV, 128), (VARS, 16, PER_DEV, COLS)],
+        [(8, 52, PER_DEV, 128), (VARS, 16, PER_DEV, COLS)],
         [plane_scratch(ROWS + 2 * HALO), plane_scratch(ROWS)],
-        10**7, 5 * size, state, top, bot, chosen,
+        10**7, 6 * size, state, top, bot, chosen, cot_sent,
     )
-    fore_owned = swap(fore_sent)
+    owned = swap(sent)
 
     cells = pltpu.VMEM((VARS, 128, 256), f32)
-    update_sent, grad_sent = call(
+    (returned,) = call(
         analysis_kernel,
-        [(8, 24, PER_DEV, 128), (8, 28, PER_DEV, 128)],
+        [(8, 52, PER_DEV, 128)],
         [
             cells, cells, pltpu.VMEM((LOCAL_OBS, 128), f32), pltpu.VMEM((LOCAL_OBS, 128), f32),
             pltpu.VMEM((LOCAL_OBS, 128), f32), pltpu.VMEM((256, 256), bf16),
         ],
-        10**10, 5 * size, fore_owned, cot_owned, lists, meta,
+        10**10, 5 * size, owned, lists, meta,
     )
-    grad = swap(grad_sent)
+    got = swap(returned)
 
     g, g_first, g_last = call(
-        collect_kernel, [(STRIDE, PER_DEV, COLS), half, half], [], 10**6, 3 * size, grad, chosen
+        collect_kernel, [(STRIDE, PER_DEV, COLS), half, half], [], 10**6, 3 * size, got, chosen
     )
     g_bot = ring(g_first, True)
     g_top = ring(g_last, False)
-    g_top, g_bot, update_sent = lax.optimization_barrier((g_top, g_bot, update_sent))
-    update = swap(update_sent)
-    (analysis,) = call(place_kernel, [shape], [], 1000, 2 * size, update)
+    (analysis,) = call(place_kernel, [shape], [], 1000, 2 * size, got)
     (gradient,) = call(
         backward_kernel,
         [shape],

time: 140 us -> 135 us (0.964)
  blocking collectives: 16.9 us -> 53.5 us
  waiting for transfers between devices: 44 us -> 19.8 us
  starting transfers between devices: 21.5 us -> 7.19 us
  local copies, waits for them, and re-layouts: 7.27 us -> 4.19 us
  other arithmetic: 0.86 us -> 3.02 us
  Pallas kernels: 47.8 us -> 46.3 us
    all_to_all x1 -> x2, blocking collectives: 16.9 us -> 53.5 us  [swap(): lax.all_to_all(value, 'member', split_axis=0, concat_axis=0, tiled=True)]
    all_to_all x3 -> x0, waiting for transfers between devices: 20.3 us -> none  [swap(): lax.all_to_all(value, 'member', split_axis=0, concat_axis=0, tiled=True)]
    all_to_all x3 -> x0, starting transfers between devices: 13.7 us -> none  [swap(): lax.all_to_all(value, 'member', split_axis=0, concat_axis=0, tiled=True)]
    unnamed x23 -> x7, local copies, waits for them, and re-layouts: 6.39 us -> 1.64 us
    ppermute x4, waiting for transfers between devices: 23.7 us -> 19.8 us  [ring(): return lax.ppermute(value, 'space', pairs)]
    squeeze x2, local copies, waits for them, and re-layouts: 0.37 us -> 2.02 us  [shards(): plane = obs_location[0] // COLS]
    pallas_call x7, Pallas kernels: 47.8 us -> 46.3 us  [call(): pl.pallas_call(kernel, out_shape=[jax.ShapeDtypeStruct(s, f32) for s in o...]
  transfers between devices with their start and end apart: 7 -> 4, of which waited for: 7 -> 4; matrix products, arithmetic and copies ran while one was open for 1% -> 5% of each run, Pallas kernels for 10% -> 1%
where the time goes in v4:
time: 135 us
  blocking collectives  53.5 us (40%)
  Pallas kernels  46.3 us (34%)
  waiting for transfers between devices  19.8 us (15%)
  starting transfers between devices  7.19 us (5%)
  local copies, waits for them, and re-layouts  4.19 us (3%)
  other arithmetic  3.02 us (2%)
    all_to_all x2, blocking collectives, swap(): lax.all_to_all(value, 'member', split_axis=0, concat_axis=0, tiled=True)  53.5 us
    pallas_call x7, Pallas kernels, call(): pl.pallas_call(kernel, out_shape=[jax.ShapeDtypeStruct(s, f32) for s in o...  46.3 us
    ppermute x4, waiting for transfers between devices, ring(): return lax.ppermute(value, 'space', pairs)  19.8 us
    ppermute x4, starting transfers between devices, ring(): return lax.ppermute(value, 'space', pairs)  7.19 us
  transfers between devices with their start and end apart: 4, of which 4 were waited for; matrix products, arithmetic and copies ran while one was open for 5% of the time, Pallas kernels for 1%

profile of v4, /device:TPU:1, one launch (start us, length us, event | category | flops | bytes accessed | tf_op | source)
XLA Modules:
  0.0 134.7 jit_solution(14272279541955672809)
XLA Ops:
  0.6 0.0 copy-start
  0.6 1.1 copy-done
  1.8 0.0 copy-start.2
  1.8 0.0 copy-start.1
  1.8 0.9 shard_map.77
  2.7 4.1 %collective-permute-start = (f32[36,8,512]{2,1,0:T(8,128)}, f32[36,8,512]{2,1,0:T(8,128)S(1)}, u32[]{:S(2)}, u32[]{:S(2)}) collective-permute-start(f32[36,8,512]{2,1,0:T(8,128)} %get-tuple-element.13), channel_id=1, source_target_pairs={{0,1},{1,2},{2,3},{3,4},{4,5},{5,6},{6,7},{7,8},{8,9},{9,10},{10,1... | collective-permute-start | bytes 1769480 | tf_op jit(solution)/shard_map/ppermute | solution.py:562
  6.8 0.0 collective-permute-start.1
  6.9 0.5 broadcast.67
  7.4 1.4 %fusion.4 = (f32[1,2048]{1,0:T(1,128)S(1)}, s32[2048]{0:T(1024)S(1)}) fusion(s32[1,2048]{1,0:T(1,128)} %param.9, s32[]{:T(128)} %broadcast.67), kind=kLoop, calls=%fused_computation.20 | loop fusion | flops 55296 | bytes 24580 | tf_op jit(solution)/shard_map/convert_element_type | solution.py:587
  8.8 0.7 pad_maximum_fusion
  9.5 0.1 fusion.7
  9.6 0.8 subtract_add_fusion
  10.4 0.1 add.34
  10.5 1.0 squeeze.4
  11.4 1.1 copy.8
  12.5 0.1 concatenate.3
  12.6 0.1 constant_dynamic-slice_fusion
  12.7 0.1 fusion.1.list_ref
  12.8 0.2 broadcast_in_dim.2.meta_ref
  13.0 0.0 copy-done.2
  13.0 0.3 shard_map.78.cot_ref
  13.3 4.4 %collective-permute-done.top_ref = f32[36,8,512]{2,1,0:T(8,128)S(1)} collective-permute-done((f32[36,8,512]{2,1,0:T(8,128)}, f32[36,8,512]{2,1,0:T(8,128)S(1)}, u32[]{:S(2)}, u32[]{:S(2)}) %collective-permute-start) | collective-permute-done | bytes 589856 | tf_op jit(solution)/shard_map/ppermute | solution.py:562
  17.6 4.3 %collective-permute-done.1.bot_ref = f32[36,8,512]{2,1,0:T(8,128)S(1)} collective-permute-done((f32[36,8,512]{2,1,0:T(8,128)S(1)}, f32[36,8,512]{2,1,0:T(8,128)S(1)}, u32[]{:S(2)}, u32[]{:S(2)}) %collective-permute-start.1) | collective-permute-done | bytes 589856 | tf_op jit(solution)/shard_map/ppermute | solution.py:562
  21.9 0.0 copy-done.1
  21.9 5.7 %shard_map.79 = (f32[8,52,8,128]{3,2,1,0:T(8,128)}, f32[6,16,8,512]{3,2,1,0:T(8,128)}) custom-call(f32[8,6,8,512]{3,2,1,0:T(8,128)S(1)} %copy-done.1, f32[36,8,512]{2,1,0:T(8,128)S(1)} %collective-permute-done.top_ref, f32[36,8,512]{2,1,0:T(8,128)S(1)} %collective-permute-done.1.bot_ref, s32[4,512]{1,0:T(4,128)S(1)} %fusion.3.sel_ref, ...), custom_call_target="tpu_custom_call" | custom-call | flops 10000000 | bytes 4718592 | tf_op jit(solution)/shard_map/pallas_call | solution.py:33
  27.6 29.0 %all_to_all.10.got_ref = f32[8,52,8,128]{3,2,1,0:T(8,128)S(1)} all-to-all(f32[8,52,8,128]{3,2,1,0:T(8,128)} %get-tuple-element.17), channel_id=1, replica_groups=mesh['member'=8,'space'=16] {'member'}, dimensions={0} | all-to-all | bytes 3407872 | tf_op jit(solution)/shard_map/all_to_all | solution.py:566
  56.6 30.1 %shard_map.80 = f32[8,52,8,128]{3,2,1,0:T(8,128)S(1)} custom-call(f32[8,52,8,128]{3,2,1,0:T(8,128)S(1)} %all_to_all.10.got_ref, s32[16,256]{1,0:T(8,128)S(1)} %fusion.1.list_ref, f32[3,320,128]{2,1,0:T(8,128)S(1)} %broadcast_in_dim.2.meta_ref), custom_call_target="tpu_custom_call" | custom-call | flops 10000000000 | bytes 3932160 | tf_op jit(solution)/shard_map/pallas_call | solution.py:33
  86.7 24.5 %all_to_all.11.got_ref = f32[8,52,8,128]{3,2,1,0:T(8,128)S(1)} all-to-all(f32[8,52,8,128]{3,2,1,0:T(8,128)S(1)} %shard_map.80), channel_id=1, replica_groups=mesh['member'=8,'space'=16] {'member'}, dimensions={0} | all-to-all | bytes 3407872 | tf_op jit(solution)/shard_map/all_to_all | solution.py:566
  111.2 0.4 shard_map.82
  111.7 3.1 %collective-permute-start.2 = (f32[24,8,512]{2,1,0:T(8,128)S(1)}, f32[24,8,512]{2,1,0:T(8,128)S(1)}, u32[]{:S(2)}, u32[]{:S(2)}) collective-permute-start(f32[24,8,512]{2,1,0:T(8,128)S(1)} %get-tuple-element.22), channel_id=1, source_target_pairs={{0,1},{1,2},{2,3},{3,4},{4,5},{5,6},{6,7},{7,8},{8,9},{9,10},{10,1... | collective-permute-start | bytes 1179656 | tf_op jit(solution)/shard_map/ppermute | solution.py:562
  114.7 0.0 collective-permute-start.3
  114.7 1.2 shard_map.81
  115.9 3.6 %collective-permute-done.2.g_top_ref = f32[24,8,512]{2,1,0:T(8,128)S(1)} collective-permute-done((f32[24,8,512]{2,1,0:T(8,128)S(1)}, f32[24,8,512]{2,1,0:T(8,128)S(1)}, u32[]{:S(2)}, u32[]{:S(2)}) %collective-permute-start.2) | collective-permute-done | bytes 393248 | tf_op jit(solution)/shard_map/ppermute | solution.py:562
  119.4 7.6 %collective-permute-done.3.g_bot_ref = f32[24,8,512]{2,1,0:T(8,128)S(1)} collective-permute-done((f32[24,8,512]{2,1,0:T(8,128)S(1)}, f32[24,8,512]{2,1,0:T(8,128)S(1)}, u32[]{:S(2)}, u32[]{:S(2)}) %collective-permute-start.3) | collective-permute-done | bytes 393248 | tf_op jit(solution)/shard_map/ppermute | solution.py:562
  127.1 7.6 %shard_map.83 = f32[8,6,8,512]{3,2,1,0:T(8,128)} custom-call(f32[8,6,8,512]{3,2,1,0:T(8,128)S(1)} %copy-done.1, f32[36,8,512]{2,1,0:T(8,128)S(1)} %collective-permute-done.top_ref, f32[36,8,512]{2,1,0:T(8,128)S(1)} %collective-permute-done.1.bot_ref, f32[6,16,8,512]{3,2,1,0:T(8,128)} %get-tuple-element.20.mid_ref, ...), custom_call_target="tpu_custom_call" | custom-call | flops 10000000 | bytes 4718592 | tf_op jit(solution)/shard_map/pallas_call | solution.py:33
  (2 shorter events, 0.0 us)
Async XLA Ops:
  0.6 1.1 copy-start
  1.8 11.2 %copy-start.2 = (f32[8,6,8,512]{3,2,1,0:T(8,128)S(1)}, f32[8,6,8,512]{3,2,1,0:T(8,128)}, u32[]{:S(2)}) copy-start(f32[8,6,8,512]{3,2,1,0:T(8,128)} %x_ref.4) | copy-start | bytes 2359300
  1.8 20.1 %copy-start.1 = (f32[8,6,8,512]{3,2,1,0:T(8,128)S(1)}, f32[8,6,8,512]{3,2,1,0:T(8,128)}, u32[]{:S(2)}) copy-start(f32[8,6,8,512]{3,2,1,0:T(8,128)} %x_ref.6) | copy-start | bytes 2359300
  2.7 14.9 %collective-permute-start = (f32[36,8,512]{2,1,0:T(8,128)}, f32[36,8,512]{2,1,0:T(8,128)S(1)}, u32[]{:S(2)}, u32[]{:S(2)}) collective-permute-start(f32[36,8,512]{2,1,0:T(8,128)} %get-tuple-element.13), channel_id=1, source_target_pairs={{0,1},{1,2},{2,3},{3,4},{4,5},{5,6},{6,7},{7,8},{8,9},{9,10},{10,1... | collective-permute-start | bytes 1769480 | tf_op jit(solution)/shard_map/ppermute | solution.py:562
  6.8 15.0 %collective-permute-start.1 = (f32[36,8,512]{2,1,0:T(8,128)S(1)}, f32[36,8,512]{2,1,0:T(8,128)S(1)}, u32[]{:S(2)}, u32[]{:S(2)}) collective-permute-start(f32[36,8,512]{2,1,0:T(8,128)S(1)} %get-tuple-element.14), channel_id=1, source_target_pairs={{1,0},{2,1},{3,2},{4,3},{5,4},{6,5},{7,6},{8,7},{9,8},{10,9},{11,1... | collective-permute-start | bytes 1769480 | tf_op jit(solution)/shard_map/ppermute | solution.py:562
  111.7 7.8 %collective-permute-start.2 = (f32[24,8,512]{2,1,0:T(8,128)S(1)}, f32[24,8,512]{2,1,0:T(8,128)S(1)}, u32[]{:S(2)}, u32[]{:S(2)}) collective-permute-start(f32[24,8,512]{2,1,0:T(8,128)S(1)} %get-tuple-element.22), channel_id=1, source_target_pairs={{0,1},{1,2},{2,3},{3,4},{4,5},{5,6},{6,7},{7,8},{8,9},{9,10},{10,1... | collective-permute-start | bytes 1179656 | tf_op jit(solution)/shard_map/ppermute | solution.py:562
  114.7 12.4 %collective-permute-start.3 = (f32[24,8,512]{2,1,0:T(8,128)S(1)}, f32[24,8,512]{2,1,0:T(8,128)S(1)}, u32[]{:S(2)}, u32[]{:S(2)}) collective-permute-start(f32[24,8,512]{2,1,0:T(8,128)S(1)} %get-tuple-element.23), channel_id=1, source_target_pairs={{1,0},{2,1},{3,2},{4,3},{5,4},{6,5},{7,6},{8,7},{9,8},{10,9},{11,1... | collective-permute-start | bytes 1179656 | tf_op jit(solution)/shard_map/ppermute | solution.py:562

commit v5 on v4

--- a/solution.py
+++ b/solution.py
@@ -19,7 +19,8 @@
 LOCAL_OBS = 320
 QUADS = 16
 HALO = 6
-PAIRS = 4
+TOGETHER = 8
+CELLS = 48
 LOC_R = 8
 
 time_step = 0.2
@@ -287,16 +288,23 @@
     return lax.dot_general(a, b, (((0,), (0,)), ((), ())), preferred_element_type=f32)
 
 
-def times(left, right, product=dot):
-    lh, ll = left
-    rh, rl = right
-    if product is dot_first:
-        return product(lh, rh) + (product(lh, rl) + product(ll, rh))
-    n = lh.shape[0]
-    if n % 16:
-        return product(lh, rh) + (product(lh, rl) + product(ll, rh))
-    both = product(jnp.concatenate([lh, ll], axis=0), rh)
-    return both[:n] + (both[n:] + product(lh, rl))
+def times(left, right, more_left=None, more_right=None):
+    n = left[0].shape[0]
+    out = []
+    for p in range(2):
+        at = slice(128 * p, 128 * p + 128)
+        rows = [x[:, at] for x in left]
+        weights = right[p]
+        if more_left is not None:
+            rows = [jnp.concatenate([r, x[:, at]], axis=1) for r, x in zip(rows, more_left)]
+            weights = jnp.concatenate([weights, more_right[p]], axis=0)
+        if n % 16:
+            high, low = dot(rows[0], weights), dot(rows[1], weights[:, :128])
+        else:
+            both = dot(jnp.concatenate(rows, axis=0), weights)
+            high, low = both[:n], both[n:, :128]
+        out.append(high[:, :128] + (high[:, 128:] + low))
+    return jnp.concatenate(out, axis=1)
 
 
 def in_step(jobs):
@@ -320,19 +328,26 @@
     got_ref, list_ref, meta_ref, out_ref, x_ref, c_ref, y_ref, d_ref, go_ref, block_ref
 ):
     width = 4 * MEMBERS
-    block_row = lax.broadcasted_iota(jnp.int32, (width, width), 0) // MEMBERS
-    block_col = lax.broadcasted_iota(jnp.int32, (width, width), 1) // MEMBERS
+    block_row = lax.broadcasted_iota(jnp.int32, (width, 128), 0) // MEMBERS % 2
+    block_col = lax.broadcasted_iota(jnp.int32, (width, 128), 1) // MEMBERS
     block_ref[...] = jnp.where(block_row == block_col, 1.0, 0.0).astype(bf16)
+
+    top_half = lax.broadcasted_iota(jnp.int32, (8, 128), 0) < 4
 
     for first, dst in ((0, x_ref), (28, c_ref)):
 
         def turn(v, carry, first=first, dst=dst):
             for h in range(2):
                 tall = [got_ref[s, first + v * 4 + 2 * h + k] for k in range(2) for s in range(8)]
-                dst[v, :, 128 * h : 128 * h + 128] = jnp.concatenate(tall, axis=0).T
+                tall = jnp.concatenate(tall, axis=0).T
+                for p in range(QUADS // 2):
+                    upper, lower = tall[8 * p : 8 * p + 8], tall[64 + 8 * p : 72 + 8 * p]
+                    at = slice(128 * h, 128 * h + 128)
+                    dst[v, 2 * p, :, at] = jnp.where(top_half, upper, pltpu.roll(lower, 4, 0))
+                    dst[v, 2 * p + 1, :, at] = jnp.where(top_half, pltpu.roll(upper, 4, 0), lower)
             return carry
 
-        lax.fori_loop(0, VARS, turn, 0)
+        lax.fori_loop(0, VARS, turn, 0, unroll=3)
 
     for o in range(4):
         tall = [got_ref[s, 24 + o] for s in range(8)]
@@ -345,12 +360,21 @@
     go_ref[...] = jnp.zeros(go_ref.shape, f32)
 
     def block_of(pair):
-        mask = block_ref[...]
-        return tuple(jnp.concatenate([p] * 4, axis=0) * mask for p in pair)
+        mask = block_ref[:128]
+        out = []
+        for p in range(2):
+            parts = [x[:, 128 * p : 128 * p + 128] for x in pair]
+            parts = [jnp.concatenate([x, x], axis=0) * mask for x in parts]
+            out.append(jnp.concatenate(parts, axis=1))
+        return out
 
     def block_sum(x):
-        high, low = halves(x)
-        return dot(high, block_ref[...]) + dot(low, block_ref[...])
+        parts = halves(x)
+        out = []
+        for p in range(2):
+            wide = jnp.concatenate([x[:, 128 * p : 128 * p + 128] for x in parts], axis=1)
+            out.append(dot(wide, block_ref[...]))
+        return jnp.concatenate(out, axis=1)
 
     def row_sum(x):
         return block_sum(jnp.broadcast_to(jnp.sum(x, axis=0, keepdims=True), (8, width)))
@@ -365,14 +389,14 @@
     patch_row = (lax.broadcasted_iota(jnp.int32, (WINDOW, width), 1) // MEMBERS).astype(f32)
     col_gap = (entry // 4).astype(f32) - 9.5
     col_gap_sq = col_gap * col_gap
-    left_half = lax.broadcasted_iota(jnp.int32, (96, width), 0) % 8 < 4
     row8 = lax.broadcasted_iota(jnp.int32, (8, width), 0)
 
     def solve(quad):
         at = pl.ds(pl.multiple_of(16 * quad, 16), WINDOW)
         lists = list_ref[pl.ds(quad, 1), :]
         hits = jnp.where(jnp.broadcast_to(lists, (WINDOW, width)) == entry, 1.0, 0.0).astype(bf16)
-        count = dot(hits, block_ref[...])
+        count = [dot(hits[:, 128 * p : 128 * p + 128], block_ref[:128]) for p in range(2)]
+        count = jnp.concatenate(count, axis=1)
         yield
         obs_row = jnp.concatenate([meta_ref[1, at, :]] * 2, axis=1)
         error = jnp.concatenate([meta_ref[2, at, :]] * 2, axis=1)
@@ -383,7 +407,10 @@
         d = d_ref[at, :]
         gain = weight * jnp.concatenate([d, d], axis=1)
         scaled_pair = halves(scaled)
-        gram = times(halves(y[:, :MEMBERS]), scaled_pair, dot_first) + (MEMBERS - 1.0) * identity
+        yh, yl = halves(y[:, :MEMBERS])
+        sh, sl = scaled_pair
+        gram = dot_first(jnp.concatenate([yh, yl, yh], axis=0), jnp.concatenate([sh, sh, sl], axis=0))
+        gram = gram + (MEMBERS - 1.0) * identity
         yield
         inv = lax.rsqrt(row_sum(gram * gram))
         yield
@@ -428,26 +455,26 @@
         dt0 = halves(e)
         dm = halves(-0.5 * e)
         s0 = block_of(dm)
-        du0 = halves(times(dt0, r0) + times(t0p, s0))
-        yield
-        dt1f = times(du0, r0) + times(u0, s0)
+        du0 = halves(times(dt0, r0, t0p, s0))
+        yield
+        dt1f = times(du0, r0, u0, s0)
         yield
         dt1 = halves(dt1f)
         s1 = block_of(halves(-0.5 * dt1f))
-        both = times(stack(dm, dt1), r1) + times(stack(z1, t1), s1)
+        both = times(stack(dm, dt1), r1, stack(z1, t1), s1)
         yield
         dz2, du1 = halves(both[:MEMBERS]), halves(both[MEMBERS:])
-        dt2f = times(du1, r1) + times(u1, s1)
+        dt2f = times(du1, r1, u1, s1)
         yield
         dt2 = halves(dt2f)
         s2 = block_of(halves(-0.5 * dt2f))
-        both = times(stack(dz2, dt2), r2) + times(stack(z2, t2), s2)
+        both = times(stack(dz2, dt2), r2, stack(z2, t2), s2)
         yield
         dz3, du2 = halves(both[:MEMBERS]), halves(both[MEMBERS:])
-        dt3f = times(du2, r2) + times(u2, s2)
+        dt3f = times(du2, r2, u2, s2)
         yield
         s3 = block_of(halves(-0.5 * dt3f))
-        got = times(dz3, r3) + times(z3, s3)
+        got = times(dz3, r3, z3, s3)
         yield
         return got
 
@@ -455,53 +482,51 @@
         x = x[:, :128] + x[:, 128:]
         return x + pltpu.roll(x, 64, 1)
 
-    def open_pair(p):
-        pieces = [
-            (v, pl.ds(pl.multiple_of(64 * k + 8 * p, 8), 8)) for v in range(VARS) for k in range(2)
-        ]
-        x = jnp.concatenate([x_ref[v, at, :] for v, at in pieces], axis=0)
-        c = jnp.concatenate([c_ref[v, at, :] for v, at in pieces], axis=0)
+    def one_quad(quad):
+        x = jnp.concatenate([x_ref[v, quad] for v in range(VARS)], axis=0)
+        c = jnp.concatenate([c_ref[v, quad] for v in range(VARS)], axis=0)
         both = block_sum(jnp.concatenate([x, c], axis=0))
-        centre = both[:96] * (1.0 / MEMBERS)
-        c_sum = both[96:]
+        centre = both[:CELLS] * (1.0 / MEMBERS)
+        c_sum = both[CELLS:]
         a = x - centre
-        a_c = halves(jnp.concatenate([a, c], axis=0))
-
-        return pieces, centre, c_sum, a, c, a_c
-
-    def one_quad(p, q, opened):
-        pieces, centre, c_sum, a, c, a_c = opened
-        at, inv, z4, forcing, half_way, mean_weight, scaled, scaled_pair, gain, state = yield from solve(2 * p + q)
+        yield
+        at, inv, z4, forcing, half_way, mean_weight, scaled, scaled_pair, gain, state = yield from solve(quad)
         alpha = math.sqrt(MEMBERS - 1.0) * jnp.sqrt(inv[:1])
-        mine = left_half if q == 0 else jnp.logical_not(left_half)
-        both = times(a_c, z4)
-        yield
-        moved = alpha * both[:96]
-        update = moved + block_sum(a * mean_weight[:1])
-        yield
-        pull = alpha * both[96:] + c_sum * mean_weight[:1]
-        a_mine = jnp.where(mine, a, 0.0)
-        g_mean = jnp.broadcast_to(jnp.sum(a_mine * c_sum, axis=0, keepdims=True), (8, width))
+        both = times(halves(jnp.concatenate([a, c], axis=0)), z4)
+        yield
+        moved = alpha * both[:CELLS]
+        update = centre + moved + block_sum(a * mean_weight[:1])
+        for v in range(VARS):
+            x_ref[v, quad] = update[8 * v : 8 * v + 8]
+        yield
+        pull = alpha * both[CELLS:] + c_sum * mean_weight[:1]
+        pull = pull + (c_sum - block_sum(pull)) * (1.0 / MEMBERS)
+        for v in range(VARS):
+            c_ref[v, quad] = pull[8 * v : 8 * v + 8]
+        yield
+        g_mean = jnp.broadcast_to(jnp.sum(a * c_sum, axis=0, keepdims=True), (8, width))
         g_half = one_row(g_mean, z4) * inv
         yield
         g_forcing = one_row(g_half, z4)
         yield
         left = jnp.where(row8 == 0, g_mean * inv, jnp.where(row8 == 1, g_half, 0.0))
         right = jnp.where(row8 == 0, half_way, jnp.where(row8 == 1, forcing, 0.0))
-        scaled_a = a_mine * alpha
+        scaled_a = a * alpha
         lhs = halves(jnp.concatenate([scaled_a, c, left, right], axis=0))
         rhs = halves(jnp.concatenate([c, scaled_a, right, left], axis=0))
-        full = times(lhs, rhs, dot_first)
-        yield
-        block = lane // MEMBERS
-        e = jnp.where(
-            block < 2,
-            jnp.where(block == 0, full[:64], full[64:128]),
-            jnp.where(block == 2, full[128:192], full[192:]),
-        ) * 0.5
+        e = []
+        for p in range(2):
+            part = slice(128 * p, 128 * p + 128)
+            tall = jnp.concatenate([x[:, part] for x in lhs], axis=1)
+            wide = jnp.concatenate([x[:, part] for x in rhs], axis=1)
+            full = dot_first(tall, wide)
+            full = full[:128, :128] + (full[:128, 128:] + full[128:, :128])
+            e.append(jnp.where(lane[:, :128] < MEMBERS, full[:64], full[64:]))
+        e = jnp.concatenate(e, axis=1) * 0.5
+        yield
         g_root = yield from pull_root(e, state)
         t0 = state[0]
-        loss = jnp.sum(jnp.where(mine, c * moved, 0.0), axis=0, keepdims=True) * 0.5
+        loss = jnp.sum(c * moved, axis=0, keepdims=True) * 0.5
         loss = loss + g_mean[:1] * mean_weight[:1] + jnp.sum(g_root * t0, axis=0, keepdims=True)
         loss = block_sum(jnp.broadcast_to(loss, (8, width)))
         yield
@@ -511,39 +536,30 @@
         g_d = scaled * g_forcing[:1]
         low = lax.broadcasted_iota(jnp.int32, (WINDOW, 128), 1) < 64
         go_ref[at, :] += jnp.where(low, fold(g_y), fold(g_d))
-        return update, pull
-
-    def close_pair(opened, updates, pulls):
-        pieces, centre, c_sum = opened[:3]
-        update = centre + jnp.where(left_half, updates[0], updates[1])
-        pull = jnp.where(left_half, pulls[0], pulls[1])
-        pull = pull + (c_sum - block_sum(pull)) * (1.0 / MEMBERS)
-        for n, (v, at) in enumerate(pieces):
-            x_ref[v, at, :] = update[8 * n : 8 * n + 8]
-            c_ref[v, at, :] = pull[8 * n : 8 * n + 8]
-
-    def group_of_pairs(g, carry):
-        pairs = [PAIRS * g + k for k in range(PAIRS)]
-        opened = [open_pair(p) for p in pairs]
-        done = in_step([one_quad(p, q, o) for p, o in zip(pairs, opened) for q in range(2)])
-        for k, o in enumerate(opened):
-            close_pair(o, *zip(*done[2 * k : 2 * k + 2]))
-        return carry
-
-    lax.fori_loop(0, QUADS // (2 * PAIRS), group_of_pairs, 0)
+
+    def group(g, carry):
+        in_step([one_quad(TOGETHER * g + k) for k in range(TOGETHER)])
+        return carry
+
+    lax.fori_loop(0, QUADS // TOGETHER, group, 0)
 
     for src, first in ((x_ref, 28), (c_ref, 0)):
 
         def turn_back(v, carry, src=src, first=first):
             for h in range(2):
-                tall = src[v, :, 128 * h : 128 * h + 128].T
+                upper, lower = [], []
+                for p in range(QUADS // 2):
+                    a, b = (src[v, 2 * p + k, :, 128 * h : 128 * h + 128] for k in range(2))
+                    upper.append(jnp.where(top_half, a, pltpu.roll(b, 4, 0)))
+                    lower.append(jnp.where(top_half, pltpu.roll(a, 4, 0), b))
+                tall = jnp.concatenate(upper + lower, axis=0).T
                 for k in range(2):
                     for s in range(8):
                         at = 64 * k + 8 * s
                         out_ref[s, first + v * 4 + 2 * h + k] = tall[at : at + 8]
             return carry
 
-        lax.fori_loop(0, VARS, turn_back, 0)
+        lax.fori_loop(0, VARS, turn_back, 0, unroll=3)
 
     for o in range(4):
         got = go_ref[pl.ds(o, WINDOW, stride=4), :]
@@ -601,13 +617,13 @@
     )
     owned = swap(sent)
 
-    cells = pltpu.VMEM((VARS, 128, 256), f32)
+    cells = pltpu.VMEM((VARS, QUADS, 8, 256), f32)
     (returned,) = call(
         analysis_kernel,
         [(8, 52, PER_DEV, 128)],
         [
             cells, cells, pltpu.VMEM((LOCAL_OBS, 128), f32), pltpu.VMEM((LOCAL_OBS, 128), f32),
-            pltpu.VMEM((LOCAL_OBS, 128), f32), pltpu.VMEM((256, 256), bf16),
+            pltpu.VMEM((LOCAL_OBS, 128), f32), pltpu.VMEM((256, 128), bf16),
         ],
         10**10, 5 * size, owned, lists, meta,
     )

time: 135 us -> 125 us (0.926)
  Pallas kernels: 46.3 us -> 36 us
    pallas_call x7, Pallas kernels: 46.3 us -> 36 us  [call(): pl.pallas_call(kernel, out_shape=[jax.ShapeDtypeStruct(s, f32) for s in o...]
where the time goes in v5:
time: 125 us; the launch traced here: 124 us
  blocking collectives  53.2 us (43%)
  Pallas kernels  36 us (29%)
  waiting for transfers between devices  19.8 us (16%)
  starting transfers between devices  7.18 us (6%)
  local copies, waits for them, and re-layouts  4.19 us (3%)
  other arithmetic  3.02 us (2%)
    all_to_all x2, blocking collectives, swap(): lax.all_to_all(value, 'member', split_axis=0, concat_axis=0, tiled=True)  53.2 us
    pallas_call x7, Pallas kernels, call(): pl.pallas_call(kernel, out_shape=[jax.ShapeDtypeStruct(s, f32) for s in o...  36 us
    ppermute x4, waiting for transfers between devices, ring(): return lax.ppermute(value, 'space', pairs)  19.8 us
    ppermute x4, starting transfers between devices, ring(): return lax.ppermute(value, 'space', pairs)  7.18 us
  transfers between devices with their start and end apart: 4, of which 4 were waited for; matrix products, arithmetic and copies ran while one was open for 5% of the time, Pallas kernels for 1%

profile of v5, /device:TPU:1, one launch (start us, length us, event | category | flops | bytes accessed | tf_op | source)
XLA Modules:
  0.0 124.2 jit_solution(7257260196023943501)
XLA Ops:
  0.6 0.0 copy-start
  0.6 1.1 copy-done
  1.8 0.0 copy-start.2
  1.8 0.0 copy-start.1
  1.8 0.9 shard_map.77
  2.7 4.1 %collective-permute-start = (f32[36,8,512]{2,1,0:T(8,128)}, f32[36,8,512]{2,1,0:T(8,128)S(1)}, u32[]{:S(2)}, u32[]{:S(2)}) collective-permute-start(f32[36,8,512]{2,1,0:T(8,128)} %get-tuple-element.13), channel_id=1, source_target_pairs={{0,1},{1,2},{2,3},{3,4},{4,5},{5,6},{6,7},{7,8},{8,9},{9,10},{10,1... | collective-permute-start | bytes 1769480 | tf_op jit(solution)/shard_map/ppermute | solution.py:578
  6.8 0.0 collective-permute-start.1
  6.9 0.5 broadcast.67
  7.4 1.4 %fusion.4 = (f32[1,2048]{1,0:T(1,128)S(1)}, s32[2048]{0:T(1024)S(1)}) fusion(s32[1,2048]{1,0:T(1,128)} %param.9, s32[]{:T(128)} %broadcast.67), kind=kLoop, calls=%fused_computation.20 | loop fusion | flops 55296 | bytes 24580 | tf_op jit(solution)/shard_map/convert_element_type | solution.py:603
  8.8 0.7 pad_maximum_fusion
  9.5 0.1 fusion.7
  9.6 0.8 subtract_add_fusion
  10.4 0.1 add.34
  10.5 1.0 squeeze.4
  11.4 1.1 copy.8
  12.5 0.1 concatenate.3
  12.6 0.1 constant_dynamic-slice_fusion
  12.7 0.1 fusion.1.list_ref
  12.8 0.2 broadcast_in_dim.2.meta_ref
  13.0 0.0 copy-done.2
  13.0 0.3 shard_map.78.cot_ref
  13.3 4.4 %collective-permute-done.top_ref = f32[36,8,512]{2,1,0:T(8,128)S(1)} collective-permute-done((f32[36,8,512]{2,1,0:T(8,128)}, f32[36,8,512]{2,1,0:T(8,128)S(1)}, u32[]{:S(2)}, u32[]{:S(2)}) %collective-permute-start) | collective-permute-done | bytes 589856 | tf_op jit(solution)/shard_map/ppermute | solution.py:578
  17.6 4.3 %collective-permute-done.1.bot_ref = f32[36,8,512]{2,1,0:T(8,128)S(1)} collective-permute-done((f32[36,8,512]{2,1,0:T(8,128)S(1)}, f32[36,8,512]{2,1,0:T(8,128)S(1)}, u32[]{:S(2)}, u32[]{:S(2)}) %collective-permute-start.1) | collective-permute-done | bytes 589856 | tf_op jit(solution)/shard_map/ppermute | solution.py:578
  21.9 0.0 copy-done.1
  21.9 5.7 %shard_map.79 = (f32[8,52,8,128]{3,2,1,0:T(8,128)}, f32[6,16,8,512]{3,2,1,0:T(8,128)}) custom-call(f32[8,6,8,512]{3,2,1,0:T(8,128)S(1)} %copy-done.1, f32[36,8,512]{2,1,0:T(8,128)S(1)} %collective-permute-done.top_ref, f32[36,8,512]{2,1,0:T(8,128)S(1)} %collective-permute-done.1.bot_ref, s32[4,512]{1,0:T(4,128)S(1)} %fusion.3.sel_ref, ...), custom_call_target="tpu_custom_call" | custom-call | flops 10000000 | bytes 4718592 | tf_op jit(solution)/shard_map/pallas_call | solution.py:34
  27.6 29.0 %all_to_all.10.got_ref = f32[8,52,8,128]{3,2,1,0:T(8,128)S(1)} all-to-all(f32[8,52,8,128]{3,2,1,0:T(8,128)} %get-tuple-element.17), channel_id=1, replica_groups=mesh['member'=8,'space'=16] {'member'}, dimensions={0} | all-to-all | bytes 3407872 | tf_op jit(solution)/shard_map/all_to_all | solution.py:582
  56.6 19.9 %shard_map.80 = f32[8,52,8,128]{3,2,1,0:T(8,128)S(1)} custom-call(f32[8,52,8,128]{3,2,1,0:T(8,128)S(1)} %all_to_all.10.got_ref, s32[16,256]{1,0:T(8,128)S(1)} %fusion.1.list_ref, f32[3,320,128]{2,1,0:T(8,128)S(1)} %broadcast_in_dim.2.meta_ref), custom_call_target="tpu_custom_call" | custom-call | flops 10000000000 | bytes 3932160 | tf_op jit(solution)/shard_map/pallas_call | solution.py:34
  76.5 24.2 %all_to_all.11.got_ref = f32[8,52,8,128]{3,2,1,0:T(8,128)S(1)} all-to-all(f32[8,52,8,128]{3,2,1,0:T(8,128)S(1)} %shard_map.80), channel_id=1, replica_groups=mesh['member'=8,'space'=16] {'member'}, dimensions={0} | all-to-all | bytes 3407872 | tf_op jit(solution)/shard_map/all_to_all | solution.py:582
  100.7 0.4 shard_map.82
  101.2 3.0 %collective-permute-start.2 = (f32[24,8,512]{2,1,0:T(8,128)S(1)}, f32[24,8,512]{2,1,0:T(8,128)S(1)}, u32[]{:S(2)}, u32[]{:S(2)}) collective-permute-start(f32[24,8,512]{2,1,0:T(8,128)S(1)} %get-tuple-element.22), channel_id=1, source_target_pairs={{0,1},{1,2},{2,3},{3,4},{4,5},{5,6},{6,7},{7,8},{8,9},{9,10},{10,1... | collective-permute-start | bytes 1179656 | tf_op jit(solution)/shard_map/ppermute | solution.py:578
  104.2 0.0 collective-permute-start.3
  104.2 1.2 shard_map.81
  105.4 3.6 %collective-permute-done.2.g_top_ref = f32[24,8,512]{2,1,0:T(8,128)S(1)} collective-permute-done((f32[24,8,512]{2,1,0:T(8,128)S(1)}, f32[24,8,512]{2,1,0:T(8,128)S(1)}, u32[]{:S(2)}, u32[]{:S(2)}) %collective-permute-start.2) | collective-permute-done | bytes 393248 | tf_op jit(solution)/shard_map/ppermute | solution.py:578
  108.9 7.6 %collective-permute-done.3.g_bot_ref = f32[24,8,512]{2,1,0:T(8,128)S(1)} collective-permute-done((f32[24,8,512]{2,1,0:T(8,128)S(1)}, f32[24,8,512]{2,1,0:T(8,128)S(1)}, u32[]{:S(2)}, u32[]{:S(2)}) %collective-permute-start.3) | collective-permute-done | bytes 393248 | tf_op jit(solution)/shard_map/ppermute | solution.py:578
  116.6 7.6 %shard_map.83 = f32[8,6,8,512]{3,2,1,0:T(8,128)} custom-call(f32[8,6,8,512]{3,2,1,0:T(8,128)S(1)} %copy-done.1, f32[36,8,512]{2,1,0:T(8,128)S(1)} %collective-permute-done.top_ref, f32[36,8,512]{2,1,0:T(8,128)S(1)} %collective-permute-done.1.bot_ref, f32[6,16,8,512]{3,2,1,0:T(8,128)} %get-tuple-element.20.mid_ref, ...), custom_call_target="tpu_custom_call" | custom-call | flops 10000000 | bytes 4718592 | tf_op jit(solution)/shard_map/pallas_call | solution.py:34
  (2 shorter events, 0.0 us)
Async XLA Ops:
  0.6 1.1 copy-start
  1.8 11.2 %copy-start.2 = (f32[8,6,8,512]{3,2,1,0:T(8,128)S(1)}, f32[8,6,8,512]{3,2,1,0:T(8,128)}, u32[]{:S(2)}) copy-start(f32[8,6,8,512]{3,2,1,0:T(8,128)} %x_ref.4) | copy-start | bytes 2359300
  1.8 20.1 %copy-start.1 = (f32[8,6,8,512]{3,2,1,0:T(8,128)S(1)}, f32[8,6,8,512]{3,2,1,0:T(8,128)}, u32[]{:S(2)}) copy-start(f32[8,6,8,512]{3,2,1,0:T(8,128)} %x_ref.6) | copy-start | bytes 2359300
  2.7 14.9 %collective-permute-start = (f32[36,8,512]{2,1,0:T(8,128)}, f32[36,8,512]{2,1,0:T(8,128)S(1)}, u32[]{:S(2)}, u32[]{:S(2)}) collective-permute-start(f32[36,8,512]{2,1,0:T(8,128)} %get-tuple-element.13), channel_id=1, source_target_pairs={{0,1},{1,2},{2,3},{3,4},{4,5},{5,6},{6,7},{7,8},{8,9},{9,10},{10,1... | collective-permute-start | bytes 1769480 | tf_op jit(solution)/shard_map/ppermute | solution.py:578
  6.8 15.0 %collective-permute-start.1 = (f32[36,8,512]{2,1,0:T(8,128)S(1)}, f32[36,8,512]{2,1,0:T(8,128)S(1)}, u32[]{:S(2)}, u32[]{:S(2)}) collective-permute-start(f32[36,8,512]{2,1,0:T(8,128)S(1)} %get-tuple-element.14), channel_id=1, source_target_pairs={{1,0},{2,1},{3,2},{4,3},{5,4},{6,5},{7,6},{8,7},{9,8},{10,9},{11,1... | collective-permute-start | bytes 1769480 | tf_op jit(solution)/shard_map/ppermute | solution.py:578
  101.2 7.8 %collective-permute-start.2 = (f32[24,8,512]{2,1,0:T(8,128)S(1)}, f32[24,8,512]{2,1,0:T(8,128)S(1)}, u32[]{:S(2)}, u32[]{:S(2)}) collective-permute-start(f32[24,8,512]{2,1,0:T(8,128)S(1)} %get-tuple-element.22), channel_id=1, source_target_pairs={{0,1},{1,2},{2,3},{3,4},{4,5},{5,6},{6,7},{7,8},{8,9},{9,10},{10,1... | collective-permute-start | bytes 1179656 | tf_op jit(solution)/shard_map/ppermute | solution.py:578
  104.2 12.4 %collective-permute-start.3 = (f32[24,8,512]{2,1,0:T(8,128)S(1)}, f32[24,8,512]{2,1,0:T(8,128)S(1)}, u32[]{:S(2)}, u32[]{:S(2)}) collective-permute-start(f32[24,8,512]{2,1,0:T(8,128)S(1)} %get-tuple-element.23), channel_id=1, source_target_pairs={{1,0},{2,1},{3,2},{4,3},{5,4},{6,5},{7,6},{8,7},{9,8},{10,9},{11,1... | collective-permute-start | bytes 1179656 | tf_op jit(solution)/shard_map/ppermute | solution.py:578

commit v6 on v5

--- a/solution.py
+++ b/solution.py
@@ -18,15 +18,16 @@
 WINDOW = 80
 LOCAL_OBS = 320
 QUADS = 16
-HALO = 6
+HALO = 4
 TOGETHER = 8
 CELLS = 48
 LOC_R = 8
 
 time_step = 0.2
+HALF_STEP = 0.1
 f32 = jnp.float32
 bf16 = jnp.bfloat16
-VMEM_LIMIT = 50 * 1024 * 1024
+VMEM_LIMIT = 32 * 1024 * 1024
 
 
 def call(kernel, outs, scratch, flops, moved, *args):
@@ -129,12 +130,12 @@
             mid_ref[v, i] = s_ref[v, i + 2] + time_step * rates[v]
         return carry
 
-    lax.fori_loop(0, 16, middle, 0, unroll=4)
+    lax.fori_loop(0, 12, middle, 0, unroll=4)
 
     def finish(i, carry):
-        rates = tendency(mid_ref, i + 4)
+        rates = tendency(mid_ref, i + 2)
         for v in range(VARS):
-            fore_ref[v, i] = 0.5 * (s_ref[v, i + HALO] + mid_ref[v, i + 4]) + 0.5 * time_step * rates[v]
+            fore_ref[v, i] = 0.5 * (s_ref[v, i + HALO] + mid_ref[v, i + 2]) + 0.5 * time_step * rates[v]
         return carry
 
     lax.fori_loop(0, ROWS, finish, 0, unroll=4)
@@ -163,7 +164,48 @@
             out_ref[d, 24 + o] = lane_shift(seen, 8 - 64 * d)[:, :128]
 
 
-def collect_kernel(got_ref, sel_ref, g_ref, first_ref, last_ref):
+def place_kernel(got_ref, out_ref):
+    for v in range(VARS):
+        planes = []
+        for r in range(4):
+            planes.extend(unpack_planes(lambda d: got_ref[d, 28 + v * 4 + r]))
+        out_ref[:, v] = jnp.swapaxes(jnp.stack(planes), 0, 1)
+
+
+def pull_products(s_ref, s_at, g_ref, prod_ref, prod_at, count):
+    def body(i, carry):
+        for l in range(2):
+            u = s_ref[l, i + s_at]
+            gu, gv, gb = g_ref[l, i], g_ref[2 + l, i], g_ref[4 + l, i]
+            prod_ref[l, i + prod_at] = u * gu + gb
+            prod_ref[2 + l, i + prod_at] = u * gv
+            prod_ref[4 + l, i + prod_at] = u * gb + gu
+        return carry
+
+    lax.fori_loop(0, count, body, 0, unroll=2)
+
+
+def pull_row(s_ref, s_at, g_ref, g_at, prod_ref, prod_at):
+    out = [None] * VARS
+    for l in range(2):
+        u, v, b = (s_ref[k + l, s_at] for k in (0, 2, 4))
+        gu, gv, gb = (g_ref[k + l, g_at] for k in (0, 2, 4))
+        ru, rv, rb = (row_diff(s_ref, k + l, s_at) for k in (0, 2, 4))
+        cu, cv, cb = col_diff(u), col_diff(v), col_diff(b)
+        pu, pv, pb = (row_diff(prod_ref, k + l, prod_at) for k in (0, 2, 4))
+        out[l] = (
+            pu + col_diff(v * gu)
+            - (gu * ru + gv * rv + gb * rb) - 0.5 * gv + 0.3 * (g_ref[1 - l, g_at] - gu)
+        )
+        out[2 + l] = (
+            pv + col_diff(v * gv + gb)
+            - (gu * cu + gv * cv + gb * cb) + 0.5 * gu + 0.3 * (g_ref[3 - l, g_at] - gv)
+        )
+        out[4 + l] = pb + col_diff(v * gb + gv) + 0.3 * (g_ref[5 - l, g_at] - gb)
+    return out
+
+
+def collect_kernel(got_ref, sel_ref, mid_ref, g_ref, prod_ref, edge_ref, first_ref, last_ref):
     lane = lax.broadcasted_iota(jnp.int32, (PER_DEV, 128), 1)
     sums, chosen = [], []
     for o in range(4):
@@ -183,96 +225,67 @@
                 value = pair[k]
                 for o in range(4):
                     value = value + jnp.where(chosen[o] == v * ROWS + row, sums[o], 0.0)
-                g_ref[v * ROWS + row] = value
-                if row < 4:
-                    first_ref[v * 4 + row] = value
-                else:
-                    last_ref[v * 4 + row - 4] = value
-
-
-def place_kernel(got_ref, out_ref):
-    for v in range(VARS):
-        planes = []
-        for r in range(4):
-            planes.extend(unpack_planes(lambda d: got_ref[d, 28 + v * 4 + r]))
-        out_ref[:, v] = jnp.swapaxes(jnp.stack(planes), 0, 1)
-
-
-def pull_products(s_ref, g_ref, prod_ref, start, stop, shift):
-    def body(i, carry):
-        for l in range(2):
-            u = s_ref[l, i + shift]
-            gu, gv, gb = g_ref[l, i], g_ref[2 + l, i], g_ref[4 + l, i]
-            prod_ref[l, i] = u * gu + gb
-            prod_ref[2 + l, i] = u * gv
-            prod_ref[4 + l, i] = u * gb + gu
-        return carry
-
-    lax.fori_loop(start, stop, body, 0, unroll=2)
-
-
-def pull_row(s_ref, g_ref, prod_ref, i, shift):
-    out = [None] * VARS
-    for l in range(2):
-        u, v, b = (s_ref[k + l, i + shift] for k in (0, 2, 4))
-        gu, gv, gb = g_ref[l, i], g_ref[2 + l, i], g_ref[4 + l, i]
-        ru, rv, rb = (row_diff(s_ref, k + l, i + shift) for k in (0, 2, 4))
-        cu, cv, cb = col_diff(u), col_diff(v), col_diff(b)
-        out[l] = (
-            row_diff(prod_ref, l, i) + col_diff(v * gu)
-            - (gu * ru + gv * rv + gb * rb) - 0.5 * gv + 0.3 * (g_ref[1 - l, i] - gu)
-        )
-        out[2 + l] = (
-            row_diff(prod_ref, 2 + l, i) + col_diff(v * gv + gb)
-            - (gu * cu + gv * cv + gb * cb) + 0.5 * gu + 0.3 * (g_ref[3 - l, i] - gv)
-        )
-        out[4 + l] = (
-            row_diff(prod_ref, 4 + l, i) + col_diff(v * gb + gv) + 0.3 * (g_ref[5 - l, i] - gb)
-        )
-    return out
+                g_ref[v, row] = value
+
+    for v in range(VARS):
+        for r in (0, 1, 10, 11):
+            prod_ref[v, r] = jnp.zeros((PER_DEV, COLS), f32)
+    pull_products(mid_ref, 2, g_ref, prod_ref, 2, ROWS)
+    for n, r in enumerate((0, 1, 6, 7)):
+        got = pull_row(mid_ref, r + 2, g_ref, r, prod_ref, r + 2)
+        to_ref = first_ref if r < 2 else last_ref
+        for v in range(VARS):
+            pulled = HALF_STEP * got[v]
+            edge_ref[v, n] = pulled
+            to_ref[2 * v + n % 2] = HALF_STEP * g_ref[v, r] + time_step * pulled
+            to_ref[12 + 2 * v + n % 2] = prod_ref[v, r + 2]
+
+
+def inner_kernel(mid_ref, g_ref, prod_ref, out_ref):
+    for r in range(2, 6):
+        got = pull_row(mid_ref, r + 2, g_ref, r, prod_ref, r + 2)
+        for v in range(VARS):
+            out_ref[v, r - 2] = HALF_STEP * got[v]
 
 
 def backward_kernel(
-    x_ref, top_ref, bot_ref, mid_ref, g_ref, g_top_ref, g_bot_ref,
-    out_ref, s_ref, c_ref, prod_ref, gm_ref,
+    x_ref, top_ref, bot_ref, g_ref, prod_ref, edge_ref, inner_ref, from_top_ref, from_bot_ref,
+    out_ref, s_ref, h_ref, prod2_ref, total_ref,
 ):
     load_state(s_ref, x_ref, top_ref, bot_ref)
-    for v in range(VARS):
+    near, far = 8.0 / 12.0, 1.0 / 12.0
+    for v in range(VARS):
+        p = [prod_ref[v, 2 + r] for r in (0, 1, 6, 7)]
+        t = [from_top_ref[12 + 2 * v + k] for k in range(2)]
+        b = [from_bot_ref[12 + 2 * v + k] for k in range(2)]
+        step = time_step * HALF_STEP
+        h_ref[v, 0] = from_top_ref[2 * v] - (step * far) * p[0]
+        h_ref[v, 1] = from_top_ref[2 * v + 1] + step * (near * p[0] - far * p[1])
+        h_ref[v, 10] = from_bot_ref[2 * v] + step * (far * p[2] - near * p[3])
+        h_ref[v, 11] = from_bot_ref[2 * v + 1] + (step * far) * p[3]
+        pulled = [
+            edge_ref[v, 0] + HALF_STEP * (far * t[0] - near * t[1]),
+            edge_ref[v, 1] + (HALF_STEP * far) * t[1],
+            *(inner_ref[v, k] for k in range(4)),
+            edge_ref[v, 2] - (HALF_STEP * far) * b[0],
+            edge_ref[v, 3] + HALF_STEP * (near * b[0] - far * b[1]),
+        ]
         for r in range(ROWS):
-            c_ref[v, 4 + r] = g_ref[v * ROWS + r]
-        for r in range(4):
-            c_ref[v, r] = g_top_ref[v * 4 + r]
-            c_ref[v, 12 + r] = g_bot_ref[v * 4 + r]
-
-    pull_products(mid_ref, c_ref, prod_ref, 0, 16, 0)
-
-    def second(i, carry):
-        got = pull_row(mid_ref, c_ref, prod_ref, i, 0)
+            g = g_ref[v, r]
+            h_ref[v, 2 + r] = HALF_STEP * g + time_step * pulled[r]
+            total_ref[v, r] = g + pulled[r]
+
+    pull_products(s_ref, HALO - 2, h_ref, prod2_ref, 0, ROWS + 4)
+
+    def first(i, carry):
+        got = pull_row(s_ref, i + HALO, h_ref, i + 2, prod2_ref, i + 2)
         for v in range(VARS):
-            gm_ref[v, i] = 0.5 * time_step * got[v]
+            total_ref[v, i] = total_ref[v, i] + got[v]
         return carry
 
-    lax.fori_loop(2, 14, second, 0, unroll=4)
-
-    def combine(i, carry):
-        for v in range(VARS):
-            g, gm = c_ref[v, i], gm_ref[v, i]
-            c_ref[v, i] = 0.5 * time_step * g + time_step * gm
-            gm_ref[v, i] = g + gm
-        return carry
-
-    lax.fori_loop(2, 14, combine, 0, unroll=2)
-    pull_products(s_ref, c_ref, prod_ref, 2, 14, HALO - 4)
-
-    def first(i, carry):
-        got = pull_row(s_ref, c_ref, prod_ref, i, HALO - 4)
-        for v in range(VARS):
-            gm_ref[v, i] = gm_ref[v, i] + got[v]
-        return carry
-
-    lax.fori_loop(4, 12, first, 0, unroll=4)
-    for v in range(VARS):
-        out_ref[:, v] = jnp.swapaxes(gm_ref[v, 4:12], 0, 1)
+    lax.fori_loop(0, ROWS, first, 0, unroll=4)
+    for v in range(VARS):
+        out_ref[:, v] = jnp.swapaxes(total_ref[v], 0, 1)
 
 
 def halves(x):
@@ -611,7 +624,7 @@
 
     sent, mid = call(
         forward_kernel,
-        [(8, 52, PER_DEV, 128), (VARS, 16, PER_DEV, COLS)],
+        [(8, 52, PER_DEV, 128), (VARS, 12, PER_DEV, COLS)],
         [plane_scratch(ROWS + 2 * HALO), plane_scratch(ROWS)],
         10**7, 6 * size, state, top, bot, chosen, cot_sent,
     )
@@ -629,17 +642,21 @@
     )
     got = swap(returned)
 
-    g, g_first, g_last = call(
-        collect_kernel, [(STRIDE, PER_DEV, COLS), half, half], [], 10**6, 3 * size, got, chosen
+    planes = lambda rows: (VARS, rows, PER_DEV, COLS)
+    g, prod, outer, g_first, g_last = call(
+        collect_kernel,
+        [planes(ROWS), planes(12), planes(4), half, half],
+        [], 10**6, 4 * size, got, chosen, mid,
     )
     g_bot = ring(g_first, True)
     g_top = ring(g_last, False)
+    (inner,) = call(inner_kernel, [planes(4)], [], 10**6, 3 * size, mid, g, prod)
     (analysis,) = call(place_kernel, [shape], [], 1000, 2 * size, got)
     (gradient,) = call(
         backward_kernel,
         [shape],
-        [plane_scratch(ROWS + 2 * HALO)] + [plane_scratch(16)] * 3,
-        10**7, 6 * size, state, top, bot, mid, g, g_top, g_bot,
+        [plane_scratch(ROWS + 2 * HALO), plane_scratch(12), plane_scratch(12), plane_scratch(ROWS)],
+        10**7, 6 * size, state, top, bot, g, prod, outer, inner, g_top, g_bot,
     )
     return analysis, gradient
 

time: 125 us -> 113 us (0.904)
  Pallas kernels: 36 us -> 30.7 us
  waiting for transfers between devices: 19.8 us -> 15.8 us
  local copies, waits for them, and re-layouts: 4.19 us -> 2.53 us
    pallas_call x7 -> x8, Pallas kernels: 36 us -> 30.7 us  [call(): pl.pallas_call(kernel, out_shape=[jax.ShapeDtypeStruct(s, f32) for s in o...]
    ppermute x4, waiting for transfers between devices: 19.8 us -> 15.8 us  [ring(): return lax.ppermute(value, 'space', pairs)]
    squeeze x2, local copies, waits for them, and re-layouts: 2.02 us -> 0.37 us  [shards(): plane = obs_location[0] // COLS]
  transfers between devices with their start and end apart: 4 -> 4, of which waited for: 4 -> 4; matrix products, arithmetic and copies ran while one was open for 5% -> 4% of each run, Pallas kernels for 1% -> 2%
where the time goes in v6:
time: 113 us
  blocking collectives  52.7 us (47%)
  Pallas kernels  30.7 us (27%)
  waiting for transfers between devices  15.8 us (14%)
  starting transfers between devices  7.57 us (7%)
  other arithmetic  3.04 us (3%)
  local copies, waits for them, and re-layouts  2.53 us (2%)
    all_to_all x2, blocking collectives, swap(): lax.all_to_all(value, 'member', split_axis=0, concat_axis=0, tiled=True)  52.7 us
    pallas_call x8, Pallas kernels, call(): pl.pallas_call(kernel, out_shape=[jax.ShapeDtypeStruct(s, f32) for s in o...  30.7 us
    ppermute x4, waiting for transfers between devices, ring(): return lax.ppermute(value, 'space', pairs)  15.8 us
    ppermute x4, starting transfers between devices, ring(): return lax.ppermute(value, 'space', pairs)  7.57 us
  transfers between devices with their start and end apart: 4, of which 4 were waited for; matrix products, arithmetic and copies ran while one was open for 4% of the time, Pallas kernels for 2%

profile of v6, /device:TPU:1, one launch (start us, length us, event | category | flops | bytes accessed | tf_op | source)
XLA Modules:
  0.0 113.1 jit_solution(16483047990959648899)
XLA Ops:
  0.6 0.0 copy-start
  0.6 1.1 copy-done
  1.8 0.0 copy-start.2
  1.8 0.0 copy-start.1
  1.8 0.1 shard_map.77
  1.9 4.2 %collective-permute-start = (f32[24,8,512]{2,1,0:T(8,128)S(1)}, f32[24,8,512]{2,1,0:T(8,128)S(1)}, u32[]{:S(2)}, u32[]{:S(2)}) collective-permute-start(f32[24,8,512]{2,1,0:T(8,128)S(1)} %get-tuple-element.15), channel_id=1, source_target_pairs={{0,1},{1,2},{2,3},{3,4},{4,5},{5,6},{6,7},{7,8},{8,9},{9,10},{10,1... | collective-permute-start | bytes 1179656 | tf_op jit(solution)/shard_map/ppermute | solution.py:591
  6.1 0.0 collective-permute-start.1
  6.1 0.5 broadcast.67
  6.6 1.4 %fusion.4 = (f32[1,2048]{1,0:T(1,128)S(1)}, s32[2048]{0:T(1024)S(1)}) fusion(s32[1,2048]{1,0:T(1,128)} %param.9, s32[]{:T(128)} %broadcast.67), kind=kLoop, calls=%fused_computation.20 | loop fusion | flops 55296 | bytes 24580 | tf_op jit(solution)/shard_map/convert_element_type | solution.py:616
  8.1 0.7 pad_maximum_fusion
  8.8 0.1 fusion.7
  8.9 0.3 squeeze.4
  9.1 0.1 copy.8
  9.3 0.8 subtract_add_fusion
  10.1 0.1 add.34
  10.1 0.1 concatenate.3
  10.3 0.1 constant_dynamic-slice_fusion
  10.3 0.1 fusion.1.list_ref
  10.4 0.2 broadcast_in_dim.2.meta_ref
  10.6 0.0 copy-done.2
  10.6 0.3 shard_map.78.cot_ref
  10.9 1.3 %collective-permute-done.top_ref = f32[24,8,512]{2,1,0:T(8,128)S(1)} collective-permute-done((f32[24,8,512]{2,1,0:T(8,128)S(1)}, f32[24,8,512]{2,1,0:T(8,128)S(1)}, u32[]{:S(2)}, u32[]{:S(2)}) %collective-permute-start) | collective-permute-done | bytes 393248 | tf_op jit(solution)/shard_map/ppermute | solution.py:591
  12.2 4.6 %collective-permute-done.1.bot_ref = f32[24,8,512]{2,1,0:T(8,128)S(1)} collective-permute-done((f32[24,8,512]{2,1,0:T(8,128)S(1)}, f32[24,8,512]{2,1,0:T(8,128)S(1)}, u32[]{:S(2)}, u32[]{:S(2)}) %collective-permute-start.1) | collective-permute-done | bytes 393248 | tf_op jit(solution)/shard_map/ppermute | solution.py:591
  16.7 0.0 copy-done.1
  16.7 3.6 %shard_map.79 = (f32[8,52,8,128]{3,2,1,0:T(8,128)S(1)}, f32[6,12,8,512]{3,2,1,0:T(8,128)S(1)}) custom-call(f32[8,6,8,512]{3,2,1,0:T(8,128)S(1)} %copy-done.1, f32[24,8,512]{2,1,0:T(8,128)S(1)} %collective-permute-done.top_ref, f32[24,8,512]{2,1,0:T(8,128)S(1)} %collective-permute-done.1.bot_ref, s32[4,512]{1,0:T(4,128)S(1)} %fusion.3.sel_ref, ...), custom_call_target="tpu_custom_call" | custom-call | flops 10000000 | bytes 4718592 | tf_op jit(solution)/shard_map/pallas_call | solution.py:35
  20.3 28.4 %all_to_all.10.got_ref = f32[8,52,8,128]{3,2,1,0:T(8,128)S(1)} all-to-all(f32[8,52,8,128]{3,2,1,0:T(8,128)S(1)} %get-tuple-element.19), channel_id=1, replica_groups=mesh['member'=8,'space'=16] {'member'}, dimensions={0} | all-to-all | bytes 3407872 | tf_op jit(solution)/shard_map/all_to_all | solution.py:595
  48.7 19.9 %shard_map.80 = f32[8,52,8,128]{3,2,1,0:T(8,128)S(1)} custom-call(f32[8,52,8,128]{3,2,1,0:T(8,128)S(1)} %all_to_all.10.got_ref, s32[16,256]{1,0:T(8,128)S(1)} %fusion.1.list_ref, f32[3,320,128]{2,1,0:T(8,128)S(1)} %broadcast_in_dim.2.meta_ref), custom_call_target="tpu_custom_call" | custom-call | flops 10000000000 | bytes 3932160 | tf_op jit(solution)/shard_map/pallas_call | solution.py:35
  68.6 24.3 %all_to_all.11.got_ref = f32[8,52,8,128]{3,2,1,0:T(8,128)S(1)} all-to-all(f32[8,52,8,128]{3,2,1,0:T(8,128)S(1)} %shard_map.80), channel_id=1, replica_groups=mesh['member'=8,'space'=16] {'member'}, dimensions={0} | all-to-all | bytes 3407872 | tf_op jit(solution)/shard_map/all_to_all | solution.py:595
  93.0 1.4 %shard_map.82 = (f32[6,8,8,512]{3,2,1,0:T(8,128)S(1)}, f32[6,12,8,512]{3,2,1,0:T(8,128)S(1)}, f32[6,4,8,512]{3,2,1,0:T(8,128)S(1)}, f32[24,8,512]{2,1,0:T(8,128)S(1)}, f32[24,8,512]{2,1,0:T(8,128)S(1)}) custom-call(f32[8,52,8,128]{3,2,1,0:T(8,128)S(1)} %all_to_all.11.got_ref, s32[4,512]{1,0:T(4,128)S(1)} %fusion.3.sel_ref, ...), custom_call_target="tpu_custom_call" | custom-call | flops 1000000 | bytes 3145728 | tf_op jit(solution)/shard_map/pallas_call | solution.py:35
  94.4 3.4 %collective-permute-start.2 = (f32[24,8,512]{2,1,0:T(8,128)S(1)}, f32[24,8,512]{2,1,0:T(8,128)S(1)}, u32[]{:S(2)}, u32[]{:S(2)}) collective-permute-start(f32[24,8,512]{2,1,0:T(8,128)S(1)} %get-tuple-element.26), channel_id=1, source_target_pairs={{0,1},{1,2},{2,3},{3,4},{4,5},{5,6},{6,7},{7,8},{8,9},{9,10},{10,1... | collective-permute-start | bytes 1179656 | tf_op jit(solution)/shard_map/ppermute | solution.py:591
  97.8 0.0 collective-permute-start.3
  97.8 1.2 %shard_map.81 = f32[8,6,8,512]{3,2,1,0:T(8,128)} custom-call(f32[8,52,8,128]{3,2,1,0:T(8,128)S(1)} %all_to_all.11.got_ref), custom_call_target="tpu_custom_call" | custom-call | flops 1000 | bytes 1572864 | tf_op jit(solution)/shard_map/pallas_call | solution.py:35
  98.9 0.9 shard_map.83.inner_ref
  99.8 2.6 %collective-permute-done.2.from_top_ref = f32[24,8,512]{2,1,0:T(8,128)S(1)} collective-permute-done((f32[24,8,512]{2,1,0:T(8,128)S(1)}, f32[24,8,512]{2,1,0:T(8,128)S(1)}, u32[]{:S(2)}, u32[]{:S(2)}) %collective-permute-start.2) | collective-permute-done | bytes 393248 | tf_op jit(solution)/shard_map/ppermute | solution.py:591
  102.5 7.3 %collective-permute-done.3.from_bot_ref = f32[24,8,512]{2,1,0:T(8,128)S(1)} collective-permute-done((f32[24,8,512]{2,1,0:T(8,128)S(1)}, f32[24,8,512]{2,1,0:T(8,128)S(1)}, u32[]{:S(2)}, u32[]{:S(2)}) %collective-permute-start.3) | collective-permute-done | bytes 393248 | tf_op jit(solution)/shard_map/ppermute | solution.py:591
  109.8 3.3 %shard_map.84 = f32[8,6,8,512]{3,2,1,0:T(8,128)} custom-call(f32[8,6,8,512]{3,2,1,0:T(8,128)S(1)} %copy-done.1, f32[24,8,512]{2,1,0:T(8,128)S(1)} %collective-permute-done.top_ref, f32[24,8,512]{2,1,0:T(8,128)S(1)} %collective-permute-done.1.bot_ref, f32[6,8,8,512]{3,2,1,0:T(8,128)S(1)} %get-tuple-element.23.g_ref, ...), custom_call_target="tpu_custom_call" | custom-call | flops 10000000 | bytes 4718592 | tf_op jit(solution)/shard_map/pallas_call | solution.py:35
  (2 shorter events, 0.0 us)
Async XLA Ops:
  0.6 1.1 %copy-start = (f32[8,6,8,512]{3,2,1,0:T(8,128)S(1)}, f32[8,6,8,512]{3,2,1,0:T(8,128)}, u32[]{:S(2)}) copy-start(f32[8,6,8,512]{3,2,1,0:T(8,128)} %x_ref.6) | copy-start | bytes 2359300
  1.8 8.8 %copy-start.2 = (f32[8,6,8,512]{3,2,1,0:T(8,128)S(1)}, f32[8,6,8,512]{3,2,1,0:T(8,128)}, u32[]{:S(2)}) copy-start(f32[8,6,8,512]{3,2,1,0:T(8,128)} %x_ref.4) | copy-start | bytes 2359300
  1.8 15.0 %copy-start.1 = (f32[8,6,8,512]{3,2,1,0:T(8,128)S(1)}, f32[8,6,8,512]{3,2,1,0:T(8,128)}, u32[]{:S(2)}) copy-start(f32[8,6,8,512]{3,2,1,0:T(8,128)} %x_ref.6) | copy-start | bytes 2359300
  1.9 10.2 %collective-permute-start = (f32[24,8,512]{2,1,0:T(8,128)S(1)}, f32[24,8,512]{2,1,0:T(8,128)S(1)}, u32[]{:S(2)}, u32[]{:S(2)}) collective-permute-start(f32[24,8,512]{2,1,0:T(8,128)S(1)} %get-tuple-element.15), channel_id=1, source_target_pairs={{0,1},{1,2},{2,3},{3,4},{4,5},{5,6},{6,7},{7,8},{8,9},{9,10},{10,1... | collective-permute-start | bytes 1179656 | tf_op jit(solution)/shard_map/ppermute | solution.py:591
  6.1 10.6 %collective-permute-start.1 = (f32[24,8,512]{2,1,0:T(8,128)S(1)}, f32[24,8,512]{2,1,0:T(8,128)S(1)}, u32[]{:S(2)}, u32[]{:S(2)}) collective-permute-start(f32[24,8,512]{2,1,0:T(8,128)S(1)} %get-tuple-element.16), channel_id=1, source_target_pairs={{1,0},{2,1},{3,2},{4,3},{5,4},{6,5},{7,6},{8,7},{9,8},{10,9},{11,1... | collective-permute-start | bytes 1179656 | tf_op jit(solution)/shard_map/ppermute | solution.py:591
  94.4 8.1 %collective-permute-start.2 = (f32[24,8,512]{2,1,0:T(8,128)S(1)}, f32[24,8,512]{2,1,0:T(8,128)S(1)}, u32[]{:S(2)}, u32[]{:S(2)}) collective-permute-start(f32[24,8,512]{2,1,0:T(8,128)S(1)} %get-tuple-element.26), channel_id=1, source_target_pairs={{0,1},{1,2},{2,3},{3,4},{4,5},{5,6},{6,7},{7,8},{8,9},{9,10},{10,1... | collective-permute-start | bytes 1179656 | tf_op jit(solution)/shard_map/ppermute | solution.py:591
  97.8 12.0 %collective-permute-start.3 = (f32[24,8,512]{2,1,0:T(8,128)S(1)}, f32[24,8,512]{2,1,0:T(8,128)S(1)}, u32[]{:S(2)}, u32[]{:S(2)}) collective-permute-start(f32[24,8,512]{2,1,0:T(8,128)S(1)} %get-tuple-element.27), channel_id=1, source_target_pairs={{1,0},{2,1},{3,2},{4,3},{5,4},{6,5},{7,6},{8,7},{9,8},{10,9},{11,1... | collective-permute-start | bytes 1179656 | tf_op jit(solution)/shard_map/ppermute | solution.py:591

commit v7 on v6

--- a/solution.py
+++ b/solution.py
@@ -311,11 +311,14 @@
         if more_left is not None:
             rows = [jnp.concatenate([r, x[:, at]], axis=1) for r, x in zip(rows, more_left)]
             weights = jnp.concatenate([weights, more_right[p]], axis=0)
-        if n % 16:
-            high, low = dot(rows[0], weights), dot(rows[1], weights[:, :128])
-        else:
-            both = dot(jnp.concatenate(rows, axis=0), weights)
-            high, low = both[:n], both[n:, :128]
+        if more_left is None:
+            zero = jnp.zeros((128, 128), bf16)
+            deep = jnp.concatenate([weights[:, :128], zero], axis=1)
+            both = dot(jnp.concatenate(rows, axis=1), jnp.concatenate([weights, deep], axis=0))
+            out.append(both[:, :128] + both[:, 128:])
+            continue
+        both = dot(jnp.concatenate(rows, axis=0), weights)
+        high, low = both[:n], both[n:, :128]
         out.append(high[:, :128] + (high[:, 128:] + low))
     return jnp.concatenate(out, axis=1)
 
@@ -360,7 +363,7 @@
                     dst[v, 2 * p + 1, :, at] = jnp.where(top_half, pltpu.roll(upper, 4, 0), lower)
             return carry
 
-        lax.fori_loop(0, VARS, turn, 0, unroll=3)
+        lax.fori_loop(0, VARS, turn, 0, unroll=6)
 
     for o in range(4):
         tall = [got_ref[s, 24 + o] for s in range(8)]
@@ -392,9 +395,6 @@
     def row_sum(x):
         return block_sum(jnp.broadcast_to(jnp.sum(x, axis=0, keepdims=True), (8, width)))
 
-    def one_row(x, right):
-        return times(halves(x), right)
-
     lane = lax.broadcasted_iota(jnp.int32, (MEMBERS, width), 1)
     sub = lax.broadcasted_iota(jnp.int32, (MEMBERS, width), 0)
     identity = jnp.where(lane % MEMBERS == sub, 1.0, 0.0)
@@ -403,14 +403,14 @@
     col_gap = (entry // 4).astype(f32) - 9.5
     col_gap_sq = col_gap * col_gap
     row8 = lax.broadcasted_iota(jnp.int32, (8, width), 0)
-
-    def solve(quad):
+    row16 = lax.broadcasted_iota(jnp.int32, (16, width), 0)
+
+    def hits_of(quad):
+        lists = list_ref[pl.ds(quad, 1), :]
+        return jnp.where(jnp.broadcast_to(lists, (WINDOW, width)) == entry, 1.0, 0.0).astype(bf16)
+
+    def solve(quad, count):
         at = pl.ds(pl.multiple_of(16 * quad, 16), WINDOW)
-        lists = list_ref[pl.ds(quad, 1), :]
-        hits = jnp.where(jnp.broadcast_to(lists, (WINDOW, width)) == entry, 1.0, 0.0).astype(bf16)
-        count = [dot(hits[:, 128 * p : 128 * p + 128], block_ref[:128]) for p in range(2)]
-        count = jnp.concatenate(count, axis=1)
-        yield
         obs_row = jnp.concatenate([meta_ref[1, at, :]] * 2, axis=1)
         error = jnp.concatenate([meta_ref[2, at, :]] * 2, axis=1)
         row_gap = obs_row - 2.0 * patch_row - 0.5
@@ -429,7 +429,6 @@
         yield
         t0 = gram * inv[:1]
         forcing = jnp.sum(scaled * jnp.concatenate([d, d], axis=1), axis=0, keepdims=True)
-        forcing = jnp.broadcast_to(forcing, (8, width))
 
         m0 = 1.5 * identity - 0.5 * t0
         z1 = halves(m0)
@@ -456,12 +455,8 @@
         r3 = block_of(halves(1.5 * identity - 0.5 * t3f))
         z4 = block_of(halves(times(z3, r3)))
         yield
-        half_way = one_row(forcing, z4)
-        yield
-        mean_weight = one_row(half_way, z4) * inv
-        yield
         state = (t0, t0p, u0, t1, u1, t2, u2, z1, z2, z3, r0, r1, r2, r3)
-        return at, inv, z4, forcing, half_way, mean_weight, scaled, scaled_pair, gain, state
+        return at, inv, z4, forcing, scaled, scaled_pair, gain, state
 
     def pull_root(e, state):
         t0, t0p, u0, t1, u1, t2, u2, z1, z2, z3, r0, r1, r2, r3 = state
@@ -495,33 +490,26 @@
         x = x[:, :128] + x[:, 128:]
         return x + pltpu.roll(x, 64, 1)
 
-    def one_quad(quad):
-        x = jnp.concatenate([x_ref[v, quad] for v in range(VARS)], axis=0)
-        c = jnp.concatenate([c_ref[v, quad] for v in range(VARS)], axis=0)
-        both = block_sum(jnp.concatenate([x, c], axis=0))
-        centre = both[:CELLS] * (1.0 / MEMBERS)
-        c_sum = both[CELLS:]
+    def one_quad(quad, count, x, c, centre, c_sum):
         a = x - centre
-        yield
-        at, inv, z4, forcing, half_way, mean_weight, scaled, scaled_pair, gain, state = yield from solve(quad)
-        alpha = math.sqrt(MEMBERS - 1.0) * jnp.sqrt(inv[:1])
-        both = times(halves(jnp.concatenate([a, c], axis=0)), z4)
-        yield
+        g_mean = jnp.sum(a * c_sum, axis=0, keepdims=True)
+        at, inv, z4, forcing, scaled, scaled_pair, gain, state = yield from solve(quad, count)
+        inv = inv[:1]
+        alpha = math.sqrt(MEMBERS - 1.0) * jnp.sqrt(inv)
+        few = jnp.where(row16 == 0, forcing, jnp.where(row16 == 1, g_mean, 0.0))
+        both = times(halves(jnp.concatenate([a, c, few], axis=0)), z4)
+        yield
+        few = both[2 * CELLS :]
+        half_way, g_half = few[:1], few[1:2] * inv
+        few = times(halves(few * jnp.where(row16 == 1, inv, 1.0)), z4)
+        yield
+        mean_weight, g_forcing = few[:1] * inv, few[1:2]
         moved = alpha * both[:CELLS]
-        update = centre + moved + block_sum(a * mean_weight[:1])
+        update = centre + moved + block_sum(a * mean_weight)
         for v in range(VARS):
             x_ref[v, quad] = update[8 * v : 8 * v + 8]
         yield
-        pull = alpha * both[CELLS:] + c_sum * mean_weight[:1]
-        pull = pull + (c_sum - block_sum(pull)) * (1.0 / MEMBERS)
-        for v in range(VARS):
-            c_ref[v, quad] = pull[8 * v : 8 * v + 8]
-        yield
-        g_mean = jnp.broadcast_to(jnp.sum(a * c_sum, axis=0, keepdims=True), (8, width))
-        g_half = one_row(g_mean, z4) * inv
-        yield
-        g_forcing = one_row(g_half, z4)
-        yield
+        pull = alpha * both[CELLS : 2 * CELLS] + c_sum * mean_weight
         left = jnp.where(row8 == 0, g_mean * inv, jnp.where(row8 == 1, g_half, 0.0))
         right = jnp.where(row8 == 0, half_way, jnp.where(row8 == 1, forcing, 0.0))
         scaled_a = a * alpha
@@ -540,18 +528,37 @@
         g_root = yield from pull_root(e, state)
         t0 = state[0]
         loss = jnp.sum(c * moved, axis=0, keepdims=True) * 0.5
-        loss = loss + g_mean[:1] * mean_weight[:1] + jnp.sum(g_root * t0, axis=0, keepdims=True)
+        loss = loss + g_mean * mean_weight + jnp.sum(g_root * t0, axis=0, keepdims=True)
         loss = block_sum(jnp.broadcast_to(loss, (8, width)))
         yield
-        g_gram = (g_root - loss[:1] * t0) * inv[:1]
-        g_y = 2.0 * times(scaled_pair, block_of(halves(g_gram))) + gain * g_forcing[:1]
-        yield
-        g_d = scaled * g_forcing[:1]
+        g_gram = (g_root - loss[:1] * t0) * inv
+        g_y = 2.0 * times(scaled_pair, block_of(halves(g_gram))) + gain * g_forcing
+        yield
+        g_d = scaled * g_forcing
         low = lax.broadcasted_iota(jnp.int32, (WINDOW, 128), 1) < 64
         go_ref[at, :] += jnp.where(low, fold(g_y), fold(g_d))
+        return pull
 
     def group(g, carry):
-        in_step([one_quad(TOGETHER * g + k) for k in range(TOGETHER)])
+        quads = [TOGETHER * g + k for k in range(TOGETHER)]
+        hits = jnp.concatenate([hits_of(q) for q in quads], axis=0)
+        counts = [dot(hits[:, 128 * p : 128 * p + 128], block_ref[:128]) for p in range(2)]
+        counts = jnp.concatenate(counts, axis=1)
+        cells = [ref[v, q] for q in quads for ref in (x_ref, c_ref) for v in range(VARS)]
+        cells = jnp.concatenate(cells, axis=0)
+        sums = block_sum(cells)
+        jobs, c_sums = [], []
+        for k, q in enumerate(quads):
+            low, mid, high = (CELLS * n for n in (2 * k, 2 * k + 1, 2 * k + 2))
+            count = counts[WINDOW * k : WINDOW * k + WINDOW]
+            centre, c_sum = sums[low:mid] * (1.0 / MEMBERS), sums[mid:high]
+            jobs.append(one_quad(q, count, cells[low:mid], cells[mid:high], centre, c_sum))
+            c_sums.append(c_sum)
+        pulls = jnp.concatenate(in_step(jobs), axis=0)
+        pulls = pulls + (jnp.concatenate(c_sums, axis=0) - block_sum(pulls)) * (1.0 / MEMBERS)
+        for k, q in enumerate(quads):
+            for v in range(VARS):
+                c_ref[v, q] = pulls[CELLS * k + 8 * v : CELLS * k + 8 * v + 8]
         return carry
 
     lax.fori_loop(0, QUADS // TOGETHER, group, 0)
@@ -572,7 +579,7 @@
                         out_ref[s, first + v * 4 + 2 * h + k] = tall[at : at + 8]
             return carry
 
-        lax.fori_loop(0, VARS, turn_back, 0, unroll=3)
+        lax.fori_loop(0, VARS, turn_back, 0, unroll=6)
 
     for o in range(4):
         got = go_ref[pl.ds(o, WINDOW, stride=4), :]

time: 113 us -> 111 us (0.982)
  Pallas kernels: 30.7 us -> 27.9 us
    pallas_call x8, Pallas kernels: 30.7 us -> 27.9 us  [call(): pl.pallas_call(kernel, out_shape=[jax.ShapeDtypeStruct(s, f32) for s in o...]
where the time goes in v7:
time: 111 us; the launch traced here: 110 us
  blocking collectives  52.8 us (48%)
  Pallas kernels  27.9 us (25%)
  waiting for transfers between devices  15.8 us (14%)
  starting transfers between devices  7.64 us (7%)
  other arithmetic  3.04 us (3%)
  local copies, waits for them, and re-layouts  2.53 us (2%)
    all_to_all x2, blocking collectives, swap(): lax.all_to_all(value, 'member', split_axis=0, concat_axis=0, tiled=True)  52.8 us
    pallas_call x8, Pallas kernels, call(): pl.pallas_call(kernel, out_shape=[jax.ShapeDtypeStruct(s, f32) for s in o...  27.9 us
    ppermute x4, waiting for transfers between devices, ring(): return lax.ppermute(value, 'space', pairs)  15.8 us
    ppermute x4, starting transfers between devices, ring(): return lax.ppermute(value, 'space', pairs)  7.64 us
  transfers between devices with their start and end apart: 4, of which 4 were waited for; matrix products, arithmetic and copies ran while one was open for 4% of the time, Pallas kernels for 2%

profile of v7, /device:TPU:1, one launch (start us, length us, event | category | flops | bytes accessed | tf_op | source)
XLA Modules:
  0.0 110.5 jit_solution(15025427005540287642)
XLA Ops:
  0.6 0.0 copy-start
  0.6 1.1 %copy-done = f32[8,6,8,512]{3,2,1,0:T(8,128)S(1)} copy-done((f32[8,6,8,512]{3,2,1,0:T(8,128)S(1)}, f32[8,6,8,512]{3,2,1,0:T(8,128)}, u32[]{:S(2)}) %copy-start) | copy-done | bytes 786456
  1.8 0.0 copy-start.2
  1.8 0.0 copy-start.1
  1.8 0.1 shard_map.77
  1.9 4.2 %collective-permute-start = (f32[24,8,512]{2,1,0:T(8,128)S(1)}, f32[24,8,512]{2,1,0:T(8,128)S(1)}, u32[]{:S(2)}, u32[]{:S(2)}) collective-permute-start(f32[24,8,512]{2,1,0:T(8,128)S(1)} %get-tuple-element.15), channel_id=1, source_target_pairs={{0,1},{1,2},{2,3},{3,4},{4,5},{5,6},{6,7},{7,8},{8,9},{9,10},{10,1... | collective-permute-start | bytes 1179656 | tf_op jit(solution)/shard_map/ppermute | solution.py:598
  6.1 0.0 collective-permute-start.1
  6.1 0.5 broadcast.67
  6.6 1.4 %fusion.4 = (f32[1,2048]{1,0:T(1,128)S(1)}, s32[2048]{0:T(1024)S(1)}) fusion(s32[1,2048]{1,0:T(1,128)} %param.9, s32[]{:T(128)} %broadcast.67), kind=kLoop, calls=%fused_computation.20 | loop fusion | flops 55296 | bytes 24580 | tf_op jit(solution)/shard_map/convert_element_type | solution.py:623
  8.1 0.7 pad_maximum_fusion
  8.8 0.1 fusion.7
  8.9 0.3 squeeze.4
  9.1 0.1 copy.8
  9.3 0.8 subtract_add_fusion
  10.1 0.1 add.34
  10.1 0.1 concatenate.3
  10.3 0.1 constant_dynamic-slice_fusion
  10.3 0.1 fusion.1.list_ref
  10.4 0.2 broadcast_in_dim.2.meta_ref
  10.6 0.0 copy-done.2
  10.6 0.3 shard_map.78.cot_ref
  10.9 1.3 %collective-permute-done.top_ref = f32[24,8,512]{2,1,0:T(8,128)S(1)} collective-permute-done((f32[24,8,512]{2,1,0:T(8,128)S(1)}, f32[24,8,512]{2,1,0:T(8,128)S(1)}, u32[]{:S(2)}, u32[]{:S(2)}) %collective-permute-start) | collective-permute-done | bytes 393248 | tf_op jit(solution)/shard_map/ppermute | solution.py:598
  12.2 4.6 %collective-permute-done.1.bot_ref = f32[24,8,512]{2,1,0:T(8,128)S(1)} collective-permute-done((f32[24,8,512]{2,1,0:T(8,128)S(1)}, f32[24,8,512]{2,1,0:T(8,128)S(1)}, u32[]{:S(2)}, u32[]{:S(2)}) %collective-permute-start.1) | collective-permute-done | bytes 393248 | tf_op jit(solution)/shard_map/ppermute | solution.py:598
  16.7 0.0 copy-done.1
  16.7 3.6 %shard_map.79 = (f32[8,52,8,128]{3,2,1,0:T(8,128)S(1)}, f32[6,12,8,512]{3,2,1,0:T(8,128)S(1)}) custom-call(f32[8,6,8,512]{3,2,1,0:T(8,128)S(1)} %copy-done.1, f32[24,8,512]{2,1,0:T(8,128)S(1)} %collective-permute-done.top_ref, f32[24,8,512]{2,1,0:T(8,128)S(1)} %collective-permute-done.1.bot_ref, s32[4,512]{1,0:T(4,128)S(1)} %fusion.3.sel_ref, ...), custom_call_target="tpu_custom_call" | custom-call | flops 10000000 | bytes 4718592 | tf_op jit(solution)/shard_map/pallas_call | solution.py:35
  20.3 28.4 %all_to_all.10.got_ref = f32[8,52,8,128]{3,2,1,0:T(8,128)S(1)} all-to-all(f32[8,52,8,128]{3,2,1,0:T(8,128)S(1)} %get-tuple-element.19), channel_id=1, replica_groups=mesh['member'=8,'space'=16] {'member'}, dimensions={0} | all-to-all | bytes 3407872 | tf_op jit(solution)/shard_map/all_to_all | solution.py:602
  48.7 17.1 %shard_map.80 = f32[8,52,8,128]{3,2,1,0:T(8,128)S(1)} custom-call(f32[8,52,8,128]{3,2,1,0:T(8,128)S(1)} %all_to_all.10.got_ref, s32[16,256]{1,0:T(8,128)S(1)} %fusion.1.list_ref, f32[3,320,128]{2,1,0:T(8,128)S(1)} %broadcast_in_dim.2.meta_ref), custom_call_target="tpu_custom_call" | custom-call | flops 10000000000 | bytes 3932160 | tf_op jit(solution)/shard_map/pallas_call | solution.py:35
  65.8 24.4 %all_to_all.11.got_ref = f32[8,52,8,128]{3,2,1,0:T(8,128)S(1)} all-to-all(f32[8,52,8,128]{3,2,1,0:T(8,128)S(1)} %shard_map.80), channel_id=1, replica_groups=mesh['member'=8,'space'=16] {'member'}, dimensions={0} | all-to-all | bytes 3407872 | tf_op jit(solution)/shard_map/all_to_all | solution.py:602
  90.2 1.4 %shard_map.82 = (f32[6,8,8,512]{3,2,1,0:T(8,128)S(1)}, f32[6,12,8,512]{3,2,1,0:T(8,128)S(1)}, f32[6,4,8,512]{3,2,1,0:T(8,128)S(1)}, f32[24,8,512]{2,1,0:T(8,128)S(1)}, f32[24,8,512]{2,1,0:T(8,128)S(1)}) custom-call(f32[8,52,8,128]{3,2,1,0:T(8,128)S(1)} %all_to_all.11.got_ref, s32[4,512]{1,0:T(4,128)S(1)} %fusion.3.sel_ref, ...), custom_call_target="tpu_custom_call" | custom-call | flops 1000000 | bytes 3145728 | tf_op jit(solution)/shard_map/pallas_call | solution.py:35
  91.7 3.4 %collective-permute-start.2 = (f32[24,8,512]{2,1,0:T(8,128)S(1)}, f32[24,8,512]{2,1,0:T(8,128)S(1)}, u32[]{:S(2)}, u32[]{:S(2)}) collective-permute-start(f32[24,8,512]{2,1,0:T(8,128)S(1)} %get-tuple-element.26), channel_id=1, source_target_pairs={{0,1},{1,2},{2,3},{3,4},{4,5},{5,6},{6,7},{7,8},{8,9},{9,10},{10,1... | collective-permute-start | bytes 1179656 | tf_op jit(solution)/shard_map/ppermute | solution.py:598
  95.1 0.0 collective-permute-start.3
  95.1 1.2 %shard_map.81 = f32[8,6,8,512]{3,2,1,0:T(8,128)} custom-call(f32[8,52,8,128]{3,2,1,0:T(8,128)S(1)} %all_to_all.11.got_ref), custom_call_target="tpu_custom_call" | custom-call | flops 1000 | bytes 1572864 | tf_op jit(solution)/shard_map/pallas_call | solution.py:35
  96.3 0.9 shard_map.83.inner_ref
  97.2 2.6 %collective-permute-done.2.from_top_ref = f32[24,8,512]{2,1,0:T(8,128)S(1)} collective-permute-done((f32[24,8,512]{2,1,0:T(8,128)S(1)}, f32[24,8,512]{2,1,0:T(8,128)S(1)}, u32[]{:S(2)}, u32[]{:S(2)}) %collective-permute-start.2) | collective-permute-done | bytes 393248 | tf_op jit(solution)/shard_map/ppermute | solution.py:598
  99.8 7.3 %collective-permute-done.3.from_bot_ref = f32[24,8,512]{2,1,0:T(8,128)S(1)} collective-permute-done((f32[24,8,512]{2,1,0:T(8,128)S(1)}, f32[24,8,512]{2,1,0:T(8,128)S(1)}, u32[]{:S(2)}, u32[]{:S(2)}) %collective-permute-start.3) | collective-permute-done | bytes 393248 | tf_op jit(solution)/shard_map/ppermute | solution.py:598
  107.2 3.3 %shard_map.84 = f32[8,6,8,512]{3,2,1,0:T(8,128)} custom-call(f32[8,6,8,512]{3,2,1,0:T(8,128)S(1)} %copy-done.1, f32[24,8,512]{2,1,0:T(8,128)S(1)} %collective-permute-done.top_ref, f32[24,8,512]{2,1,0:T(8,128)S(1)} %collective-permute-done.1.bot_ref, f32[6,8,8,512]{3,2,1,0:T(8,128)S(1)} %get-tuple-element.23.g_ref, ...), custom_call_target="tpu_custom_call" | custom-call | flops 10000000 | bytes 4718592 | tf_op jit(solution)/shard_map/pallas_call | solution.py:35
  (2 shorter events, 0.0 us)
Async XLA Ops:
  0.6 1.1 %copy-start = (f32[8,6,8,512]{3,2,1,0:T(8,128)S(1)}, f32[8,6,8,512]{3,2,1,0:T(8,128)}, u32[]{:S(2)}) copy-start(f32[8,6,8,512]{3,2,1,0:T(8,128)} %x_ref.6) | copy-start | bytes 2359300
  1.8 8.8 %copy-start.2 = (f32[8,6,8,512]{3,2,1,0:T(8,128)S(1)}, f32[8,6,8,512]{3,2,1,0:T(8,128)}, u32[]{:S(2)}) copy-start(f32[8,6,8,512]{3,2,1,0:T(8,128)} %x_ref.4) | copy-start | bytes 2359300
  1.8 15.0 %copy-start.1 = (f32[8,6,8,512]{3,2,1,0:T(8,128)S(1)}, f32[8,6,8,512]{3,2,1,0:T(8,128)}, u32[]{:S(2)}) copy-start(f32[8,6,8,512]{3,2,1,0:T(8,128)} %x_ref.6) | copy-start | bytes 2359300
  1.9 10.2 %collective-permute-start = (f32[24,8,512]{2,1,0:T(8,128)S(1)}, f32[24,8,512]{2,1,0:T(8,128)S(1)}, u32[]{:S(2)}, u32[]{:S(2)}) collective-permute-start(f32[24,8,512]{2,1,0:T(8,128)S(1)} %get-tuple-element.15), channel_id=1, source_target_pairs={{0,1},{1,2},{2,3},{3,4},{4,5},{5,6},{6,7},{7,8},{8,9},{9,10},{10,1... | collective-permute-start | bytes 1179656 | tf_op jit(solution)/shard_map/ppermute | solution.py:598
  6.1 10.6 %collective-permute-start.1 = (f32[24,8,512]{2,1,0:T(8,128)S(1)}, f32[24,8,512]{2,1,0:T(8,128)S(1)}, u32[]{:S(2)}, u32[]{:S(2)}) collective-permute-start(f32[24,8,512]{2,1,0:T(8,128)S(1)} %get-tuple-element.16), channel_id=1, source_target_pairs={{1,0},{2,1},{3,2},{4,3},{5,4},{6,5},{7,6},{8,7},{9,8},{10,9},{11,1... | collective-permute-start | bytes 1179656 | tf_op jit(solution)/shard_map/ppermute | solution.py:598
  91.7 8.2 %collective-permute-start.2 = (f32[24,8,512]{2,1,0:T(8,128)S(1)}, f32[24,8,512]{2,1,0:T(8,128)S(1)}, u32[]{:S(2)}, u32[]{:S(2)}) collective-permute-start(f32[24,8,512]{2,1,0:T(8,128)S(1)} %get-tuple-element.26), channel_id=1, source_target_pairs={{0,1},{1,2},{2,3},{3,4},{4,5},{5,6},{6,7},{7,8},{8,9},{9,10},{10,1... | collective-permute-start | bytes 1179656 | tf_op jit(solution)/shard_map/ppermute | solution.py:598
  95.1 12.1 %collective-permute-start.3 = (f32[24,8,512]{2,1,0:T(8,128)S(1)}, f32[24,8,512]{2,1,0:T(8,128)S(1)}, u32[]{:S(2)}, u32[]{:S(2)}) collective-permute-start(f32[24,8,512]{2,1,0:T(8,128)S(1)} %get-tuple-element.27), channel_id=1, source_target_pairs={{1,0},{2,1},{3,2},{4,3},{5,4},{6,5},{7,6},{8,7},{9,8},{10,9},{11,1... | collective-permute-start | bytes 1179656 | tf_op jit(solution)/shard_map/ppermute | solution.py:598

commit v8 on v7

--- a/solution.py
+++ b/solution.py
@@ -341,7 +341,7 @@
 
 
 def analysis_kernel(
-    got_ref, list_ref, meta_ref, out_ref, x_ref, c_ref, y_ref, d_ref, go_ref, block_ref
+    got_ref, list_ref, meta_ref, out_ref, x_ref, c_ref, y_ref, d_ref, go_ref, block_ref, near_ref
 ):
     width = 4 * MEMBERS
     block_row = lax.broadcasted_iota(jnp.int32, (width, 128), 0) // MEMBERS % 2
@@ -401,7 +401,13 @@
     entry = lax.broadcasted_iota(jnp.int32, (WINDOW, width), 0)
     patch_row = (lax.broadcasted_iota(jnp.int32, (WINDOW, width), 1) // MEMBERS).astype(f32)
     col_gap = (entry // 4).astype(f32) - 9.5
-    col_gap_sq = col_gap * col_gap
+    spread_sq = 2.0 * LOC_R * LOC_R
+    near_col = jnp.exp(col_gap * col_gap * (-1.0 / spread_sq))
+    for n in range(LOCAL_OBS // WINDOW):
+        at = pl.ds(WINDOW * n, WINDOW)
+        row_gap = jnp.concatenate([meta_ref[1, at, :]] * 2, axis=1) - 2.0 * patch_row - 0.5
+        error = jnp.concatenate([meta_ref[2, at, :]] * 2, axis=1)
+        near_ref[at, :] = jnp.exp(row_gap * row_gap * (-1.0 / spread_sq)) / error
     row8 = lax.broadcasted_iota(jnp.int32, (8, width), 0)
     row16 = lax.broadcasted_iota(jnp.int32, (16, width), 0)
 
@@ -411,10 +417,7 @@
 
     def solve(quad, count):
         at = pl.ds(pl.multiple_of(16 * quad, 16), WINDOW)
-        obs_row = jnp.concatenate([meta_ref[1, at, :]] * 2, axis=1)
-        error = jnp.concatenate([meta_ref[2, at, :]] * 2, axis=1)
-        row_gap = obs_row - 2.0 * patch_row - 0.5
-        weight = count * jnp.exp((row_gap * row_gap + col_gap_sq) * (-1.0 / (2.0 * LOC_R * LOC_R))) / error
+        weight = count * (near_ref[at, :] * near_col)
         y = y_ref[at, :]
         scaled = weight * jnp.concatenate([y, y], axis=1)
         d = d_ref[at, :]
@@ -644,6 +647,7 @@
         [
             cells, cells, pltpu.VMEM((LOCAL_OBS, 128), f32), pltpu.VMEM((LOCAL_OBS, 128), f32),
             pltpu.VMEM((LOCAL_OBS, 128), f32), pltpu.VMEM((256, 128), bf16),
+            pltpu.VMEM((LOCAL_OBS, 256), f32),
         ],
         10**10, 5 * size, owned, lists, meta,
     )

time: 111 us -> 111 us (level)
  no operation moved by 1% of the time
where the time goes in v8:
time: 111 us; the launch traced here: 110 us
  blocking collectives  52.7 us (47%)
  Pallas kernels  27.8 us (25%)
  waiting for transfers between devices  15.8 us (14%)
  starting transfers between devices  7.57 us (7%)
  other arithmetic  3.04 us (3%)
  local copies, waits for them, and re-layouts  2.53 us (2%)
    all_to_all x2, blocking collectives, swap(): lax.all_to_all(value, 'member', split_axis=0, concat_axis=0, tiled=True)  52.7 us
    pallas_call x8, Pallas kernels, call(): pl.pallas_call(kernel, out_shape=[jax.ShapeDtypeStruct(s, f32) for s in o...  27.8 us
    ppermute x4, waiting for transfers between devices, ring(): return lax.ppermute(value, 'space', pairs)  15.8 us
    ppermute x4, starting transfers between devices, ring(): return lax.ppermute(value, 'space', pairs)  7.57 us
  transfers between devices with their start and end apart: 4, of which 4 were waited for; matrix products, arithmetic and copies ran while one was open for 4% of the time, Pallas kernels for 2%

profile of v8, /device:TPU:1, one launch (start us, length us, event | category | flops | bytes accessed | tf_op | source)
XLA Modules:
  0.0 110.2 jit_solution(1837957950246956218)
XLA Ops:
  0.6 0.0 copy-start
  0.6 1.1 %copy-done = f32[8,6,8,512]{3,2,1,0:T(8,128)S(1)} copy-done((f32[8,6,8,512]{3,2,1,0:T(8,128)S(1)}, f32[8,6,8,512]{3,2,1,0:T(8,128)}, u32[]{:S(2)}) %copy-start) | copy-done | bytes 786456
  1.8 0.0 copy-start.2
  1.8 0.0 copy-start.1
  1.8 0.1 shard_map.77
  1.9 4.2 %collective-permute-start = (f32[24,8,512]{2,1,0:T(8,128)S(1)}, f32[24,8,512]{2,1,0:T(8,128)S(1)}, u32[]{:S(2)}, u32[]{:S(2)}) collective-permute-start(f32[24,8,512]{2,1,0:T(8,128)S(1)} %get-tuple-element.15), channel_id=1, source_target_pairs={{0,1},{1,2},{2,3},{3,4},{4,5},{5,6},{6,7},{7,8},{8,9},{9,10},{10,1... | collective-permute-start | bytes 1179656 | tf_op jit(solution)/shard_map/ppermute | solution.py:601
  6.1 0.0 collective-permute-start.1
  6.1 0.5 broadcast.67
  6.6 1.4 %fusion.4 = (f32[1,2048]{1,0:T(1,128)S(1)}, s32[2048]{0:T(1024)S(1)}) fusion(s32[1,2048]{1,0:T(1,128)} %param.9, s32[]{:T(128)} %broadcast.67), kind=kLoop, calls=%fused_computation.20 | loop fusion | flops 55296 | bytes 24580 | tf_op jit(solution)/shard_map/convert_element_type | solution.py:626
  8.1 0.7 pad_maximum_fusion
  8.8 0.1 fusion.7
  8.9 0.3 squeeze.4
  9.1 0.1 copy.8
  9.3 0.8 subtract_add_fusion
  10.1 0.1 add.34
  10.1 0.1 concatenate.3
  10.3 0.1 constant_dynamic-slice_fusion
  10.3 0.1 fusion.1.list_ref
  10.4 0.2 broadcast_in_dim.2.meta_ref
  10.6 0.0 copy-done.2
  10.6 0.3 shard_map.78.cot_ref
  10.9 1.3 %collective-permute-done.top_ref = f32[24,8,512]{2,1,0:T(8,128)S(1)} collective-permute-done((f32[24,8,512]{2,1,0:T(8,128)S(1)}, f32[24,8,512]{2,1,0:T(8,128)S(1)}, u32[]{:S(2)}, u32[]{:S(2)}) %collective-permute-start) | collective-permute-done | bytes 393248 | tf_op jit(solution)/shard_map/ppermute | solution.py:601
  12.2 4.6 %collective-permute-done.1.bot_ref = f32[24,8,512]{2,1,0:T(8,128)S(1)} collective-permute-done((f32[24,8,512]{2,1,0:T(8,128)S(1)}, f32[24,8,512]{2,1,0:T(8,128)S(1)}, u32[]{:S(2)}, u32[]{:S(2)}) %collective-permute-start.1) | collective-permute-done | bytes 393248 | tf_op jit(solution)/shard_map/ppermute | solution.py:601
  16.7 0.0 copy-done.1
  16.7 3.6 %shard_map.79 = (f32[8,52,8,128]{3,2,1,0:T(8,128)S(1)}, f32[6,12,8,512]{3,2,1,0:T(8,128)S(1)}) custom-call(f32[8,6,8,512]{3,2,1,0:T(8,128)S(1)} %copy-done.1, f32[24,8,512]{2,1,0:T(8,128)S(1)} %collective-permute-done.top_ref, f32[24,8,512]{2,1,0:T(8,128)S(1)} %collective-permute-done.1.bot_ref, s32[4,512]{1,0:T(4,128)S(1)} %fusion.3.sel_ref, ...), custom_call_target="tpu_custom_call" | custom-call | flops 10000000 | bytes 4718592 | tf_op jit(solution)/shard_map/pallas_call | solution.py:35
  20.3 28.4 %all_to_all.10.got_ref = f32[8,52,8,128]{3,2,1,0:T(8,128)S(1)} all-to-all(f32[8,52,8,128]{3,2,1,0:T(8,128)S(1)} %get-tuple-element.19), channel_id=1, replica_groups=mesh['member'=8,'space'=16] {'member'}, dimensions={0} | all-to-all | bytes 3407872 | tf_op jit(solution)/shard_map/all_to_all | solution.py:605
  48.7 16.9 %shard_map.80 = f32[8,52,8,128]{3,2,1,0:T(8,128)S(1)} custom-call(f32[8,52,8,128]{3,2,1,0:T(8,128)S(1)} %all_to_all.10.got_ref, s32[16,256]{1,0:T(8,128)S(1)} %fusion.1.list_ref, f32[3,320,128]{2,1,0:T(8,128)S(1)} %broadcast_in_dim.2.meta_ref), custom_call_target="tpu_custom_call" | custom-call | flops 10000000000 | bytes 3932160 | tf_op jit(solution)/shard_map/pallas_call | solution.py:35
  65.7 24.4 %all_to_all.11.got_ref = f32[8,52,8,128]{3,2,1,0:T(8,128)S(1)} all-to-all(f32[8,52,8,128]{3,2,1,0:T(8,128)S(1)} %shard_map.80), channel_id=1, replica_groups=mesh['member'=8,'space'=16] {'member'}, dimensions={0} | all-to-all | bytes 3407872 | tf_op jit(solution)/shard_map/all_to_all | solution.py:605
  90.0 1.4 %shard_map.82 = (f32[6,8,8,512]{3,2,1,0:T(8,128)S(1)}, f32[6,12,8,512]{3,2,1,0:T(8,128)S(1)}, f32[6,4,8,512]{3,2,1,0:T(8,128)S(1)}, f32[24,8,512]{2,1,0:T(8,128)S(1)}, f32[24,8,512]{2,1,0:T(8,128)S(1)}) custom-call(f32[8,52,8,128]{3,2,1,0:T(8,128)S(1)} %all_to_all.11.got_ref, s32[4,512]{1,0:T(4,128)S(1)} %fusion.3.sel_ref, ...), custom_call_target="tpu_custom_call" | custom-call | flops 1000000 | bytes 3145728 | tf_op jit(solution)/shard_map/pallas_call | solution.py:35
  91.5 3.4 %collective-permute-start.2 = (f32[24,8,512]{2,1,0:T(8,128)S(1)}, f32[24,8,512]{2,1,0:T(8,128)S(1)}, u32[]{:S(2)}, u32[]{:S(2)}) collective-permute-start(f32[24,8,512]{2,1,0:T(8,128)S(1)} %get-tuple-element.26), channel_id=1, source_target_pairs={{0,1},{1,2},{2,3},{3,4},{4,5},{5,6},{6,7},{7,8},{8,9},{9,10},{10,1... | collective-permute-start | bytes 1179656 | tf_op jit(solution)/shard_map/ppermute | solution.py:601
  94.8 0.0 collective-permute-start.3
  94.8 1.2 %shard_map.81 = f32[8,6,8,512]{3,2,1,0:T(8,128)} custom-call(f32[8,52,8,128]{3,2,1,0:T(8,128)S(1)} %all_to_all.11.got_ref), custom_call_target="tpu_custom_call" | custom-call | flops 1000 | bytes 1572864 | tf_op jit(solution)/shard_map/pallas_call | solution.py:35
  96.0 0.9 shard_map.83.inner_ref
  96.9 2.6 %collective-permute-done.2.from_top_ref = f32[24,8,512]{2,1,0:T(8,128)S(1)} collective-permute-done((f32[24,8,512]{2,1,0:T(8,128)S(1)}, f32[24,8,512]{2,1,0:T(8,128)S(1)}, u32[]{:S(2)}, u32[]{:S(2)}) %collective-permute-start.2) | collective-permute-done | bytes 393248 | tf_op jit(solution)/shard_map/ppermute | solution.py:601
  99.6 7.3 %collective-permute-done.3.from_bot_ref = f32[24,8,512]{2,1,0:T(8,128)S(1)} collective-permute-done((f32[24,8,512]{2,1,0:T(8,128)S(1)}, f32[24,8,512]{2,1,0:T(8,128)S(1)}, u32[]{:S(2)}, u32[]{:S(2)}) %collective-permute-start.3) | collective-permute-done | bytes 393248 | tf_op jit(solution)/shard_map/ppermute | solution.py:601
  106.9 3.3 %shard_map.84 = f32[8,6,8,512]{3,2,1,0:T(8,128)} custom-call(f32[8,6,8,512]{3,2,1,0:T(8,128)S(1)} %copy-done.1, f32[24,8,512]{2,1,0:T(8,128)S(1)} %collective-permute-done.top_ref, f32[24,8,512]{2,1,0:T(8,128)S(1)} %collective-permute-done.1.bot_ref, f32[6,8,8,512]{3,2,1,0:T(8,128)S(1)} %get-tuple-element.23.g_ref, ...), custom_call_target="tpu_custom_call" | custom-call | flops 10000000 | bytes 4718592 | tf_op jit(solution)/shard_map/pallas_call | solution.py:35
  (2 shorter events, 0.0 us)
Async XLA Ops:
  0.6 1.1 %copy-start = (f32[8,6,8,512]{3,2,1,0:T(8,128)S(1)}, f32[8,6,8,512]{3,2,1,0:T(8,128)}, u32[]{:S(2)}) copy-start(f32[8,6,8,512]{3,2,1,0:T(8,128)} %x_ref.6) | copy-start | bytes 2359300
  1.8 8.8 %copy-start.2 = (f32[8,6,8,512]{3,2,1,0:T(8,128)S(1)}, f32[8,6,8,512]{3,2,1,0:T(8,128)}, u32[]{:S(2)}) copy-start(f32[8,6,8,512]{3,2,1,0:T(8,128)} %x_ref.4) | copy-start | bytes 2359300
  1.8 15.0 %copy-start.1 = (f32[8,6,8,512]{3,2,1,0:T(8,128)S(1)}, f32[8,6,8,512]{3,2,1,0:T(8,128)}, u32[]{:S(2)}) copy-start(f32[8,6,8,512]{3,2,1,0:T(8,128)} %x_ref.6) | copy-start | bytes 2359300
  1.9 10.2 %collective-permute-start = (f32[24,8,512]{2,1,0:T(8,128)S(1)}, f32[24,8,512]{2,1,0:T(8,128)S(1)}, u32[]{:S(2)}, u32[]{:S(2)}) collective-permute-start(f32[24,8,512]{2,1,0:T(8,128)S(1)} %get-tuple-element.15), channel_id=1, source_target_pairs={{0,1},{1,2},{2,3},{3,4},{4,5},{5,6},{6,7},{7,8},{8,9},{9,10},{10,1... | collective-permute-start | bytes 1179656 | tf_op jit(solution)/shard_map/ppermute | solution.py:601
  6.1 10.6 %collective-permute-start.1 = (f32[24,8,512]{2,1,0:T(8,128)S(1)}, f32[24,8,512]{2,1,0:T(8,128)S(1)}, u32[]{:S(2)}, u32[]{:S(2)}) collective-permute-start(f32[24,8,512]{2,1,0:T(8,128)S(1)} %get-tuple-element.16), channel_id=1, source_target_pairs={{1,0},{2,1},{3,2},{4,3},{5,4},{6,5},{7,6},{8,7},{9,8},{10,9},{11,1... | collective-permute-start | bytes 1179656 | tf_op jit(solution)/shard_map/ppermute | solution.py:601
  91.5 8.1 %collective-permute-start.2 = (f32[24,8,512]{2,1,0:T(8,128)S(1)}, f32[24,8,512]{2,1,0:T(8,128)S(1)}, u32[]{:S(2)}, u32[]{:S(2)}) collective-permute-start(f32[24,8,512]{2,1,0:T(8,128)S(1)} %get-tuple-element.26), channel_id=1, source_target_pairs={{0,1},{1,2},{2,3},{3,4},{4,5},{5,6},{6,7},{7,8},{8,9},{9,10},{10,1... | collective-permute-start | bytes 1179656 | tf_op jit(solution)/shard_map/ppermute | solution.py:601
  94.8 12.0 %collective-permute-start.3 = (f32[24,8,512]{2,1,0:T(8,128)S(1)}, f32[24,8,512]{2,1,0:T(8,128)S(1)}, u32[]{:S(2)}, u32[]{:S(2)}) collective-permute-start(f32[24,8,512]{2,1,0:T(8,128)S(1)} %get-tuple-element.27), channel_id=1, source_target_pairs={{1,0},{2,1},{3,2},{4,3},{5,4},{6,5},{7,6},{8,7},{9,8},{10,9},{11,1... | collective-permute-start | bytes 1179656 | tf_op jit(solution)/shard_map/ppermute | solution.py:601
